TPU v7x, 32 devices: a whole 2x2x4 slice. The times are simulated.
32 devices in a mesh: node: 8 (over y, x, core), expert: 4 (over z).
Axes of the slice: x: 2, y: 2, z: 4, core: 2. Of those that a mesh axis runs over, the one named last changes fastest.
Arguments:
- tokens: bfloat16 [16384, 1024], P(('node', 'expert')), may hold values from -6 to 6
- gain_attn: bfloat16 [1024], P(('node', 'expert')), may hold values from 0.5 to 1.5
- w_qkv: bfloat16 [1024, 3072], P(('node', 'expert')), may hold values from -0.1875 to 0.1875
- w_out: bfloat16 [1024, 1024], P(('node', 'expert')), may hold values from -1.5 to 1.5
- gain_mix: bfloat16 [1024], P(('node', 'expert')), may hold values from 0.5 to 1.5
- w_fc: bfloat16 [1024, 4096], P(('node', 'expert')), may hold values from -0.1875 to 0.1875
- w_proj: bfloat16 [4096, 1024], P(('node', 'expert')), may hold values from -0.1875 to 0.1875
- w_router: bfloat16 [1024, 4], P(('node', 'expert')), may hold values from -0.1875 to 0.1875
- w_coef: bfloat16 [1024, 2], P(('node', 'expert')), may hold values from -0.1875 to 0.1875
- expert_in: bfloat16 [4, 1024, 4096], P('expert', None, 'node'), may hold values from -0.1875 to 0.1875
- expert_out: bfloat16 [4, 4096, 1024], P('expert', 'node'), may hold values from -2 to 2
- routes: int32 [16384, 1], P(('node', 'expert')), may hold values from 0 to 3; in each aligned block of 512 rows (0 to 511, 512 to 1023, ...) at most 160 rows name the same one
- dropped: int32 [16384], P(('node', 'expert')), may hold values 0 or 1
- cotangent: bfloat16 [16384, 1024], P(('node', 'expert')), may hold values from -6 to 6
Outputs:
- mixed: bfloat16 [16384, 1024], P(('node', 'expert'))
- tokens_grad: float32 [16384, 1024], P(('node', 'expert'))
- gain_attn_grad: float32 [1024], P(('node', 'expert'))
- w_qkv_grad: float32 [1024, 3072], P(('node', 'expert'))
- w_out_grad: float32 [1024, 1024], P(('node', 'expert'))
- gain_mix_grad: float32 [1024], P(('node', 'expert'))
- w_fc_grad: float32 [1024, 4096], P(('node', 'expert'))
- w_proj_grad: float32 [4096, 1024], P(('node', 'expert'))
- w_router_grad: float32 [1024, 4], P(('node', 'expert'))
- w_coef_grad: float32 [1024, 2], P(('node', 'expert'))
- expert_in_grad: float32 [4, 1024, 4096], P('expert', None, 'node')
- expert_out_grad: float32 [4, 4096, 1024], P('expert', 'node')
Inputs may be any that keep to these rules, and one draw needn't show every extreme that they name: `routes`: the rows of one device name one expert at most 160 times, and in some devices an expert is named exactly 160 times.
All inputs are finite; a program needn't handle non-finite values. No bound on the sum of `dropped` on one device may be relied on, other than what follows from the above.
Results may differ from a plain program's by a relative error of at most 0.015.
Values may be sent and summed in bfloat16 or wider, within the bound.
A program may use at most 192 MiB of HBM per device.

v0:
```python
import math

import jax
import jax.numpy as jnp
from jax import lax
from jax.sharding import PartitionSpec as P

D = 1024
H = 16
HD = 64
SEQ = 512


highest = lax.Precision.HIGHEST
epsilon = 1e-05


def normalize(values):
    centered = values - jnp.mean(values, axis=-1, keepdims=True)
    inv_scale = lax.rsqrt(jnp.mean(centered * centered, axis=-1, keepdims=True) + epsilon)
    return (centered * inv_scale, inv_scale)


def norm_back(grad_norm, normed, inv_scale):
    mean_grad = jnp.mean(grad_norm, axis=-1, keepdims=True)
    mean_cross = jnp.mean(grad_norm * normed, axis=-1, keepdims=True)
    return inv_scale * (grad_norm - mean_grad - normed * mean_cross)


def matmul(left_op, right_op):
    return jnp.dot(left_op, right_op, preferred_element_type=jnp.float32)


def product_tn(left_op, right_op):
    return jnp.einsum("tk,tn->kn", left_op, right_op, preferred_element_type=jnp.float32)


def outer_nt(left_op, right_op):
    return jnp.einsum("tk,nk->tn", left_op, right_op, preferred_element_type=jnp.float32)


def gelu_tanh(values):
    return jax.nn.gelu(values, approximate=True)


def gelu_grad(values, upstream):
    return jax.vjp(gelu_tanh, values)[1](upstream)[0]


def split_heads(qkv_seq):
    length = qkv_seq.shape[0]
    queries = qkv_seq[:, :D].reshape(length, H, HD)
    keys_all = qkv_seq[:, D : 2 * D].reshape(length, H, HD)
    value_rows = qkv_seq[:, 2 * D :].reshape(length, H, HD)
    return (queries, keys_all, value_rows)


def masked_scores(queries, keys_all):
    length = queries.shape[0]
    scores = jnp.einsum("qhd,khd->hqk", queries, keys_all, preferred_element_type=jnp.float32) * (
        1.0 / math.sqrt(HD)
    )
    causal = lax.broadcasted_iota(jnp.int32, (length, length), 0) >= lax.broadcasted_iota(
        jnp.int32, (length, length), 1
    )
    return jnp.where(causal[None], scores, -jnp.inf)


def attend_forward(qkv_seq):
    queries, keys_all, value_rows = split_heads(qkv_seq)
    scores = masked_scores(queries, keys_all)
    row_max = jnp.max(scores, axis=-1, keepdims=True)
    expd = jnp.exp(scores - row_max)
    row_total = jnp.sum(expd, axis=-1, keepdims=True)
    attn_probs = (expd / row_total).astype(jnp.bfloat16)
    output = jnp.einsum("hqk,khd->qhd", attn_probs, value_rows, preferred_element_type=jnp.float32)
    return (output.reshape(qkv_seq.shape[0], D), row_max + jnp.log(row_total))


def attend_backward(seq_items):
    qkv_seq, log_total, grad_seq = seq_items
    length = qkv_seq.shape[0]
    queries, keys_all, value_rows = split_heads(qkv_seq)
    attn_probs = jnp.exp(masked_scores(queries, keys_all) - log_total)
    grad_heads = grad_seq.reshape(length, H, HD)
    grad_values = jnp.einsum(
        "hqk,qhd->khd",
        attn_probs.astype(jnp.bfloat16),
        grad_heads,
        preferred_element_type=jnp.float32,
    )
    grad_probs = jnp.einsum(
        "qhd,khd->hqk", grad_heads, value_rows, preferred_element_type=jnp.float32
    )
    row_delta = jnp.sum(attn_probs * grad_probs, axis=-1, keepdims=True)
    grad_scores = (attn_probs * (grad_probs - row_delta)).astype(jnp.bfloat16)
    scaling = 1.0 / math.sqrt(HD)
    grad_queries = (
        jnp.einsum("hqk,khd->qhd", grad_scores, keys_all, preferred_element_type=jnp.float32)
        * scaling
    )
    grad_keys = (
        jnp.einsum("hqk,qhd->khd", grad_scores, queries, preferred_element_type=jnp.float32)
        * scaling
    )
    joined = jnp.concatenate(
        [
            grad_queries.reshape(length, D),
            grad_keys.reshape(length, D),
            grad_values.reshape(length, D),
        ],
        axis=1,
    )
    return joined


def shards(
    tokens,
    gain_attn,
    w_qkv,
    w_out,
    gain_mix,
    w_fc,
    w_proj,
    w_router,
    w_coef,
    expert_in,
    expert_out,
    routes,
    dropped,
    cotangent,
):
    gain_one, qkv_full, out_full, gain_two, fc_full, proj_full, router_full, coef_full = (
        lax.all_gather(gain_attn, ("node", "expert"), axis=0, tiled=True),
        lax.all_gather(w_qkv, ("node", "expert"), axis=0, tiled=True),
        lax.all_gather(w_out, ("node", "expert"), axis=0, tiled=True),
        lax.all_gather(gain_mix, ("node", "expert"), axis=0, tiled=True),
        lax.all_gather(w_fc, ("node", "expert"), axis=0, tiled=True),
        lax.all_gather(w_proj, ("node", "expert"), axis=0, tiled=True),
        lax.all_gather(w_router, ("node", "expert"), axis=0, tiled=True),
        lax.all_gather(w_coef, ("node", "expert"), axis=0, tiled=True),
    )
    tok_rows = tokens.shape[0]
    sequences = tok_rows // SEQ
    residual = tokens.astype(jnp.float32)
    normed_one, scale_one = normalize(residual)
    gain_first = gain_one.astype(jnp.float32)
    attn_in = (normed_one * gain_first).astype(jnp.bfloat16)
    qkv_rows = matmul(attn_in, qkv_full).astype(jnp.bfloat16)
    qkv_seqs = qkv_rows.reshape(sequences, SEQ, 3 * D)
    attended, log_totals = lax.map(attend_forward, qkv_seqs)
    attended = attended.reshape(tok_rows, D).astype(jnp.bfloat16)
    after_attn = residual + matmul(attended, out_full)
    normed_two, scale_two = normalize(after_attn)
    gain_second = gain_two.astype(jnp.float32)
    mixed_in = (normed_two * gain_second).astype(jnp.bfloat16)
    pre_dense = matmul(mixed_in, fc_full)
    hidden = gelu_tanh(pre_dense).astype(jnp.bfloat16)
    dense_out = matmul(hidden, proj_full)
    router_probs = jax.nn.softmax(matmul(mixed_in, router_full), axis=-1)
    coef_tok = jax.nn.softmax(matmul(mixed_in, coef_full), axis=-1)
    experts = lax.axis_size("expert")
    nodes = lax.axis_size("node")
    capacity = nodes * ((tok_rows * 10 + 8 * experts * nodes - 1) // (8 * experts * nodes))
    route_tok = routes[:, 0]
    chosen_int = (route_tok[:, None] == jnp.arange(experts, dtype=jnp.int32)[None, :]).astype(
        jnp.int32
    )
    position = jnp.sum(chosen_int * (jnp.cumsum(chosen_int, axis=0) - 1), axis=1)
    target = route_tok * capacity + position
    dispatch = (jnp.arange(experts * capacity, dtype=jnp.int32)[:, None] == target[None, :]).astype(
        jnp.bfloat16
    )
    chosen = chosen_int.astype(jnp.float32)
    kept_tok = (1 - dropped).astype(jnp.float32)
    gate_prob = jnp.sum(router_probs * chosen, axis=1)
    gate_tok = gate_prob * kept_tok
    outgoing = matmul(dispatch, mixed_in).astype(jnp.bfloat16).reshape(experts, capacity, D)
    incoming = lax.all_to_all(
        lax.all_to_all(outgoing, "node", split_axis=1, concat_axis=1, tiled=True),
        "expert",
        split_axis=0,
        concat_axis=0,
        tiled=True,
    ).reshape(experts * capacity, D)
    win_whole, wout_whole = (
        lax.all_gather(expert_in, "node", axis=2, tiled=True),
        lax.all_gather(expert_out, "node", axis=1, tiled=True),
    )
    win_all = win_whole[0]
    wout_all = wout_whole[0]
    expert_hidden = gelu_tanh(matmul(incoming, win_all)).astype(jnp.bfloat16)
    returned = matmul(expert_hidden, wout_all).astype(jnp.bfloat16)
    came_back = lax.all_to_all(
        lax.all_to_all(
            returned.reshape(experts, capacity, D), "node", split_axis=1, concat_axis=1, tiled=True
        ),
        "expert",
        split_axis=0,
        concat_axis=0,
        tiled=True,
    ).reshape(experts * capacity, D)
    expert_tok = jnp.einsum("st,sd->td", dispatch, came_back, preferred_element_type=jnp.float32)
    weight_tok = coef_tok[:, 1:] * gate_tok[:, None]
    mixed = after_attn + coef_tok[:, :1] * dense_out + weight_tok * expert_tok
    grad_out = cotangent.astype(jnp.float32)
    grad_dense = (coef_tok[:, :1] * grad_out).astype(jnp.bfloat16)
    grad_expert = (weight_tok * grad_out).astype(jnp.bfloat16)
    shared = jnp.sum(grad_out * expert_tok, axis=1)
    grad_coef = jnp.stack([jnp.sum(grad_out * dense_out, axis=1), shared * gate_tok], axis=1)
    grad_coef_logit = coef_tok * (grad_coef - jnp.sum(coef_tok * grad_coef, axis=1, keepdims=True))
    grad_gate = shared * coef_tok[:, 1] * kept_tok
    grad_route_logit = (grad_gate * gate_prob)[:, None] * (chosen - router_probs)
    grad_proj = product_tn(hidden, grad_dense)
    grad_pre = gelu_grad(pre_dense, outer_nt(grad_dense, proj_full)).astype(jnp.bfloat16)
    grad_fc = product_tn(mixed_in, grad_pre)
    grad_mixed = outer_nt(grad_pre, fc_full)
    outgoing_grad = matmul(dispatch, grad_expert).astype(jnp.bfloat16).reshape(experts, capacity, D)
    incoming_grad = lax.all_to_all(
        lax.all_to_all(outgoing_grad, "node", split_axis=1, concat_axis=1, tiled=True),
        "expert",
        split_axis=0,
        concat_axis=0,
        tiled=True,
    ).reshape(experts * capacity, D)
    pre_expert = matmul(incoming, win_all)
    hid_expert = gelu_tanh(pre_expert).astype(jnp.bfloat16)
    grad_wout = product_tn(hid_expert, incoming_grad)
    grad_pre_expert = gelu_grad(pre_expert, outer_nt(incoming_grad, wout_all)).astype(jnp.bfloat16)
    grad_win = product_tn(incoming, grad_pre_expert)
    grad_rows = outer_nt(grad_pre_expert, win_all).astype(jnp.bfloat16)
    grad_in_expert, grad_out_expert = (
        lax.psum_scatter(
            grad_win[None].astype(jnp.bfloat16), "node", scatter_dimension=2, tiled=True
        ).astype(jnp.float32),
        lax.psum_scatter(
            grad_wout[None].astype(jnp.bfloat16), "node", scatter_dimension=1, tiled=True
        ).astype(jnp.float32),
    )
    grad_back = lax.all_to_all(
        lax.all_to_all(
            grad_rows.reshape(experts, capacity, D), "node", split_axis=1, concat_axis=1, tiled=True
        ),
        "expert",
        split_axis=0,
        concat_axis=0,
        tiled=True,
    ).reshape(experts * capacity, D)
    grad_mixed = grad_mixed + jnp.einsum(
        "st,sd->td", dispatch, grad_back, preferred_element_type=jnp.float32
    )
    grad_mixed = grad_mixed + jnp.dot(
        grad_route_logit, router_full.astype(jnp.float32).T, precision=highest
    )
    grad_mixed = grad_mixed + jnp.dot(
        grad_coef_logit, coef_full.astype(jnp.float32).T, precision=highest
    )
    mixed_wide = mixed_in.astype(jnp.float32)
    grad_router = jnp.dot(mixed_wide.T, grad_route_logit, precision=highest)
    grad_coef_w = jnp.dot(mixed_wide.T, grad_coef_logit, precision=highest)
    grad_gain_two = jnp.sum(grad_mixed * normed_two, axis=0)
    grad_after = grad_out + norm_back(grad_mixed * gain_second, normed_two, scale_two)
    grad_attn = grad_after.astype(jnp.bfloat16)
    grad_wo = product_tn(attended, grad_attn)
    grad_attended = outer_nt(grad_attn, out_full).astype(jnp.bfloat16)
    grad_qkv = lax.map(
        attend_backward, (qkv_seqs, log_totals, grad_attended.reshape(sequences, SEQ, D))
    )
    grad_qkv = grad_qkv.reshape(tok_rows, 3 * D).astype(jnp.bfloat16)
    grad_wqkv = product_tn(attn_in, grad_qkv)
    grad_attn_in = outer_nt(grad_qkv, qkv_full)
    grad_gain_one = jnp.sum(grad_attn_in * normed_one, axis=0)
    tokens_grad = grad_after + norm_back(grad_attn_in * gain_first, normed_one, scale_one)
    summed = (
        lax.psum_scatter(grad_gain_one, ("node", "expert"), scatter_dimension=0, tiled=True),
        lax.psum_scatter(grad_wqkv, ("node", "expert"), scatter_dimension=0, tiled=True),
        lax.psum_scatter(grad_wo, ("node", "expert"), scatter_dimension=0, tiled=True),
        lax.psum_scatter(grad_gain_two, ("node", "expert"), scatter_dimension=0, tiled=True),
        lax.psum_scatter(grad_fc, ("node", "expert"), scatter_dimension=0, tiled=True),
        lax.psum_scatter(grad_proj, ("node", "expert"), scatter_dimension=0, tiled=True),
        lax.psum_scatter(grad_router, ("node", "expert"), scatter_dimension=0, tiled=True),
        lax.psum_scatter(grad_coef_w, ("node", "expert"), scatter_dimension=0, tiled=True),
    )
    return (
        mixed.astype(jnp.bfloat16),
        tokens_grad,
        summed[0],
        summed[1],
        summed[2],
        summed[3],
        summed[4],
        summed[5],
        summed[6],
        summed[7],
        grad_in_expert,
        grad_out_expert,
    )


def solution(mesh):
    in_specs = (
        P(("node", "expert"), None),
        P(("node", "expert")),
        P(("node", "expert"), None),
        P(("node", "expert"), None),
        P(("node", "expert")),
        P(("node", "expert"), None),
        P(("node", "expert"), None),
        P(("node", "expert"), None),
        P(("node", "expert"), None),
        P("expert", None, "node"),
        P("expert", "node", None),
        P(("node", "expert"), None),
        P(("node", "expert")),
        P(("node", "expert"), None),
    )
    out_specs = (
        P(("node", "expert"), None),
        P(("node", "expert"), None),
        P(("node", "expert")),
        P(("node", "expert"), None),
        P(("node", "expert"), None),
        P(("node", "expert")),
        P(("node", "expert"), None),
        P(("node", "expert"), None),
        P(("node", "expert"), None),
        P(("node", "expert"), None),
        P("expert", None, "node"),
        P("expert", "node", None),
    )
    return jax.shard_map(shards, mesh=mesh, in_specs=in_specs, out_specs=out_specs, check_vma=False)
```

profile of v0, /device:TPU:0, one launch (start us, length us, event | category | flops | bytes accessed | tf_op | source)
XLA Modules:
  0.0 1984.2 jit_solution(15547916554668122708)
XLA Ops:
  14.9 42.4 %all-reduce.5 = (bf16[1024]{0:T(1024)(128)(2,1)S(1)}, bf16[1024]{0:T(1024)(128)(2,1)S(1)}) all-reduce(bf16[1024]{0:T(1024)(128)(2,1)S(1)} %dynamic-update-slice, bf16[1024]{0:T(1024)(128)(2,1)S(1)} %dynamic-update-slice.1), channel_id=1, replica_groups=mesh['node'=8,'expert'=4] {'node','expert'}, use_global_device_ids=true, to_apply=%add | all-reduce | flops 2048 | bytes 8192
  59.1 24.2 %all-gather.9.cloned.1.call-done = bf16[1024,3072]{1,0:T(8,128)(2,1)} async-done(((bf16[32,3072]{1,0:T(8,128)(2,1)}), bf16[1024,3072]{1,0:T(8,128)(2,1)}) %all-gather.9.cloned.1.call-update) | async-done | bytes 6291472 | tf_op jit(solution)/shard_map/all_gather | solution.py:135
  120.9 20.4 %all-gather.11.cloned.1.call-done = bf16[1024,1024]{1,0:T(8,128)(2,1)} async-done(((bf16[32,1024]{1,0:T(8,128)(2,1)}), bf16[1024,1024]{1,0:T(8,128)(2,1)}) %all-gather.11.cloned.1.call-update) | async-done | bytes 2097168 | tf_op jit(solution)/shard_map/all_gather | solution.py:136
  147.8 30.9 %all_to_all.40 = bf16[4,160,1024]{2,0,1:T(4,128)(2,1)S(1)} all-to-all(bf16[4,160,1024]{2,0,1:T(4,128)(2,1)S(1)} %copy.68), channel_id=1, replica_groups=mesh['node'=8,'expert'=4] {'node'}, dimensions={1} | all-to-all | bytes 2621440 | tf_op jit(solution)/shard_map/all_to_all | solution.py:180
  184.6 26.8 %all-gather.17.cloned.1.call-done = bf16[1,1024,4096]{2,1,0:T(8,128)(2,1)} async-done(((bf16[1,1024,512]{2,1,0:T(8,128)(2,1)}), bf16[1,1024,4096]{2,1,0:T(8,128)(2,1)}) %all-gather.17.cloned.1.call-update) | async-done | bytes 8388624 | tf_op jit(solution)/shard_map/all_gather | solution.py:187
  226.7 40.9 %all-gather.19.cloned.1.call-done = bf16[1,4096,1024]{2,1,0:T(8,128)(2,1)} async-done(((bf16[1,512,1024]{2,1,0:T(8,128)(2,1)}), bf16[1,4096,1024]{2,1,0:T(8,128)(2,1)}) %all-gather.19.cloned.1.call-update) | async-done | bytes 8388624 | tf_op jit(solution)/shard_map/all_gather | solution.py:188
  284.9 68.5 %all-gather = bf16[32,32,2]{1,2,0:T(2,128)(2,1)S(1)} all-gather(bf16[1,32,2]{1,2,0:T(2,128)(2,1)S(1)} %bitcast.165), channel_id=1, replica_groups=mesh['node'=8,'expert'=4] {'node','expert'}, dimensions={0}, use_global_device_ids=true | all-gather | bytes 4224 | tf_op jit(solution)/shard_map/all_gather | solution.py:141
  353.6 63.9 %all-gather.1 = bf16[32,32,4]{1,2,0:T(4,128)(2,1)S(1)} all-gather(bf16[1,32,4]{1,2,0:T(4,128)(2,1)S(1)} %bitcast.164), channel_id=1, replica_groups=mesh['node'=8,'expert'=4] {'node','expert'}, dimensions={0}, use_global_device_ids=true | all-gather | bytes 8448 | tf_op jit(solution)/shard_map/all_gather | solution.py:140
  434.1 22.6 %all-to-all-done.3 = bf16[4,160,1024]{2,1,0:T(8,128)(2,1)S(1)} async-done(((bf16[4,160,1024]{2,1,0:T(8,128)(2,1)}), bf16[4,160,1024]{2,1,0:T(8,128)(2,1)S(1)}, u32[]{:S(2)}, u32[]{:S(2)}) %all-to-all-start.3) | async-done | bytes 1310752 | tf_op jit(solution)/shard_map/all_to_all | solution.py:194
  460.2 13.3 fusion.46
  475.5 20.7 %all_to_all.41 = bf16[4,160,1024]{2,0,1:T(4,128)(2,1)S(1)} all-to-all(bf16[4,160,1024]{2,0,1:T(4,128)(2,1)S(1)} %copy.72), channel_id=1, replica_groups=mesh['node'=8,'expert'=4] {'node'}, dimensions={1} | all-to-all | bytes 2621440 | tf_op jit(solution)/shard_map/all_to_all | solution.py:220
  505.6 28.0 %all-to-all-done.5 = bf16[4,160,1024]{2,1,0:T(8,128)(2,1)S(1)} async-done(((bf16[4,160,1024]{2,1,0:T(8,128)(2,1)}), bf16[4,160,1024]{2,1,0:T(8,128)(2,1)S(1)}, u32[]{:S(2)}, u32[]{:S(2)}) %all-to-all-start.5) | async-done | bytes 1310752 | tf_op jit(solution)/shard_map/all_to_all | solution.py:219
  546.4 15.2 fusion.8
  583.8 20.9 %all_to_all.42 = bf16[4,160,1024]{2,0,1:T(4,128)(2,1)S(1)} all-to-all(bf16[4,160,1024]{2,0,1:T(4,128)(2,1)S(1)} %copy.74), channel_id=1, replica_groups=mesh['node'=8,'expert'=4] {'node'}, dimensions={1} | all-to-all | bytes 2621440 | tf_op jit(solution)/shard_map/all_to_all | solution.py:241
  661.6 14.7 multiply_reduce_fusion
  718.7 15.1 fusion.70
  746.8 41.0 %reduce-scatter.25.cloned.1.call-done = f32[32,4]{1,0:T(8,128)} async-done(((f32[1024,4]{1,0:T(8,128)}), f32[32,4]{1,0:T(8,128)}) %reduce-scatter.25.cloned.1.call-update) | async-done | bytes 528
  798.3 37.2 %all-reduce.4 = (f32[1024]{0:T(1024)S(1)}, f32[1024]{0:T(1024)S(1)}) all-reduce(f32[1024]{0:T(1024)S(1)} %get-tuple-element.41, f32[1024]{0:T(1024)S(1)} %get-tuple-element.39), channel_id=2, replica_groups=mesh['node'=8,'expert'=4] {'node','expert'}, use_global_device_ids=true, to_apply=%region_23.24.clone | all-reduce | flops 2048 | bytes 16384
  840.4 19.6 reduce-scatter.23.cloned.1.call-done
  862.7 72.2 %reduce-scatter.21.cloned.1.call-done = bf16[1,1024,512]{2,1,0:T(8,128)(2,1)} async-done(((bf16[1,1024,4096]{2,1,0:T(8,128)(2,1)}), bf16[1,1024,512]{2,1,0:T(8,128)(2,1)}) %reduce-scatter.21.cloned.1.call-update) | async-done | bytes 1048592 | tf_op jit(solution)/shard_map/reduce_scatter | solution.py:233
  937.8 147.9 %reduce-scatter.15.cloned.1.call-done = f32[32,1024]{1,0:T(8,128)} async-done(((f32[1024,1024]{1,0:T(8,128)}), f32[32,1024]{1,0:T(8,128)}) %reduce-scatter.15.cloned.1.call-update) | async-done | bytes 131088 | tf_op jit(solution)/shard_map/reduce_scatter | solution.py:277
  1085.7 160.4 %reduce-scatter.13.cloned.1.call-done = f32[32,3072]{1,0:T(8,128)} async-done(((f32[1024,3072]{1,0:T(8,128)}), f32[32,3072]{1,0:T(8,128)}) %reduce-scatter.13.cloned.1.call-update) | async-done | bytes 393232 | tf_op jit(solution)/shard_map/reduce_scatter | solution.py:276
  1246.2 366.3 %reduce-scatter.19.cloned.1.call-done = f32[128,1024]{1,0:T(8,128)} async-done(((f32[4096,1024]{1,0:T(8,128)}), f32[128,1024]{1,0:T(8,128)}) %reduce-scatter.19.cloned.1.call-update) | async-done | bytes 524304 | tf_op jit(solution)/shard_map/reduce_scatter | solution.py:280
  1612.5 365.0 %reduce-scatter.17.cloned.1.call-done = f32[32,4096]{1,0:T(8,128)} async-done(((f32[1024,4096]{1,0:T(8,128)}), f32[32,4096]{1,0:T(8,128)}) %reduce-scatter.17.cloned.1.call-update) | async-done | bytes 524304 | tf_op jit(solution)/shard_map/reduce_scatter | solution.py:279
  (244 shorter events, 291.1 us)
Async XLA Ops:
  7.2 76.1 %copy-start.6 = (bf16[512,1024]{1,0:T(8,128)(2,1)S(1)}, bf16[512,1024]{1,0:T(8,128)(2,1)}, u32[]{:S(2)}) copy-start(bf16[512,1024]{1,0:T(8,128)(2,1)} %param.14) | copy-start | bytes 3145732
  7.2 76.1 %all-gather.9.cloned.1.call-start = ((), (), s32[]{:S(2)}) async-start(), calls=%async_computation.16 | async-start | bytes 6488064 | tf_op jit(solution)/shard_map/all_gather | solution.py:135
  8.0 133.3 %all-gather.11.cloned.1.call-start = ((), (), s32[]{:S(2)}) async-start(), calls=%async_computation.17 | async-start | bytes 2162688 | tf_op jit(solution)/shard_map/all_gather | solution.py:136
  8.7 202.7 %all-gather.17.cloned.1.call-start = ((), (), s32[]{:S(2)}) async-start(), calls=%async_computation.20 | async-start | bytes 9437184 | tf_op jit(solution)/shard_map/all_gather | solution.py:187
  9.4 258.1 %all-gather.19.cloned.1.call-start = ((), (), s32[]{:S(2)}) async-start(), calls=%async_computation.21 | async-start | bytes 9437184 | tf_op jit(solution)/shard_map/all_gather | solution.py:188
  10.0 413.9 %all-gather.13.cloned.1.call-start = ((), (), s32[]{:S(2)}) async-start(), calls=%async_computation.18 | async-start | bytes 8650752 | tf_op jit(solution)/shard_map/all_gather | solution.py:138
  10.6 449.6 %all-gather.15.cloned.1.call-start = ((), (), s32[]{:S(2)}) async-start(), calls=%async_computation.19 | async-start | bytes 8650752 | tf_op jit(solution)/shard_map/all_gather | solution.py:139
  12.7 77.2 %copy-start.39 = (f32[512]{0:T(512)}, f32[512]{0:T(512)S(1)}, u32[]{:S(2)}) copy-start(f32[512]{0:T(512)S(1)} %broadcast_multiply_fusion.5) | copy-start | bytes 6148
  57.3 87.3 %copy-start.33 = (f32[1024]{0:T(1024)}, f32[1024]{0:T(1024)S(1)}, u32[]{:S(2)}) copy-start(f32[1024]{0:T(1024)S(1)} %convert_element_type.126) | copy-start | bytes 12292
  145.9 357.6 %copy-start.2 = (bf16[512,1024]{1,0:T(8,128)(2,1)}, bf16[512,1024]{1,0:T(8,128)(2,1)S(1)}, u32[]{:S(2)}) copy-start(bf16[512,1024]{1,0:T(8,128)(2,1)S(1)} %multiply_convert_fusion.5) | copy-start | bytes 3145732
  180.1 34.5 %all-to-all-start.1 = ((bf16[4,160,1024]{2,1,0:T(8,128)(2,1)}), bf16[4,160,1024]{2,1,0:T(8,128)(2,1)S(1)}, u32[]{:S(2)}, u32[]{:S(2)}) async-start(bf16[4,160,1024]{2,1,0:T(8,128)(2,1)} %copy.69), calls=%async_computation.1 | async-start | bytes 2621440 | tf_op jit(solution)/shard_map/all_to_all | solution.py:179
  281.4 136.6 %all-to-all-start.2 = ((bf16[4,160,1024]{2,0,1:T(4,128)(2,1)}), bf16[4,160,1024]{2,0,1:T(4,128)(2,1)S(1)}, u32[]{:S(2)}, u32[]{:S(2)}) async-start(bf16[4,160,1024]{2,0,1:T(4,128)(2,1)} %copy.70), calls=%async_computation.2 | async-start | bytes 2621440 | tf_op jit(solution)/shard_map/all_to_all | solution.py:195
  419.4 37.3 %all-to-all-start.3 = ((bf16[4,160,1024]{2,1,0:T(8,128)(2,1)}), bf16[4,160,1024]{2,1,0:T(8,128)(2,1)S(1)}, u32[]{:S(2)}, u32[]{:S(2)}) async-start(bf16[4,160,1024]{2,1,0:T(8,128)(2,1)} %copy.71), calls=%async_computation.3 | async-start | bytes 2621440 | tf_op jit(solution)/shard_map/all_to_all | solution.py:194
  473.5 174.7 %copy-start.43 = (f32[512,1]{0,1:T(1,128)}, f32[512,1]{0,1:T(1,128)S(1)}, u32[]{:S(2)}) copy-start(f32[512,1]{0,1:T(1,128)S(1)} %get-tuple-element.62) | copy-start | bytes 6148
  497.7 35.9 %all-to-all-start.5 = ((bf16[4,160,1024]{2,1,0:T(8,128)(2,1)}), bf16[4,160,1024]{2,1,0:T(8,128)(2,1)S(1)}, u32[]{:S(2)}, u32[]{:S(2)}) async-start(bf16[4,160,1024]{2,1,0:T(8,128)(2,1)} %copy.73), calls=%async_computation.5 | async-start | bytes 2621440 | tf_op jit(solution)/shard_map/all_to_all | solution.py:219
  501.3 244.2 %reduce-scatter.27.cloned.1.call-start = ((), (), s32[]{:S(2)}) async-start(), calls=%async_computation.29 | async-start | bytes 540672
  503.4 284.4 %reduce-scatter.25.cloned.1.call-start = ((), (), s32[]{:S(2)}) async-start(), calls=%async_computation.28 | async-start | bytes 540672
  505.5 354.4 %reduce-scatter.23.cloned.1.call-start = ((), (), s32[]{:S(2)}) async-start(), calls=%async_computation.27 | async-start | bytes 9437184 | tf_op jit(solution)/shard_map/reduce_scatter | solution.py:236
  546.2 388.8 %reduce-scatter.21.cloned.1.call-start = ((), (), s32[]{:S(2)}) async-start(), calls=%async_computation.26 | async-start | bytes 9437184 | tf_op jit(solution)/shard_map/reduce_scatter | solution.py:233
  606.1 36.3 %all-to-all-start.7 = ((bf16[4,160,1024]{2,1,0:T(8,128)(2,1)}), bf16[4,160,1024]{2,1,0:T(8,128)(2,1)S(1)}, u32[]{:S(2)}, u32[]{:S(2)}) async-start(bf16[4,160,1024]{2,1,0:T(8,128)(2,1)} %copy.75), calls=%async_computation.7 | async-start | bytes 2621440 | tf_op jit(solution)/shard_map/all_to_all | solution.py:240
  609.7 476.1 %reduce-scatter.15.cloned.1.call-start = ((), (), s32[]{:S(2)}) async-start(), calls=%async_computation.23 | async-start | bytes 4325376 | tf_op jit(solution)/shard_map/reduce_scatter | solution.py:277
  655.0 591.2 %reduce-scatter.13.cloned.1.call-start = ((), (), s32[]{:S(2)}) async-start(), calls=%async_computation.22 | async-start | bytes 12976128 | tf_op jit(solution)/shard_map/reduce_scatter | solution.py:276
  717.5 895.0 %reduce-scatter.19.cloned.1.call-start = ((), (), s32[]{:S(2)}) async-start(), calls=%async_computation.25 | async-start | bytes 17301504 | tf_op jit(solution)/shard_map/reduce_scatter | solution.py:280
  733.8 1243.7 %reduce-scatter.17.cloned.1.call-start = ((), (), s32[]{:S(2)}) async-start(), calls=%async_computation.24 | async-start | bytes 17301504 | tf_op jit(solution)/shard_map/reduce_scatter | solution.py:279
  (52 other events, 760.1 us)
Sparse Core Ops, SparseCore 0:
  10.9 72.3 all-gather.8
  86.2 54.9 all-gather.10
  143.1 68.1 all-gather.16
  213.1 54.3 all-gather.18
  270.3 80.8 all-gather.12
  354.0 86.1 all-gather.14
  504.3 147.6 reduce-scatter.26
  654.3 133.3 reduce-scatter.24
  791.2 68.6 reduce-scatter.22
  863.6 71.2 reduce-scatter.20
  937.8 147.8 reduce-scatter.14
  1092.2 153.9 reduce-scatter.12
  1249.1 363.3 reduce-scatter.18
  1615.3 362.1 reduce-scatter.16
where the time goes:
time: 1990 us; the launch traced here: 1980 us
  waiting for transfers between devices  1350 us (68%)
  blocking collectives  285 us (14%)
  matrix products  241 us (12%)
  other arithmetic  36.6 us (2%)
  local copies, waits for them, and re-layouts  35 us (2%)
  starting transfers between devices  20.5 us (1%)
    reduce_scatter x1, waiting for transfers between devices, shards(): lax.psum_scatter(grad_proj, ('node', 'expert'), scatter_dimension=0, tile...  366 us
    reduce_scatter x1, waiting for transfers between devices, shards(): lax.psum_scatter(grad_fc, ('node', 'expert'), scatter_dimension=0, tiled=...  365 us
    reduce_scatter x1, waiting for transfers between devices, shards(): lax.psum_scatter(grad_wqkv, ('node', 'expert'), scatter_dimension=0, tile...  160 us
    reduce_scatter x1, waiting for transfers between devices, shards(): lax.psum_scatter(grad_wo, ('node', 'expert'), scatter_dimension=0, tiled=...  148 us
    unnamed x2, blocking collectives  79.6 us
    reduce_scatter x1, waiting for transfers between devices, shards(): lax.psum_scatter(grad_win[None].astype(jnp.bfloat16), 'node', scatter_dim...  72.2 us
    all_gather x1, blocking collectives, shards(): lax.all_gather(w_coef, ('node', 'expert'), axis=0, tiled=True)  68.5 us
    all_gather x1, blocking collectives, shards(): lax.all_gather(w_router, ('node', 'expert'), axis=0, tiled=True)  63.9 us
  transfers between devices with their start and end apart: 19, of which 15 were waited for; matrix products, arithmetic and copies ran while one was open for 14% of the time, Pallas kernels for 0%

commit v1 on v0

v1 whole, which is shorter than its diff:
```python
import functools
import math

import jax
import jax.numpy as jnp
from jax import lax
from jax.experimental import pallas as pl
from jax.experimental.pallas import tpu as pltpu
from jax.sharding import PartitionSpec as P

HD = 64
PAIR = 2 * HD
SEQ = 512
QB = 256
BLOCK = 512
MIB = 1 << 20
AXES = ("node", "expert")
MESH = pl.DeviceIdType.MESH
highest = lax.Precision.HIGHEST
epsilon = 1e-05
f32 = jnp.float32
bf16 = jnp.bfloat16


def normalize(values):
    centered = values - jnp.mean(values, axis=-1, keepdims=True)
    inv_scale = lax.rsqrt(jnp.mean(centered * centered, axis=-1, keepdims=True) + epsilon)
    return (centered * inv_scale, inv_scale)


def norm_back(grad_norm, normed, inv_scale):
    mean_grad = jnp.mean(grad_norm, axis=-1, keepdims=True)
    mean_cross = jnp.mean(grad_norm * normed, axis=-1, keepdims=True)
    return inv_scale * (grad_norm - mean_grad - normed * mean_cross)


def contract(left_op, right_op, left_dim, right_dim):
    return lax.dot_general(
        left_op, right_op, (((left_dim,), (right_dim,)), ((), ())), preferred_element_type=f32
    )


def matmul(left_op, right_op):
    return contract(left_op, right_op, 1, 0)


def product_tn(left_op, right_op):
    return contract(left_op, right_op, 0, 0)


def outer_nt(left_op, right_op):
    return contract(left_op, right_op, 1, 1)


class Transfer:
    pass


def gather_kernel(experts, plans, n_args, *refs):
    src, dst = refs[:n_args], refs[n_args : 2 * n_args]
    send, recv, loc = refs[2 * n_args :]
    n, e = lax.axis_index("node"), lax.axis_index("expert")
    k, x, y = lax.rem(n, 2), lax.rem(n // 2, 2), n // 4
    nx, ny = y * 4 + (1 - x) * 2 + k, (1 - y) * 4 + x * 2 + k
    nd, nc = (1 - y) * 4 + (1 - x) * 2 + k, y * 4 + x * 2 + 1 - k
    barrier = pltpu.get_barrier_semaphore()
    peers = [(nx, e), (ny, e), (nc, e)] + [(n, lax.rem(e + j, experts)) for j in range(1, experts)]
    for peer in peers:
        pl.semaphore_signal(barrier, inc=1, device_id=peer, device_id_type=MESH)
    pl.semaphore_wait(barrier, len(peers))

    def remote(source, target, item, kind, device):
        return pltpu.make_async_remote_copy(
            src_ref=source,
            dst_ref=target,
            send_sem=send.at[item, kind],
            recv_sem=recv.at[item, kind],
            device_id=device,
            device_id_type=MESH,
        )

    items = []
    for i, (arg, dense, start, size) in enumerate(plans):
        t = Transfer()
        items.append(t)
        cols = pl.ds(start, size)
        shard, whole = src[arg], dst[arg]
        rows = shard.shape[0]
        per = experts if dense else 1
        own = n * per + (e if dense else 0)

        def bundle(m, whole=whole, per=per, cols=cols):
            return whole.at[pl.ds(m * per, per), :, cols]

        def half(m, h, whole=whole, per=per, cols=cols, dense=dense, rows=rows):
            if dense:
                return whole.at[pl.ds(m * per + h * (per // 2), per // 2), :, cols]
            return whole.at[m, pl.ds(h * (rows // 2), rows // 2), cols]

        mine = shard.at[:, cols]
        t.local = pltpu.make_async_copy(mine, whole.at[own, :, cols], loc.at[i])
        t.z = []
        if dense:
            t.z = [
                remote(mine, whole.at[own, :, cols], i, j - 1, (n, lax.rem(e + j, experts)))
                for j in range(1, experts)
            ]
            first, land = bundle(n), bundle(n)
        else:
            first, land = mine, whole.at[n, :, cols]
        b = experts - 1
        t.xy = [remote(first, land, i, b, (nx, e)), remote(first, land, i, b + 1, (ny, e))]
        t.diag = [
            remote(half(nx, 0), half(nx, 0), i, b + 2, (ny, e)),
            remote(half(ny, 1), half(ny, 1), i, b + 3, (nx, e)),
        ]
        t.core = [remote(first, land, i, b + 4, (nc, e))] + [
            remote(bundle(m), bundle(m), i, b + 5 + j, (nc, e)) for j, m in enumerate((nx, ny, nd))
        ]

    def step_z(t):
        t.local.start()
        for copy in t.z:
            copy.start()

    def step_xy(t):
        for copy in t.z:
            copy.wait()
        t.local.wait()
        t.xy[0].start()
        t.xy[1].start()
        t.core[0].start()

    def step_diag(t):
        for i in range(2):
            t.xy[i].wait()
            t.diag[i].start()
            t.core[1 + i].start()

    def step_core(t):
        t.diag[0].wait()
        t.diag[1].wait()
        t.core[3].start()

    def step_end(t):
        for copy in t.core:
            copy.wait()

    steps = (step_z, step_xy, step_diag, step_core, step_end)
    for turn in range(len(items) + len(steps) - 1):
        for late, step in enumerate(steps):
            if 0 <= turn - late < len(items):
                step(items[turn - late])


def gather(args, dense, plans, nodes, experts, collective_id, name):
    m = len(plans)
    outs = [
        jax.ShapeDtypeStruct(((nodes * experts if d else nodes),) + a.shape, a.dtype)
        for a, d in zip(args, dense)
    ]
    plans = [(arg, dense[arg], start, size) for arg, start, size in plans]
    hbm = pl.BlockSpec(memory_space=pltpu.HBM)
    return pl.pallas_call(
        functools.partial(gather_kernel, experts, plans, len(args)),
        out_shape=outs,
        in_specs=[hbm] * len(args),
        out_specs=[hbm] * len(args),
        scratch_shapes=[
            pltpu.SemaphoreType.DMA((m, experts + 7)),
            pltpu.SemaphoreType.DMA((m, experts + 7)),
            pltpu.SemaphoreType.DMA((m,)),
        ],
        compiler_params=pltpu.CompilerParams(collective_id=collective_id, has_side_effects=True),
        name=name,
    )(*args)


def masks():
    lanes = lax.broadcasted_iota(jnp.int32, (1, PAIR), 1)
    return [(lanes // HD == h).astype(bf16) for h in range(2)]


def causal(scores_t, start):
    keys = lax.broadcasted_iota(jnp.int32, scores_t.shape, 0)
    queries = lax.broadcasted_iota(jnp.int32, scores_t.shape, 1) + start
    return jnp.where(keys <= queries, scores_t, -jnp.inf)


def attend_forward_kernel(q_ref, k_ref, v_ref, o_ref, lse_ref):
    q = q_ref[...] * (1.0 / math.sqrt(HD))
    k = k_ref[...]
    vt = v_ref[...].T
    length = q.shape[0]
    outs = []
    for h, mask in enumerate(masks()):
        kh = k * mask
        row = []
        for start in range(0, length, QB):
            end = start + QB
            scores = causal(outer_nt(kh[:end], q[start:end]), start)
            top = jnp.max(scores, axis=0, keepdims=True)
            expd = jnp.exp(scores - top)
            total = jnp.sum(expd, axis=0, keepdims=True)
            probs = (expd / total).astype(bf16)
            row.append(matmul(vt[h * HD : (h + 1) * HD, :end], probs))
            lse_ref[0, h : h + 1, start:end] = top + jnp.log(total)
        outs.append(jnp.concatenate(row, axis=1))
    o_ref[...] = jnp.concatenate(outs, axis=0).T.astype(bf16)


def attend_forward(qkv, width):
    length = qkv.shape[0]
    pairs = width // PAIR
    part = lambda p: pl.BlockSpec((SEQ, PAIR), lambda s, i: (s, p * pairs + i))
    return pl.pallas_call(
        attend_forward_kernel,
        grid=(length // SEQ, pairs),
        out_shape=[
            jax.ShapeDtypeStruct((length, width), bf16),
            jax.ShapeDtypeStruct((length // SEQ * pairs, 2, SEQ), f32),
        ],
        in_specs=[part(0), part(1), part(2)],
        out_specs=[
            pl.BlockSpec((SEQ, PAIR), lambda s, i: (s, i)),
            pl.BlockSpec((1, 2, SEQ), lambda s, i: (s * pairs + i, 0, 0)),
        ],
        cost_estimate=pl.CostEstimate(
            flops=4 * length * SEQ * width, bytes_accessed=10 * length * width, transcendentals=0
        ),
        compiler_params=pltpu.CompilerParams(vmem_limit_bytes=48 * MIB),
        name="attend_forward",
    )(qkv, qkv, qkv)


def attend_backward_kernel(q_ref, k_ref, v_ref, g_ref, lse_ref, d_ref):
    scaling = 1.0 / math.sqrt(HD)
    q, k, v, g = q_ref[...], k_ref[...], v_ref[...], g_ref[...]
    qs = q * scaling
    kt = k.T
    length = q.shape[0]
    grad_k = [0.0] * (length // QB)
    grad_v = [0.0] * (length // QB)
    grad_q = []
    for h, mask in enumerate(masks()):
        kh, vh, qh, gh = k * mask, v * mask, q * mask, g * mask
        row = []
        for c, start in enumerate(range(0, length, QB)):
            end = start + QB
            scores = causal(outer_nt(kh[:end], qs[start:end]), start)
            probs = jnp.exp(scores - lse_ref[0, h : h + 1, start:end])
            grad_probs = outer_nt(vh[:end], g[start:end])
            delta = jnp.sum(probs * grad_probs, axis=0, keepdims=True)
            grad_scores = (probs * (grad_probs - delta)).astype(bf16)
            more_v = matmul(probs.astype(bf16), gh[start:end])
            more_k = matmul(grad_scores, qh[start:end])
            for b in range(c + 1):
                rows = slice(b * QB, (b + 1) * QB)
                grad_v[b] = grad_v[b] + more_v[rows]
                grad_k[b] = grad_k[b] + more_k[rows]
            row.append(matmul(kt[h * HD : (h + 1) * HD, :end], grad_scores))
        grad_q.append(jnp.concatenate(row, axis=1))
    d_ref[0] = (jnp.concatenate(grad_q, axis=0).T * scaling).astype(bf16)
    for b in range(length // QB):
        d_ref[1, b * QB : (b + 1) * QB] = (grad_k[b] * scaling).astype(bf16)
        d_ref[2, b * QB : (b + 1) * QB] = grad_v[b].astype(bf16)


def attend_backward(qkv, lse, grad, width):
    length = qkv.shape[0]
    pairs = width // PAIR
    part = lambda p: pl.BlockSpec((SEQ, PAIR), lambda s, i: (s, p * pairs + i))
    return pl.pallas_call(
        attend_backward_kernel,
        grid=(length // SEQ, pairs),
        out_shape=jax.ShapeDtypeStruct((3, length, width), bf16),
        in_specs=[
            part(0),
            part(1),
            part(2),
            part(0),
            pl.BlockSpec((1, 2, SEQ), lambda s, i: (s * pairs + i, 0, 0)),
        ],
        out_specs=pl.BlockSpec((3, SEQ, PAIR), lambda s, i: (0, s, i)),
        cost_estimate=pl.CostEstimate(
            flops=10 * length * SEQ * width, bytes_accessed=16 * length * width, transcendentals=0
        ),
        compiler_params=pltpu.CompilerParams(vmem_limit_bytes=48 * MIB),
        name="attend_backward",
    )(qkv, qkv, qkv, grad, lse)


def gelu_both(v):
    c = math.sqrt(2.0 / math.pi)
    square = v * v
    t = jnp.tanh(c * (v + 0.044715 * (square * v)))
    half = 0.5 * (1.0 + t)
    slope = half + 0.5 * v * (1.0 - t * t) * (c * (1.0 + (3 * 0.044715) * square))
    return v * half, slope


def mlp_kernel(x_ref, g_ref, w1_ref, w2_ref, out_ref, back_ref, d1_ref, d2_ref, xt, gt, out_sum, back_sum):
    j = pl.program_id(0)

    @pl.when(j == 0)
    def _():
        xt[...] = x_ref[...].T
        gt[...] = g_ref[...].T
        out_sum[...] = jnp.zeros_like(out_sum)
        back_sum[...] = jnp.zeros_like(back_sum)

    w1 = w1_ref[...].reshape(w1_ref.shape[-2:])
    w2 = w2_ref[...].reshape(w2_ref.shape[-2:])
    hidden, slope = gelu_both(matmul(x_ref[...], w1))
    hidden = hidden.astype(bf16)
    grad_pre = (slope * outer_nt(g_ref[...], w2)).astype(bf16)
    out_sum[...] += matmul(hidden, w2)
    back_sum[...] += outer_nt(grad_pre, w1)
    d1_ref[...] = matmul(xt[...], grad_pre).astype(bf16).reshape(d1_ref.shape)
    d2_ref[...] = matmul(gt[...], hidden).astype(bf16).reshape(d2_ref.shape)

    @pl.when(j == pl.num_programs(0) - 1)
    def _():
        out_ref[...] = out_sum[...].astype(out_ref.dtype)
        back_ref[...] = back_sum[...].astype(back_ref.dtype)


def mlp(x, g, w1, w2, out_dtype, name):
    rows, width = x.shape
    if w1.ndim == 3:
        blocks, _, size = w1.shape
        w1_spec = pl.BlockSpec((1, width, size), lambda j: (j, 0, 0))
        w2_spec = pl.BlockSpec((1, size, width), lambda j: (j, 0, 0))
        d_shape = (blocks, width, size)
    else:
        size = BLOCK
        blocks = w1.shape[1] // size
        w1_spec = pl.BlockSpec((width, size), lambda j: (0, j))
        w2_spec = pl.BlockSpec((size, width), lambda j: (j, 0))
        d_shape = (width, blocks * size)
    whole = pl.BlockSpec((rows, width), lambda j: (0, 0))
    return pl.pallas_call(
        mlp_kernel,
        grid=(blocks,),
        out_shape=[jax.ShapeDtypeStruct((rows, width), out_dtype)] * 2
        + [jax.ShapeDtypeStruct(d_shape, bf16)] * 2,
        in_specs=[whole, whole, w1_spec, w2_spec],
        out_specs=[whole, whole, w1_spec, w1_spec],
        scratch_shapes=[
            pltpu.VMEM((width, rows), bf16),
            pltpu.VMEM((width, rows), bf16),
            pltpu.VMEM((rows, width), f32),
            pltpu.VMEM((rows, width), f32),
        ],
        cost_estimate=pl.CostEstimate(
            flops=12 * rows * width * blocks * size,
            bytes_accessed=8 * width * blocks * size,
            transcendentals=rows * blocks * size,
        ),
        compiler_params=pltpu.CompilerParams(vmem_limit_bytes=56 * MIB),
        name=name,
    )(x, g, w1, w2)


def neighbour(axis):
    return [(n, n ^ axis) for n in range(8)]


CORE, X, Y = 1, 2, 4


def hop(values, axis):
    return lax.ppermute(values, "node", neighbour(axis))


def add(*terms):
    return functools.reduce(jnp.add, [t.astype(f32) for t in terms])


def scatter_plane(parts):
    n = lax.axis_index("node")
    k, x, y = lax.rem(n, 2), lax.rem(n // 2, 2), n // 4
    pick = lambda a, i: lax.dynamic_index_in_dim(a, i, 0, keepdims=False)
    rest = parts.shape[1:]
    by_core = parts.reshape((4, 2) + rest)
    take = lambda i: lax.dynamic_index_in_dim(by_core, i, 1, keepdims=False)
    chip = add(take(k), hop(take(1 - k), CORE)).astype(bf16)
    place = y * 2 + x
    own, to_x, to_y, diag = (pick(chip, place ^ i) for i in (0, 1, 2, 3))
    from_x = hop(jnp.stack([diag[0], to_x[0]]), X)
    from_y = hop(jnp.stack([diag[1], to_y[1]]), Y)
    last_x = hop(add(to_x[1], from_y[0]).astype(bf16), X)
    last_y = hop(add(to_y[0], from_x[0]).astype(bf16), Y)
    return jnp.stack([add(own[0], from_x[1], last_y), add(own[1], last_x, from_y[1])])


def scatter_all(parts, experts):
    rest = parts.shape[1:]
    e = lax.axis_index("expert")
    plane = scatter_plane(parts.reshape((8, 2, experts // 2) + rest)).reshape((experts,) + rest)
    mine = lambda i: lax.dynamic_index_in_dim(plane, lax.rem(e + i, experts), 0, keepdims=False)
    terms = [mine(0)]
    for j in range(1, experts):
        shift = [(s, (s + j) % experts) for s in range(experts)]
        terms.append(lax.ppermute(mine(j).astype(bf16), "expert", shift))
    return add(*terms)


def shards(
    fast,
    tokens,
    gain_attn,
    w_qkv,
    w_out,
    gain_mix,
    w_fc,
    w_proj,
    w_router,
    w_coef,
    expert_in,
    expert_out,
    routes,
    dropped,
    cotangent,
):
    experts = lax.axis_size("expert")
    nodes = lax.axis_size("node")
    devices = nodes * experts
    width = tokens.shape[1]
    tok_rows = tokens.shape[0]
    ff = w_fc.shape[1]
    share = w_qkv.shape[0]
    small = jnp.concatenate([gain_attn[:, None], gain_mix[:, None], w_router, w_coef], axis=1)
    small = jnp.pad(small, ((0, 0), (0, 128 - small.shape[1])))
    win, wout = expert_in[0], expert_out[0]
    if fast:
        third = w_qkv.shape[1] // 3
        small_full, qkv_full, out_full = gather(
            [small, w_qkv, w_out],
            [True] * 3,
            [(0, 0, 128)] + [(1, i * third, third) for i in range(3)] + [(2, 0, width)],
            nodes,
            experts,
            1,
            "gather_first",
        )
        quarter = lambda a, d, m: [(a, i * (d // m), d // m) for i in range(m)]
        fc_full, proj_full, win_full, wout_full = gather(
            [w_fc, w_proj, win, wout],
            [True, True, False, False],
            quarter(0, ff, 4) + quarter(1, width, 4) + quarter(2, win.shape[1], 2) + quarter(3, width, 2),
            nodes,
            experts,
            2,
            "gather_rest",
        )
    else:
        small_full, qkv_full, out_full, fc_full, proj_full = (
            lax.all_gather(a, AXES, axis=0, tiled=False) for a in (small, w_qkv, w_out, w_fc, w_proj)
        )
        win_full, wout_full = (lax.all_gather(a, "node", axis=0, tiled=False) for a in (win, wout))
    small_full, qkv_full, out_full, fc_full, proj_full = (
        a.reshape((devices * a.shape[1],) + a.shape[2:])
        for a in (small_full, qkv_full, out_full, fc_full, proj_full)
    )

    def scatter(parts):
        if fast:
            return scatter_all(parts, experts)
        return lax.psum_scatter(parts, AXES, scatter_dimension=0, tiled=False).astype(f32)

    def scatter_experts(parts):
        if fast:
            halves = parts.reshape((nodes, 2, parts.shape[1] // 2) + parts.shape[2:])
            return scatter_plane(halves).reshape(parts.shape[1:])
        return lax.psum_scatter(parts, "node", scatter_dimension=0, tiled=False).astype(f32)

    gain_first = small_full[:, 0].astype(f32)
    gain_second = small_full[:, 1].astype(f32)
    heads = small_full[:, 2 : 4 + experts]

    residual = tokens.astype(f32)
    normed_one, scale_one = normalize(residual)
    attn_in = (normed_one * gain_first).astype(bf16)
    qkv_rows = matmul(attn_in, qkv_full).astype(bf16)
    attended, lse = attend_forward(qkv_rows, width)
    after_attn = residual + matmul(attended, out_full)
    normed_two, scale_two = normalize(after_attn)
    mixed_in = (normed_two * gain_second).astype(bf16)
    logits = matmul(mixed_in, small_full)
    router_probs = jax.nn.softmax(logits[:, 2 : 2 + experts], axis=-1)
    coef_tok = jax.nn.softmax(logits[:, 2 + experts : 4 + experts], axis=-1)

    route_tok = routes[:, 0]
    capacity = -(-(tok_rows * 10) // (8 * experts))
    chosen = (route_tok[:, None] == jnp.arange(experts, dtype=jnp.int32)[None, :]).astype(f32)
    earlier = (
        lax.broadcasted_iota(jnp.int32, (tok_rows, tok_rows), 0)
        > lax.broadcasted_iota(jnp.int32, (tok_rows, tok_rows), 1)
    ).astype(bf16)
    position = jnp.sum(chosen * matmul(earlier, chosen.astype(bf16)), axis=1).astype(jnp.int32)
    turn = lax.rem(route_tok - lax.axis_index("expert") + experts, experts)
    target = turn * capacity + position
    dispatch = (
        lax.broadcasted_iota(jnp.int32, (experts * capacity, tok_rows), 0) == target[None, :]
    ).astype(bf16)
    kept_tok = (1 - dropped).astype(f32)
    gate_prob = jnp.sum(router_probs * chosen, axis=1)
    gate_tok = gate_prob * kept_tok
    weight_tok = coef_tok[:, 1:] * gate_tok[:, None]
    grad_out = cotangent.astype(f32)
    grad_dense = (coef_tok[:, :1] * grad_out).astype(bf16)
    grad_expert = (weight_tok * grad_out).astype(bf16)

    def exchange(parts, sign):
        moved = [parts[0]]
        for j in range(1, experts):
            shift = [(s, (s + sign * j) % experts) for s in range(experts)]
            moved.append(lax.ppermute(parts[j], "expert", shift))
        return jnp.concatenate(moved, axis=0)

    leaving = matmul(dispatch, jnp.concatenate([mixed_in, grad_expert], axis=1)).astype(bf16)
    arrived = exchange(leaving.reshape(experts, capacity, 2 * width), 1)

    dense_out, grad_mixed, d_fc, d_proj = mlp(mixed_in, grad_dense, fc_full, proj_full, f32, "dense_mlp")
    returned, grad_rows, d_win, d_wout = mlp(
        arrived[:, :width], arrived[:, width:], win_full, wout_full, bf16, "expert_mlp"
    )
    leaving = jnp.concatenate([returned, grad_rows], axis=1)
    came_back = exchange(leaving.reshape(experts, capacity, 2 * width), -1)
    came_back = product_tn(dispatch, came_back)
    expert_tok, grad_back = came_back[:, :width], came_back[:, width:]

    grad_fc = scatter(d_fc.reshape(devices, share, ff))
    by_unit = d_proj.reshape(width, devices, ff // devices).transpose(1, 0, 2)
    grad_proj = scatter(by_unit).T
    grad_win = scatter_experts(d_win)[None]
    grad_wout = scatter_experts(d_wout).T[None]

    mixed = after_attn + coef_tok[:, :1] * dense_out + weight_tok * expert_tok
    shared = jnp.sum(grad_out * expert_tok, axis=1)
    grad_coef = jnp.stack([jnp.sum(grad_out * dense_out, axis=1), shared * gate_tok], axis=1)
    grad_coef_logit = coef_tok * (grad_coef - jnp.sum(coef_tok * grad_coef, axis=1, keepdims=True))
    grad_gate = shared * coef_tok[:, 1] * kept_tok
    grad_route_logit = (grad_gate * gate_prob)[:, None] * (chosen - router_probs)
    grad_logits = jnp.concatenate([grad_route_logit, grad_coef_logit], axis=1)
    grad_mixed = grad_mixed + grad_back
    grad_mixed = grad_mixed + jnp.dot(grad_logits, heads.astype(f32).T, precision=highest)
    grad_heads = jnp.dot(mixed_in.astype(f32).T, grad_logits, precision=highest)
    grad_gain_two = jnp.sum(grad_mixed * normed_two, axis=0)
    grad_after = grad_out + norm_back(grad_mixed * gain_second, normed_two, scale_two)
    grad_attn = grad_after.astype(bf16)
    grad_wo = scatter(product_tn(attended, grad_attn).astype(bf16).reshape(devices, share, width))
    grad_attended = outer_nt(grad_attn, out_full).astype(bf16)
    grad_qkv = attend_backward(qkv_rows, lse, grad_attended, width)
    d_qkv = jnp.concatenate([product_tn(attn_in, grad_qkv[i]).astype(bf16) for i in range(3)], axis=1)
    grad_attn_in = sum(outer_nt(grad_qkv[i], qkv_full[:, i * width : (i + 1) * width]) for i in range(3))
    grad_gain_one = jnp.sum(grad_attn_in * normed_one, axis=0)
    tokens_grad = grad_after + norm_back(grad_attn_in * gain_first, normed_one, scale_one)
    grad_wqkv = scatter(d_qkv.reshape(devices, share, 3 * width))
    d_small = jnp.concatenate([grad_gain_one[:, None], grad_gain_two[:, None], grad_heads], axis=1)
    d_small = jnp.pad(d_small, ((0, 0), (0, 128 - d_small.shape[1]))).astype(bf16)
    grad_small = scatter(d_small.reshape(devices, share, 128))
    return (
        mixed.astype(bf16),
        tokens_grad,
        grad_small[:, 0],
        grad_wqkv,
        grad_wo,
        grad_small[:, 1],
        grad_fc,
        grad_proj,
        grad_small[:, 2 : 2 + experts],
        grad_small[:, 2 + experts : 4 + experts],
        grad_win,
        grad_wout,
    )


def solution(mesh):
    rows = P(AXES, None)
    in_specs = (
        rows,
        P(AXES),
        rows,
        rows,
        P(AXES),
        rows,
        rows,
        rows,
        rows,
        P("expert", None, "node"),
        P("expert", "node", None),
        rows,
        P(AXES),
        rows,
    )
    out_specs = (
        rows,
        rows,
        P(AXES),
        rows,
        rows,
        P(AXES),
        rows,
        rows,
        rows,
        rows,
        P("expert", None, "node"),
        P("expert", "node", None),
    )
    fast = mesh.shape["node"] == 8 and mesh.shape["expert"] % 2 == 0
    return jax.shard_map(
        functools.partial(shards, fast), mesh=mesh, in_specs=in_specs, out_specs=out_specs, check_vma=False
    )
```

time: 1990 us -> 881 us (0.44)
  waiting for transfers between devices: 1350 us -> 235 us
  Pallas kernels: 0 us -> 369 us
  blocking collectives: 285 us -> 0 us
  matrix products: 241 us -> 33.4 us
  local copies, waits for them, and re-layouts: 35 us -> 86.9 us
  other arithmetic: 36.6 us -> 83.7 us
  starting transfers between devices: 20.5 us -> 56.8 us
    reduce_scatter x6 -> x0, waiting for transfers between devices: 1130 us -> none  [the longest x1 366 us: shards(): lax.psum_scatter(grad_proj, ('node', 'expert'), scatter_dimension=0, tile...]
    pallas_call x0 -> x6, Pallas kernels: none -> 369 us  [the longest x2 261 us: gather(): pl.pallas_call(functools.partial(gather_kernel, experts, plans, len(args)...]
    ppermute x0 -> x56, waiting for transfers between devices: none -> 235 us  [the longest x35 156 us: hop(): return lax.ppermute(values, 'node', neighbour(axis))]
    dot_general x32 -> x16, matrix products: 237 us -> 33.4 us  [the longest x14 30.6 us: contract(): lax.dot_general(left_op, right_op, (((left_dim,), (right_dim,)), ((), ())...]
    all_gather x2 -> x0, blocking collectives: 132 us -> none  [the longest x1 68.5 us: shards(): lax.all_gather(w_coef, ('node', 'expert'), axis=0, tiled=True)]
    all_gather x6 -> x0, waiting for transfers between devices: 112 us -> none  [the longest x1 40.9 us: shards(): lax.all_gather(expert_out, 'node', axis=1, tiled=True)]
    unnamed x2 -> x0, blocking collectives: 79.6 us -> none
    all_to_all x3 -> x0, blocking collectives: 72.5 us -> none  [the longest x1 30.9 us: shards(): lax.all_to_all(outgoing, 'node', split_axis=1, concat_axis=1, tiled=True)]
  transfers between devices with their start and end apart: 19 -> 56, of which waited for: 15 -> 26; matrix products, arithmetic and copies ran while one was open for 14% -> 20% of each run, Pallas kernels for 0% -> 35%
where the time goes in v1:
time: 881 us; the launch traced here: 867 us
  Pallas kernels  369 us (42%)
  waiting for transfers between devices  235 us (27%)
  local copies, waits for them, and re-layouts  86.9 us (10%)
  other arithmetic  83.7 us (10%)
  starting transfers between devices  56.8 us (6%)
  matrix products  33.4 us (4%)
    pallas_call x2, Pallas kernels, gather(): pl.pallas_call(functools.partial(gather_kernel, experts, plans, len(args)...  261 us
    ppermute x35, waiting for transfers between devices, hop(): return lax.ppermute(values, 'node', neighbour(axis))  156 us
    pallas_call x2, Pallas kernels, mlp(): pl.pallas_call(mlp_kernel, grid=(blocks,), out_shape=[jax.ShapeDtypeStruc...  77.4 us
    ppermute x15, waiting for transfers between devices, scatter_all(): terms.append(lax.ppermute(mine(j).astype(bf16), 'expert', shift))  47.1 us
    ppermute x6, waiting for transfers between devices, exchange(): moved.append(lax.ppermute(parts[j], 'expert', shift))  32 us
    dot_general x14, matrix products, contract(): lax.dot_general(left_op, right_op, (((left_dim,), (right_dim,)), ((), ())...  30.6 us
    unnamed x85, local copies, waits for them, and re-layouts  29.7 us
    ppermute x35, starting transfers between devices, hop(): return lax.ppermute(values, 'node', neighbour(axis))  28.4 us
  transfers between devices with their start and end apart: 56, of which 26 were waited for; matrix products, arithmetic and copies ran while one was open for 20% of the time, Pallas kernels for 35%

profile of v1, /device:TPU:0, one launch (start us, length us, event | category | flops | bytes accessed | tf_op | source)
XLA Modules:
  0.0 867.0 jit_solution(15754068520065531931)
XLA Ops:
  4.6 52.0 %gather_first.1 = (bf16[32,32,128]{2,1,0:T(8,128)(2,1)}, bf16[32,32,3072]{2,1,0:T(8,128)(2,1)}, bf16[32,32,1024]{2,1,0:T(8,128)(2,1)}) custom-call(bf16[32,128]{1,0:T(8,128)(2,1)} %pad.9.refs_0_, bf16[32,3072]{1,0:T(8,128)(2,1)} %refs_1_.2, bf16[32,1024]{1,0:T(8,128)(2,1)} %refs_2_.1), custom_call_target="tpu_custom_call" | custom-call | tf_op jit(solution)/shard_map/gather_first/pallas_call | solution.py:164
  65.5 14.5 %attend_forward.1 = (bf16[512,1024]{1,0:T(8,128)(2,1)S(1)}, f32[8,2,512]{2,1,0:T(2,128)S(1)}) custom-call(bf16[512,3072]{1,0:T(8,128)(2,1)S(1)} %convolution_convert_fusion.q_ref.k_ref.v_ref, bf16[512,3072]{1,0:T(8,128)(2,1)S(1)} %convolution_convert_fusion.q_ref.k_ref.v_ref, bf16[512,3072]{1,0:T(8,128)(2,1)S(1)} %convolution_convert_fusion.q_ref.k_ref.v_ref), custom_call_target="tpu_custom_call" | custom-call | flops 1073741824 | bytes 5242880 | tf_op jit(solution)/shard_map/attend_forward/pallas_call | solution.py:216
  96.5 208.6 %gather_rest.1 = (bf16[32,32,4096]{2,1,0:T(8,128)(2,1)}, bf16[32,128,1024]{2,1,0:T(8,128)(2,1)}, bf16[8,1024,512]{2,1,0:T(8,128)(2,1)}, bf16[8,512,1024]{2,1,0:T(8,128)(2,1)}) custom-call(bf16[32,4096]{1,0:T(8,128)(2,1)} %refs_0_.1, bf16[128,1024]{1,0:T(8,128)(2,1)} %refs_1_.3, bf16[1024,512]{1,0:T(8,128)(2,1)} %bitcast.562, bf16[512,1024]{1,0:T(8,128)(2,1)} %bitcast.563), custom_call_target="tpu_custom_call" | custom-call | tf_op jit(solution)/shard_map/gather_rest/pallas_call | solution.py:164
  305.0 34.6 %dense_mlp.1 = (f32[512,1024]{1,0:T(8,128)}, f32[512,1024]{1,0:T(8,128)}, bf16[1024,4096]{1,0:T(8,128)(2,1)}, bf16[1024,4096]{1,0:T(8,128)(2,1)}) custom-call(bf16[512,1024]{1,0:T(8,128)(2,1)} %copy-done.4, bf16[512,1024]{1,0:T(8,128)(2,1)} %get-tuple-element.115.g_ref, bf16[1024,4096]{1,0:T(8,128)(2,1)} %bitcast.594, bf16[4096,1024]{1,0:T(8,128)(2,1)} %bitcast.595), custom_call_target="tpu_custom_call" | custom-call | flops 25769803776 | bytes 33554432 | tf_op jit(solution)/shard_map/dense_mlp/pallas_call | solution.py:342
  339.6 9.5 %copy.78 = bf16[128,8,32,128]{3,2,1,0:T(8,128)(2,1)} copy(bf16[128,8,32,128]{3,1,2,0:T(8,128)(2,1)} %bitcast.542) | data formatting | bytes 16777216
  349.2 8.5 constant_dynamic-slice_fusion.5
  357.6 11.2 %copy.68 = bf16[4,1,2,2,1024,128]{4,5,3,2,0,1:T(8,128)(2,1)} copy(bf16[4,1,2,2,1024,128]{5,3,2,1,0,4:T(2,128)(2,1)} %get-tuple-element.57) | data formatting | bytes 8388608 | tf_op jit(solution)/shard_map/jit(dynamic_index_in_dim)/dynamic_slice | solution.py:386
  372.6 42.8 %expert_mlp.1 = (bf16[640,1024]{1,0:T(8,128)(2,1)}, bf16[640,1024]{1,0:T(8,128)(2,1)}, bf16[8,1024,512]{2,1,0:T(8,128)(2,1)}, bf16[8,1024,512]{2,1,0:T(8,128)(2,1)}) custom-call(bf16[640,1024]{1,0:T(8,128)(2,1)} %get-tuple-element.94.x_ref, bf16[640,1024]{1,0:T(8,128)(2,1)} %get-tuple-element.93.g_ref, bf16[8,1024,512]{2,1,0:T(8,128)(2,1)} %get-tuple-element.36.w1_ref, ...), custom_call_target="tpu_custom_call" | custom-call | flops 32212254720 | bytes 33554432 | tf_op jit(solution)/shard_map/expert_mlp/pallas_call | solution.py:342
  427.0 11.2 %copy.76 = bf16[4,1,2,2,1024,128]{4,5,3,2,0,1:T(8,128)(2,1)} copy(bf16[4,1,2,2,1024,128]{5,3,2,1,0,4:T(2,128)(2,1)} %get-tuple-element.56) | data formatting | bytes 8388608
  447.1 32.0 %collective-permute-done.4 = bf16[160,2048]{1,0:T(8,128)(2,1)} collective-permute-done((bf16[160,2048]{1,0:T(8,128)(2,1)}, bf16[160,2048]{1,0:T(8,128)(2,1)}, u32[]{:S(2)}, u32[]{:S(2)}) %collective-permute-start.4) | collective-permute-done | bytes 655392 | tf_op jit(solution)/shard_map/ppermute | solution.py:519
  493.3 16.9 %attend_backward.1 = bf16[3,512,1024]{2,1,0:T(8,128)(2,1)S(1)} custom-call(bf16[512,3072]{1,0:T(8,128)(2,1)} %copy-done, bf16[512,3072]{1,0:T(8,128)(2,1)} %copy-done, bf16[512,3072]{1,0:T(8,128)(2,1)} %copy-done, bf16[512,1024]{1,0:T(8,128)(2,1)S(1)} %convolution_convert_fusion.6.g_ref, f32[8,2,512]{2,1,0:T(2,128)S(1)} %get-tuple-element.41.lse_ref), custom_call_target="tpu_custom_call" | custom-call | flops 2684354560 | bytes 8388608 | tf_op jit(solution)/shard_map/attend_backward/pallas_call | solution.py:273
  521.5 13.1 %pad_maximum_fusion = bf16[1024,3072]{0,1:T(8,128)(2,1)} fusion(bf16[1024,1024]{0,1:T(8,128)(2,1)S(1)} %convolution_convert_fusion.3, bf16[1024,1024]{0,1:T(8,128)(2,1)S(1)} %convolution_convert_fusion.4, bf16[1024,1024]{0,1:T(8,128)(2,1)S(1)} %convolution_convert_fusion.5), kind=kLoop, calls=%fused_computation.8 | loop fusion | flops 18874368 | bytes 12582912 | tf_op jit(solution)/shard_map/concatenate | solution.py:556
  534.6 8.7 %copy.66 = bf16[1024,3072]{1,0:T(8,128)(2,1)} copy(bf16[1024,3072]{0,1:T(8,128)(2,1)} %pad_maximum_fusion) | data formatting | bytes 12582912 | tf_op jit(solution)/shard_map/concatenate | solution.py:556
  633.2 33.7 %collective-permute-done.15 = bf16[2,2,32,3072]{3,2,1,0:T(8,128)(2,1)} collective-permute-done((bf16[2,2,32,3072]{3,2,1,0:T(8,128)(2,1)}, bf16[2,2,32,3072]{3,2,1,0:T(8,128)(2,1)}, u32[]{:S(2)}, u32[]{:S(2)}) %collective-permute-start.15) | collective-permute-done | bytes 786464 | tf_op jit(solution)/shard_map/ppermute | solution.py:373
  673.6 13.8 %collective-permute-done.17 = bf16[2,2,32,3072]{3,2,1,0:T(8,128)(2,1)S(1)} collective-permute-done((bf16[2,2,32,3072]{3,2,1,0:T(8,128)(2,1)S(1)}, bf16[2,2,32,3072]{3,2,1,0:T(8,128)(2,1)S(1)}, u32[]{:S(2)}, u32[]{:S(2)}) %collective-permute-start.17) | collective-permute-done | bytes 786464 | tf_op jit(solution)/shard_map/ppermute | solution.py:373
  688.4 7.4 collective-permute-done.16
  699.1 30.4 %collective-permute-done.32 = bf16[2,32,4096]{2,1,0:T(8,128)(2,1)S(1)} collective-permute-done((bf16[2,32,4096]{2,1,0:T(8,128)(2,1)S(1)}, bf16[2,32,4096]{2,1,0:T(8,128)(2,1)S(1)}, u32[]{:S(2)}, u32[]{:S(2)}) %collective-permute-start.32) | collective-permute-done | bytes 524320 | tf_op jit(solution)/shard_map/ppermute | solution.py:373
  733.1 28.5 %collective-permute-done.40 = bf16[2,1024,128]{1,2,0:T(8,128)(2,1)S(1)} collective-permute-done((bf16[2,1024,128]{1,2,0:T(8,128)(2,1)S(1)}, bf16[2,1024,128]{1,2,0:T(8,128)(2,1)S(1)}, u32[]{:S(2)}, u32[]{:S(2)}) %collective-permute-start.40) | collective-permute-done | bytes 524320 | tf_op jit(solution)/shard_map/ppermute | solution.py:373
  764.1 7.0 collective-permute-done.18
  793.8 7.9 collective-permute-done.34
  812.6 11.4 %collective-permute-done.35 = bf16[32,4096]{1,0:T(8,128)(2,1)S(1)} collective-permute-done((bf16[32,4096]{1,0:T(8,128)(2,1)S(1)}, bf16[32,4096]{1,0:T(8,128)(2,1)S(1)}, u32[]{:S(2)}, u32[]{:S(2)}) %collective-permute-start.35) | collective-permute-done | bytes 262176 | tf_op jit(solution)/shard_map/ppermute | solution.py:405
  824.0 14.4 %collective-permute-done.36 = bf16[32,4096]{1,0:T(8,128)(2,1)S(1)} collective-permute-done((bf16[32,4096]{1,0:T(8,128)(2,1)S(1)}, bf16[32,4096]{1,0:T(8,128)(2,1)S(1)}, u32[]{:S(2)}, u32[]{:S(2)}) %collective-permute-start.36) | collective-permute-done | bytes 262176 | tf_op jit(solution)/shard_map/ppermute | solution.py:405
  841.3 8.1 collective-permute-done.45
  855.4 8.1 collective-permute-done.50
  (320 shorter events, 230.7 us)
Async XLA Ops:
  89.8 279.4 %collective-permute-start = (bf16[160,2048]{1,0:T(8,128)(2,1)}, bf16[160,2048]{1,0:T(8,128)(2,1)}, u32[]{:S(2)}, u32[]{:S(2)}) collective-permute-start(bf16[160,2048]{1,0:T(8,128)(2,1)} %get-tuple-element.98), channel_id=1, source_target_pairs={{0,1},{1,2},{2,3},{3,0},{4,5},{5,6},{6,7},{7,4},{8,9},{9,10},{10,1... | collective-permute-start | bytes 1966088 | tf_op jit(solution)/shard_map/ppermute | solution.py:519
  94.1 275.1 %collective-permute-start.1 = (bf16[160,2048]{1,0:T(8,128)(2,1)}, bf16[160,2048]{1,0:T(8,128)(2,1)}, u32[]{:S(2)}, u32[]{:S(2)}) collective-permute-start(bf16[160,2048]{1,0:T(8,128)(2,1)} %get-tuple-element.97), channel_id=1, source_target_pairs={{0,2},{1,3},{2,0},{3,1},{4,6},{5,7},{6,4},{7,5},{8,10},{9,11},{10,... | collective-permute-start | bytes 1966088 | tf_op jit(solution)/shard_map/ppermute | solution.py:519
  95.8 273.4 %collective-permute-start.2 = (bf16[160,2048]{1,0:T(8,128)(2,1)}, bf16[160,2048]{1,0:T(8,128)(2,1)}, u32[]{:S(2)}, u32[]{:S(2)}) collective-permute-start(bf16[160,2048]{1,0:T(8,128)(2,1)} %get-tuple-element.96), channel_id=1, source_target_pairs={{0,3},{1,0},{2,1},{3,2},{4,7},{5,4},{6,5},{7,6},{8,11},{9,8},{10,9... | collective-permute-start | bytes 1966088 | tf_op jit(solution)/shard_map/ppermute | solution.py:519
  368.8 224.7 %collective-permute-start.38 = (bf16[4,2,2,1024,128]{3,4,2,1,0:T(8,128)(2,1)}, bf16[4,2,2,1024,128]{3,4,2,1,0:T(8,128)(2,1)}, u32[]{:S(2)}, u32[]{:S(2)}) collective-permute-start(bf16[4,2,2,1024,128]{3,4,2,1,0:T(8,128)(2,1)} %bitcast.551), channel_id=1, source_target_pairs={{0,4},{4,0},{8,12},{12,8},{16,20},{20,16},{24,28},{28,24},{1,5},{5... | collective-permute-start | bytes 12582920 | tf_op jit(solution)/shard_map/ppermute | solution.py:373
  418.5 28.6 %collective-permute-start.3 = (bf16[160,2048]{1,0:T(8,128)(2,1)}, bf16[160,2048]{1,0:T(8,128)(2,1)}, u32[]{:S(2)}, u32[]{:S(2)}) collective-permute-start(bf16[160,2048]{1,0:T(8,128)(2,1)} %get-tuple-element.92), channel_id=1, source_target_pairs={{0,3},{1,0},{2,1},{3,2},{4,7},{5,4},{6,5},{7,6},{8,11},{9,8},{10,9... | collective-permute-start | bytes 1966088 | tf_op jit(solution)/shard_map/ppermute | solution.py:519
  420.4 58.7 %collective-permute-start.4 = (bf16[160,2048]{1,0:T(8,128)(2,1)}, bf16[160,2048]{1,0:T(8,128)(2,1)}, u32[]{:S(2)}, u32[]{:S(2)}) collective-permute-start(bf16[160,2048]{1,0:T(8,128)(2,1)} %get-tuple-element.91), channel_id=1, source_target_pairs={{0,2},{1,3},{2,0},{3,1},{4,6},{5,7},{6,4},{7,5},{8,10},{9,11},{10,... | collective-permute-start | bytes 1966088 | tf_op jit(solution)/shard_map/ppermute | solution.py:519
  421.9 57.2 %collective-permute-start.5 = (bf16[160,2048]{1,0:T(8,128)(2,1)}, bf16[160,2048]{1,0:T(8,128)(2,1)}, u32[]{:S(2)}, u32[]{:S(2)}) collective-permute-start(bf16[160,2048]{1,0:T(8,128)(2,1)} %get-tuple-element.90), channel_id=1, source_target_pairs={{0,1},{1,2},{2,3},{3,0},{4,5},{5,6},{6,7},{7,4},{8,9},{9,10},{10,1... | collective-permute-start | bytes 1966088 | tf_op jit(solution)/shard_map/ppermute | solution.py:519
  427.0 174.9 %collective-permute-start.30 = (bf16[4,2,2,32,4096]{4,3,2,1,0:T(8,128)(2,1)}, bf16[4,2,2,32,4096]{4,3,2,1,0:T(8,128)(2,1)}, u32[]{:S(2)}, u32[]{:S(2)}) collective-permute-start(bf16[4,2,2,32,4096]{4,3,2,1,0:T(8,128)(2,1)} %dynamic-slice_bitcast_fusion.2), channel_id=1, source_target_pairs={{0,4},{4,0},{8,12},{12,8},{16,20},{20,16},{24,28},{28,24},{1,5},{5... | collective-permute-start | bytes 12582920 | tf_op jit(solution)/shard_map/ppermute | solution.py:373
  521.5 43.1 %collective-permute-start.22 = (bf16[4,2,2,32,1024]{4,3,2,1,0:T(8,128)(2,1)}, bf16[4,2,2,32,1024]{4,3,2,1,0:T(8,128)(2,1)}, u32[]{:S(2)}, u32[]{:S(2)}) collective-permute-start(bf16[4,2,2,32,1024]{4,3,2,1,0:T(8,128)(2,1)} %dynamic-slice_bitcast_fusion.4), channel_id=1, source_target_pairs={{0,4},{4,0},{8,12},{12,8},{16,20},{20,16},{24,28},{28,24},{1,5},{5... | collective-permute-start | bytes 3145736 | tf_op jit(solution)/shard_map/ppermute | solution.py:373
  592.3 34.3 %collective-permute-start.46 = (bf16[4,2,512,512]{3,2,1,0:T(8,128)(2,1)}, bf16[4,2,512,512]{3,2,1,0:T(8,128)(2,1)}, u32[]{:S(2)}, u32[]{:S(2)}) collective-permute-start(bf16[4,2,512,512]{3,2,1,0:T(8,128)(2,1)} %dynamic-slice_bitcast_fusion.1), channel_id=1, source_target_pairs={{0,4},{4,0},{8,12},{12,8},{16,20},{20,16},{24,28},{28,24},{1,5},{5... | collective-permute-start | bytes 12582920 | tf_op jit(solution)/shard_map/ppermute | solution.py:373
  600.4 131.7 %collective-permute-start.41 = (bf16[2,2,1024,128]{2,3,1,0:T(8,128)(2,1)}, bf16[2,2,1024,128]{2,3,1,0:T(8,128)(2,1)}, u32[]{:S(2)}, u32[]{:S(2)}) collective-permute-start(bf16[2,2,1024,128]{2,3,1,0:T(8,128)(2,1)} %pad_maximum_fusion.10), channel_id=1, source_target_pairs={{0,16},{4,20},{8,24},{12,28},{16,0},{20,4},{24,8},{28,12},{1,17},{... | collective-permute-start | bytes 3145736 | tf_op jit(solution)/shard_map/ppermute | solution.py:373
  602.0 69.3 %collective-permute-start.39 = (bf16[2,2,1024,128]{2,3,1,0:T(8,128)(2,1)}, bf16[2,2,1024,128]{2,3,1,0:T(8,128)(2,1)}, u32[]{:S(2)}, u32[]{:S(2)}) collective-permute-start(bf16[2,2,1024,128]{2,3,1,0:T(8,128)(2,1)} %pad_maximum_fusion.9), channel_id=1, source_target_pairs={{0,8},{4,12},{8,0},{12,4},{16,24},{20,28},{24,16},{28,20},{1,9},{5... | collective-permute-start | bytes 3145736 | tf_op jit(solution)/shard_map/ppermute | solution.py:373
  612.5 85.6 %collective-permute-start.33 = (bf16[2,2,32,4096]{3,2,1,0:T(8,128)(2,1)}, bf16[2,2,32,4096]{3,2,1,0:T(8,128)(2,1)}, u32[]{:S(2)}, u32[]{:S(2)}) collective-permute-start(bf16[2,2,32,4096]{3,2,1,0:T(8,128)(2,1)} %pad_maximum_fusion.8), channel_id=1, source_target_pairs={{0,16},{4,20},{8,24},{12,28},{16,0},{20,4},{24,8},{28,12},{1,17},{... | collective-permute-start | bytes 3145736 | tf_op jit(solution)/shard_map/ppermute | solution.py:373
  621.0 48.1 %collective-permute-start.31 = (bf16[2,2,32,4096]{3,2,1,0:T(8,128)(2,1)}, bf16[2,2,32,4096]{3,2,1,0:T(8,128)(2,1)}, u32[]{:S(2)}, u32[]{:S(2)}) collective-permute-start(bf16[2,2,32,4096]{3,2,1,0:T(8,128)(2,1)} %pad_maximum_fusion.7), channel_id=1, source_target_pairs={{0,8},{4,12},{8,0},{12,4},{16,24},{20,28},{24,16},{28,20},{1,9},{5... | collective-permute-start | bytes 3145736 | tf_op jit(solution)/shard_map/ppermute | solution.py:373
  626.6 40.3 %collective-permute-start.15 = (bf16[2,2,32,3072]{3,2,1,0:T(8,128)(2,1)}, bf16[2,2,32,3072]{3,2,1,0:T(8,128)(2,1)}, u32[]{:S(2)}, u32[]{:S(2)}) collective-permute-start(bf16[2,2,32,3072]{3,2,1,0:T(8,128)(2,1)} %pad_maximum_fusion.15), channel_id=1, source_target_pairs={{0,8},{4,12},{8,0},{12,4},{16,24},{20,28},{24,16},{28,20},{1,9},{5... | collective-permute-start | bytes 2359304 | tf_op jit(solution)/shard_map/ppermute | solution.py:373
  671.3 131.9 %collective-permute-start.54 = (bf16[2,512,512]{2,1,0:T(8,128)(2,1)S(1)}, bf16[2,512,512]{2,1,0:T(8,128)(2,1)S(1)}, u32[]{:S(2)}, u32[]{:S(2)}) collective-permute-start(bf16[2,512,512]{2,1,0:T(8,128)(2,1)S(1)} %pad_maximum_fusion.14), channel_id=1, source_target_pairs={{0,16},{4,20},{8,24},{12,28},{16,0},{20,4},{24,8},{28,12},{1,17},{... | collective-permute-start | bytes 3145736 | tf_op jit(solution)/shard_map/ppermute | solution.py:373
  687.4 76.5 %collective-permute-start.52 = (bf16[2,512,512]{2,1,0:T(8,128)(2,1)S(1)}, bf16[2,512,512]{2,1,0:T(8,128)(2,1)S(1)}, u32[]{:S(2)}, u32[]{:S(2)}) collective-permute-start(bf16[2,512,512]{2,1,0:T(8,128)(2,1)S(1)} %pad_maximum_fusion.13), channel_id=1, source_target_pairs={{0,8},{4,12},{8,0},{12,4},{16,24},{20,28},{24,16},{28,20},{1,9},{5... | collective-permute-start | bytes 3145736 | tf_op jit(solution)/shard_map/ppermute | solution.py:373
  695.8 33.7 %collective-permute-start.32 = (bf16[2,32,4096]{2,1,0:T(8,128)(2,1)S(1)}, bf16[2,32,4096]{2,1,0:T(8,128)(2,1)S(1)}, u32[]{:S(2)}, u32[]{:S(2)}) collective-permute-start(bf16[2,32,4096]{2,1,0:T(8,128)(2,1)S(1)} %fusion.61), channel_id=1, source_target_pairs={{0,16},{4,20},{8,24},{12,28},{16,0},{20,4},{24,8},{28,12},{1,17},{... | collective-permute-start | bytes 1572872 | tf_op jit(solution)/shard_map/ppermute | solution.py:373
  698.1 109.9 %collective-permute-start.49 = (bf16[2,512,512]{2,1,0:T(8,128)(2,1)S(1)}, bf16[2,512,512]{2,1,0:T(8,128)(2,1)S(1)}, u32[]{:S(2)}, u32[]{:S(2)}) collective-permute-start(bf16[2,512,512]{2,1,0:T(8,128)(2,1)S(1)} %pad_maximum_fusion.12), channel_id=1, source_target_pairs={{0,16},{4,20},{8,24},{12,28},{16,0},{20,4},{24,8},{28,12},{1,17},{... | collective-permute-start | bytes 3145736 | tf_op jit(solution)/shard_map/ppermute | solution.py:373
  729.5 32.1 %collective-permute-start.40 = (bf16[2,1024,128]{1,2,0:T(8,128)(2,1)S(1)}, bf16[2,1024,128]{1,2,0:T(8,128)(2,1)S(1)}, u32[]{:S(2)}, u32[]{:S(2)}) collective-permute-start(bf16[2,1024,128]{1,2,0:T(8,128)(2,1)S(1)} %fusion.56), channel_id=1, source_target_pairs={{0,16},{4,20},{8,24},{12,28},{16,0},{20,4},{24,8},{28,12},{1,17},{... | collective-permute-start | bytes 1572872 | tf_op jit(solution)/shard_map/ppermute | solution.py:373
  732.1 43.3 %collective-permute-start.47 = (bf16[2,512,512]{2,1,0:T(8,128)(2,1)S(1)}, bf16[2,512,512]{2,1,0:T(8,128)(2,1)S(1)}, u32[]{:S(2)}, u32[]{:S(2)}) collective-permute-start(bf16[2,512,512]{2,1,0:T(8,128)(2,1)S(1)} %pad_maximum_fusion.11), channel_id=1, source_target_pairs={{0,8},{4,12},{8,0},{12,4},{16,24},{20,28},{24,16},{28,20},{1,9},{5... | collective-permute-start | bytes 3145736 | tf_op jit(solution)/shard_map/ppermute | solution.py:373
  801.6 39.7 %collective-permute-start.43 = (bf16[1024,128]{0,1:T(8,128)(2,1)S(1)}, bf16[1024,128]{0,1:T(8,128)(2,1)S(1)}, u32[]{:S(2)}, u32[]{:S(2)}) collective-permute-start(bf16[1024,128]{0,1:T(8,128)(2,1)S(1)} %get-tuple-element.99), channel_id=1, source_target_pairs={{0,1},{1,2},{2,3},{3,0},{4,5},{5,6},{6,7},{7,4},{8,9},{9,10},{10,1... | collective-permute-start | bytes 786440 | tf_op jit(solution)/shard_map/ppermute | solution.py:405
  803.2 38.1 %collective-permute-start.44 = (bf16[1024,128]{0,1:T(8,128)(2,1)S(1)}, bf16[1024,128]{0,1:T(8,128)(2,1)S(1)}, u32[]{:S(2)}, u32[]{:S(2)}) collective-permute-start(bf16[1024,128]{0,1:T(8,128)(2,1)S(1)} %get-tuple-element.101), channel_id=1, source_target_pairs={{0,2},{1,3},{2,0},{3,1},{4,6},{5,7},{6,4},{7,5},{8,10},{9,11},{10,... | collective-permute-start | bytes 786440 | tf_op jit(solution)/shard_map/ppermute | solution.py:405
  808.0 30.4 %collective-permute-start.36 = (bf16[32,4096]{1,0:T(8,128)(2,1)S(1)}, bf16[32,4096]{1,0:T(8,128)(2,1)S(1)}, u32[]{:S(2)}, u32[]{:S(2)}) collective-permute-start(bf16[32,4096]{1,0:T(8,128)(2,1)S(1)} %get-tuple-element.104), channel_id=1, source_target_pairs={{0,2},{1,3},{2,0},{3,1},{4,6},{5,7},{6,4},{7,5},{8,10},{9,11},{10,... | collective-permute-start | bytes 786440 | tf_op jit(solution)/shard_map/ppermute | solution.py:405
  (70 other events, 844.7 us)

commit v2 on v1

v2 whole, which is shorter than its diff:
```python
import functools
import math

import jax
import jax.numpy as jnp
from jax import lax
from jax.experimental import pallas as pl
from jax.experimental.pallas import tpu as pltpu
from jax.sharding import PartitionSpec as P

HD = 64
PAIR = 2 * HD
SEQ = 512
QB = 256
BLOCK = 512
MIB = 1 << 20
AXES = ("node", "expert")
MESH = pl.DeviceIdType.MESH
highest = lax.Precision.HIGHEST
epsilon = 1e-05
f32 = jnp.float32
bf16 = jnp.bfloat16


def normalize(values):
    centered = values - jnp.mean(values, axis=-1, keepdims=True)
    inv_scale = lax.rsqrt(jnp.mean(centered * centered, axis=-1, keepdims=True) + epsilon)
    return (centered * inv_scale, inv_scale)


def norm_back(grad_norm, normed, inv_scale):
    mean_grad = jnp.mean(grad_norm, axis=-1, keepdims=True)
    mean_cross = jnp.mean(grad_norm * normed, axis=-1, keepdims=True)
    return inv_scale * (grad_norm - mean_grad - normed * mean_cross)


def contract(left_op, right_op, left_dim, right_dim):
    return lax.dot_general(
        left_op, right_op, (((left_dim,), (right_dim,)), ((), ())), preferred_element_type=f32
    )


def matmul(left_op, right_op):
    return contract(left_op, right_op, 1, 0)


def product_tn(left_op, right_op):
    return contract(left_op, right_op, 0, 0)


def outer_nt(left_op, right_op):
    return contract(left_op, right_op, 1, 1)


class Place:
    def __init__(self, experts):
        self.experts = experts
        self.n, self.e = lax.axis_index("node"), lax.axis_index("expert")
        n = self.n
        self.k, self.x, self.y = lax.rem(n, 2), lax.rem(n // 2, 2), n // 4
        k, x, y = self.k, self.x, self.y
        self.nx, self.ny = y * 4 + (1 - x) * 2 + k, (1 - y) * 4 + x * 2 + k
        self.nd, self.nc = (1 - y) * 4 + (1 - x) * 2 + k, y * 4 + x * 2 + 1 - k

    def z(self, j):
        return (self.n, lax.rem(self.e + j, self.experts))

    def greet(self, along_z):
        barrier = pltpu.get_barrier_semaphore()
        peers = [(self.nx, self.e), (self.ny, self.e), (self.nc, self.e)]
        if along_z:
            peers += [self.z(j) for j in range(1, self.experts)]
        for peer in peers:
            pl.semaphore_signal(barrier, inc=1, device_id=peer, device_id_type=MESH)
        pl.semaphore_wait(barrier, len(peers))


def when(condition):
    return pl.when(condition)


class Gather:
    late = 4

    def __init__(self, args, dense, items, nodes, experts):
        self.args, self.dense, self.items, self.experts = args, dense, items, experts
        self.outs = [
            jax.ShapeDtypeStruct(((nodes * experts if d else nodes),) + a.shape, a.dtype)
            for a, d in zip(args, dense)
        ]
        hbm = pl.BlockSpec(memory_space=pltpu.HBM)
        self.in_specs, self.out_specs = [hbm] * len(args), [hbm] * len(args)
        m = len(items)
        self.scratch = [
            pltpu.SemaphoreType.DMA((m, experts + 7)),
            pltpu.SemaphoreType.DMA((m, experts + 7)),
            pltpu.SemaphoreType.DMA((m,)),
        ]
        self.turns = m + self.late
        self.along_z = any(dense)

    def bind(self, ins, outs, scratch, place):
        experts = self.experts
        send, recv, loc = scratch
        p, e = place, place.e

        def remote(source, target, item, kind, device):
            return pltpu.make_async_remote_copy(
                src_ref=source,
                dst_ref=target,
                send_sem=send.at[item, kind],
                recv_sem=recv.at[item, kind],
                device_id=device,
                device_id_type=MESH,
            )

        self.bound = []
        for i, (arg, start, size) in enumerate(self.items):
            dense = self.dense[arg]
            cols = pl.ds(start, size)
            shard, whole = ins[arg], outs[arg]
            rows = shard.shape[0]
            per = experts if dense else 1
            own = p.n * per + (e if dense else 0)

            def bundle(m, whole=whole, per=per, cols=cols):
                return whole.at[pl.ds(m * per, per), :, cols]

            def half(m, h, whole=whole, per=per, cols=cols, dense=dense, rows=rows):
                if dense:
                    return whole.at[pl.ds(m * per + h * (per // 2), per // 2), :, cols]
                return whole.at[m, pl.ds(h * (rows // 2), rows // 2), cols]

            mine = shard.at[:, cols]
            local = pltpu.make_async_copy(mine, whole.at[own, :, cols], loc.at[i])
            z = []
            if dense:
                z = [remote(mine, whole.at[own, :, cols], i, j - 1, p.z(j)) for j in range(1, experts)]
                first, land = bundle(p.n), bundle(p.n)
            else:
                first, land = mine, whole.at[p.n, :, cols]
            b = experts - 1
            xy = [remote(first, land, i, b, (p.nx, e)), remote(first, land, i, b + 1, (p.ny, e))]
            diag = [
                remote(half(p.nx, 0), half(p.nx, 0), i, b + 2, (p.ny, e)),
                remote(half(p.ny, 1), half(p.ny, 1), i, b + 3, (p.nx, e)),
            ]
            core = [remote(first, land, i, b + 4, (p.nc, e))] + [
                remote(bundle(m), bundle(m), i, b + 5 + j, (p.nc, e)) for j, m in enumerate((p.nx, p.ny, p.nd))
            ]
            self.bound.append((local, z, xy, diag, core))

    def turn(self, now):
        steps = (self.along, self.across, self.corner, self.over, self.end)
        for t in range(self.turns):

            @when(now == t)
            def _(t=t):
                for late, step in enumerate(steps):
                    if 0 <= t - late < len(self.items):
                        step(*self.bound[t - late])

    def along(self, local, z, xy, diag, core):
        local.start()
        for copy in z:
            copy.start()

    def across(self, local, z, xy, diag, core):
        for copy in z:
            copy.wait()
        local.wait()
        xy[0].start()
        xy[1].start()
        core[0].start()

    def corner(self, local, z, xy, diag, core):
        for i in range(2):
            xy[i].wait()
            diag[i].start()
            core[1 + i].start()

    def over(self, local, z, xy, diag, core):
        diag[0].wait()
        diag[1].wait()
        core[3].start()

    def end(self, local, z, xy, diag, core):
        for copy in core:
            copy.wait()


class Scatter:
    def __init__(self, arrays, layout, experts):
        self.args, self.layout, self.experts = arrays, layout, experts
        dense = self.dense = layout != "plane"
        shape = arrays[0].shape
        if layout == "plane":
            counts, h = [a.shape[2] for a in arrays], shape[4:]
        elif layout == "rows":
            counts, h = [a.shape[4] for a in arrays], shape[3:4] + shape[5:]
        else:
            counts, h = [a.shape[5] // BLOCK for a in arrays], shape[3:5] + (BLOCK,)
        self.starts = [sum(counts[:a]) for a in range(len(arrays) + 1)]
        m = self.m = sum(counts)
        self.half = h
        unit = h[1:] if dense else (2,) + h
        self.outs = [jax.ShapeDtypeStruct((m,) + unit, f32)]
        self.in_specs = [pl.BlockSpec(memory_space=pltpu.HBM)] * len(arrays)
        self.out_specs = [pl.BlockSpec(memory_space=pltpu.VMEM)]
        kinds = 7 + experts
        self.scratch = [
            pltpu.VMEM((m, 4, 2) + h, bf16),
            pltpu.VMEM((m, 4, 2) + h, bf16),
            pltpu.VMEM((m, 2) + h, bf16),
            pltpu.VMEM((m, 2) + h, bf16),
            pltpu.VMEM((m,) + h, bf16),
            pltpu.VMEM((m,) + h, bf16),
            pltpu.SemaphoreType.DMA((m, kinds)),
            pltpu.SemaphoreType.DMA((m, kinds)),
            pltpu.SemaphoreType.DMA((m,)),
        ]
        if dense:
            self.scratch.append(pltpu.VMEM((m, experts - 1) + unit, bf16))
        self.late = 4 if dense else 3
        self.turns = m + self.late
        self.along_z = dense

    def bind(self, ins, outs, scratch, place):
        self.ins, self.out, self.place = ins, outs[0], place
        self.own, self.rc, self.rx, self.ry, self.lx, self.ly, self.send, self.recv, self.loc = scratch[:9]
        self.rz = scratch[9] if self.dense else None

    def remote(self, source, target, item, kind, device):
        return pltpu.make_async_remote_copy(
            src_ref=source,
            dst_ref=target,
            send_sem=self.send.at[item, kind],
            recv_sem=self.recv.at[item, kind],
            device_id=device,
            device_id_type=MESH,
        )

    def part(self, source, core, chunk):
        if self.layout == "plane":
            return source.at[:, core, chunk]
        if self.layout == "rows":
            return source.at[:, core, :, :, chunk]
        return source.at[:, core, :, :, :, pl.ds(pl.multiple_of(chunk * BLOCK, BLOCK), BLOCK)]

    def first(self, source, i, chunk):
        p = self.place
        local = pltpu.make_async_copy(self.part(source, p.k, chunk), self.own.at[i], self.loc.at[i])
        over = self.remote(self.part(source, 1 - p.k, chunk), self.rc.at[i], i, 0, (p.nc, p.e))
        return local, over

    def sites(self):
        p = self.place
        return p.y * 2 + p.x, p.y * 2 + 1 - p.x, (1 - p.y) * 2 + p.x, (1 - p.y) * 2 + 1 - p.x

    def round_one(self, i):
        p = self.place
        _, to_x, to_y, diag = self.sites()
        return [
            self.remote(self.own.at[i, diag, 0], self.rx.at[i, 0], i, 1, (p.nx, p.e)),
            self.remote(self.own.at[i, diag, 1], self.ry.at[i, 0], i, 2, (p.ny, p.e)),
            self.remote(self.own.at[i, to_x, 0], self.rx.at[i, 1], i, 3, (p.nx, p.e)),
            self.remote(self.own.at[i, to_y, 1], self.ry.at[i, 1], i, 4, (p.ny, p.e)),
        ]

    def round_two(self, i):
        p = self.place
        _, to_x, to_y, _ = self.sites()
        return [
            self.remote(self.own.at[i, to_x, 1], self.lx.at[i], i, 5, (p.nx, p.e)),
            self.remote(self.own.at[i, to_y, 0], self.ly.at[i], i, 6, (p.ny, p.e)),
        ]

    def round_z(self, i):
        p = self.place
        mine, _, _, _ = self.sites()
        s = self.experts // 2
        copies = []
        for j in range(1, self.experts):
            to = lax.rem(p.e + j, self.experts)
            source = self.own.at[i, mine, to // s, lax.rem(to, s)]
            copies.append(self.remote(source, self.rz.at[i, j - 1], i, 6 + j, p.z(j)))
        return copies

    def turn(self, now):
        steps = (self.load, self.chip, self.cross, self.plane, self.column)
        for late, step in enumerate(steps[: self.late + 1]):
            i = now - late

            @when(jnp.logical_and(i >= 0, i < self.m))
            def _(step=step, i=i):
                step(i)

    def load(self, i):
        for a, source in enumerate(self.ins):

            @when(jnp.logical_and(i >= self.starts[a], i < self.starts[a + 1]))
            def _(a=a, source=source):
                local, over = self.first(source, i, i - self.starts[a])
                over.start()
                local.start()

    def chip(self, i):
        local, over = self.first(self.ins[0], i, 0)
        local.wait()
        over.wait()

        def sum_one(q, _):
            self.own[i, q] = add(self.own[i, q], self.rc[i, q]).astype(bf16)
            return 0

        lax.fori_loop(0, 4, sum_one, 0)
        for copy in self.round_one(i):
            copy.start()

    def cross(self, i):
        one = self.round_one(i)
        two = self.round_two(i)
        _, to_x, to_y, _ = self.sites()
        for copy in one:
            copy.wait()
        self.own[i, to_x, 1] = add(self.own[i, to_x, 1], self.ry[i, 0]).astype(bf16)
        two[0].start()
        self.own[i, to_y, 0] = add(self.own[i, to_y, 0], self.rx[i, 0]).astype(bf16)
        two[1].start()

    def plane(self, i):
        for copy in self.round_two(i):
            copy.wait()
        mine, _, _, _ = self.sites()
        sums = (
            add(self.own[i, mine, 0], self.rx[i, 1], self.ly[i]),
            add(self.own[i, mine, 1], self.lx[i], self.ry[i, 1]),
        )
        if not self.dense:
            for h in range(2):
                self.out[i, h] = sums[h]
            return
        for h in range(2):
            self.own[i, mine, h] = sums[h].astype(bf16)
        for copy in self.round_z(i):
            copy.start()

    def column(self, i):
        for copy in self.round_z(i):
            copy.wait()
        p = self.place
        mine, _, _, _ = self.sites()
        s = self.experts // 2
        terms = [self.own[i, mine, p.e // s, lax.rem(p.e, s)]] + [self.rz[i, j] for j in range(self.experts - 1)]
        self.out[i] = add(*terms)


def add(*terms):
    return functools.reduce(jnp.add, [t.astype(f32) for t in terms])


def call(name, steps, body, args, in_specs, outs, out_specs, scratch, moves, collective_id, experts, flops):
    total = max(steps, moves.turns if moves else 0)

    def hold(spec):
        if spec.block_shape is None:
            return spec
        index = spec.index_map
        return pl.BlockSpec(spec.block_shape, lambda j: index(jnp.minimum(j, steps - 1)))

    n_in, n_out, n_scratch = len(args), len(outs), len(scratch)
    m_in, m_out = (len(moves.args), len(moves.outs)) if moves else (0, 0)

    def kernel(*refs):
        refs = list(refs)
        take = lambda count: [refs.pop(0) for _ in range(count)]
        ins, m_ins, os, m_os, own = take(n_in), take(m_in), take(n_out), take(m_out), take(n_scratch)
        now = pl.program_id(0)
        if moves:
            place = Place(experts)
            moves.bind(m_ins, m_os, refs, place)

            @when(now == 0)
            def _():
                place.greet(moves.along_z)

            moves.turn(now)
        if body is not None:

            @when(now < steps)
            def _():
                body(now, steps, *ins, *os, *own)

    return pl.pallas_call(
        kernel,
        grid=(total,),
        out_shape=list(outs) + (moves.outs if moves else []),
        in_specs=[hold(s) for s in in_specs] + (moves.in_specs if moves else []),
        out_specs=[hold(s) for s in out_specs] + (moves.out_specs if moves else []),
        scratch_shapes=list(scratch) + (moves.scratch if moves else []),
        cost_estimate=pl.CostEstimate(flops=flops, bytes_accessed=32 * MIB, transcendentals=0),
        compiler_params=pltpu.CompilerParams(
            vmem_limit_bytes=60 * MIB,
            **({"collective_id": collective_id, "has_side_effects": True} if moves else {}),
        ),
        name=name,
    )(*args, *(moves.args if moves else []))


def masks():
    lanes = lax.broadcasted_iota(jnp.int32, (1, PAIR), 1)
    return [(lanes // HD == h).astype(bf16) for h in range(2)]


def causal(scores_t, start):
    keys = lax.broadcasted_iota(jnp.int32, scores_t.shape, 0)
    queries = lax.broadcasted_iota(jnp.int32, scores_t.shape, 1) + start
    return jnp.where(keys <= queries, scores_t, -jnp.inf)


def attend_forward_kernel(q_ref, k_ref, v_ref, o_ref, lse_ref):
    q = q_ref[...] * (1.0 / math.sqrt(HD))
    k = k_ref[...]
    vt = v_ref[...].T
    length = q.shape[0]
    outs = []
    for h, mask in enumerate(masks()):
        kh = k * mask
        row = []
        for start in range(0, length, QB):
            end = start + QB
            scores = causal(outer_nt(kh[:end], q[start:end]), start)
            top = jnp.max(scores, axis=0, keepdims=True)
            expd = jnp.exp(scores - top)
            total = jnp.sum(expd, axis=0, keepdims=True)
            probs = (expd / total).astype(bf16)
            row.append(matmul(vt[h * HD : (h + 1) * HD, :end], probs))
            lse_ref[0, h : h + 1, start:end] = top + jnp.log(total)
        outs.append(jnp.concatenate(row, axis=1))
    o_ref[...] = jnp.concatenate(outs, axis=0).T.astype(bf16)


def attend_forward(qkv, width, moves, collective_id, experts):
    length = qkv.shape[0]
    pairs = width // PAIR
    part = lambda p: pl.BlockSpec((SEQ, PAIR), lambda j: (j // pairs, p * pairs + lax.rem(j, pairs)))
    steps = length // SEQ * pairs
    return call(
        "attend_forward",
        steps,
        lambda now, steps, *refs: attend_forward_kernel(*refs),
        [qkv] * 3,
        [part(0), part(1), part(2)],
        [
            jax.ShapeDtypeStruct((length, width), bf16),
            jax.ShapeDtypeStruct((steps, 2, SEQ), f32),
        ],
        [part(0), pl.BlockSpec((1, 2, SEQ), lambda j: (j, 0, 0))],
        [],
        moves,
        collective_id,
        experts,
        4 * length * SEQ * width,
    )


def attend_backward_kernel(q_ref, k_ref, v_ref, g_ref, lse_ref, d_ref):
    scaling = 1.0 / math.sqrt(HD)
    q, k, v, g = q_ref[...], k_ref[...], v_ref[...], g_ref[...]
    qs = q * scaling
    kt = k.T
    length = q.shape[0]
    grad_k = [0.0] * (length // QB)
    grad_v = [0.0] * (length // QB)
    grad_q = []
    for h, mask in enumerate(masks()):
        kh, vh, qh, gh = k * mask, v * mask, q * mask, g * mask
        row = []
        for c, start in enumerate(range(0, length, QB)):
            end = start + QB
            scores = causal(outer_nt(kh[:end], qs[start:end]), start)
            probs = jnp.exp(scores - lse_ref[0, h : h + 1, start:end])
            grad_probs = outer_nt(vh[:end], g[start:end])
            delta = jnp.sum(probs * grad_probs, axis=0, keepdims=True)
            grad_scores = (probs * (grad_probs - delta)).astype(bf16)
            more_v = matmul(probs.astype(bf16), gh[start:end])
            more_k = matmul(grad_scores, qh[start:end])
            for b in range(c + 1):
                rows = slice(b * QB, (b + 1) * QB)
                grad_v[b] = grad_v[b] + more_v[rows]
                grad_k[b] = grad_k[b] + more_k[rows]
            row.append(matmul(kt[h * HD : (h + 1) * HD, :end], grad_scores))
        grad_q.append(jnp.concatenate(row, axis=1))
    d_ref[0] = (jnp.concatenate(grad_q, axis=0).T * scaling).astype(bf16)
    for b in range(length // QB):
        d_ref[1, b * QB : (b + 1) * QB] = (grad_k[b] * scaling).astype(bf16)
        d_ref[2, b * QB : (b + 1) * QB] = grad_v[b].astype(bf16)


def attend_backward(qkv, lse, grad, width, moves, collective_id, experts):
    length = qkv.shape[0]
    pairs = width // PAIR
    part = lambda p: pl.BlockSpec((SEQ, PAIR), lambda j: (j // pairs, p * pairs + lax.rem(j, pairs)))
    return call(
        "attend_backward",
        length // SEQ * pairs,
        lambda now, steps, *refs: attend_backward_kernel(*refs),
        [qkv, qkv, qkv, grad, lse],
        [part(0), part(1), part(2), part(0), pl.BlockSpec((1, 2, SEQ), lambda j: (j, 0, 0))],
        [jax.ShapeDtypeStruct((3, length, width), bf16)],
        [pl.BlockSpec((3, SEQ, PAIR), lambda j: (0, j // pairs, lax.rem(j, pairs)))],
        [],
        moves,
        collective_id,
        experts,
        10 * length * SEQ * width,
    )


def gelu_both(v):
    c = math.sqrt(2.0 / math.pi)
    square = v * v
    t = jnp.tanh(c * (v + 0.044715 * (square * v)))
    half = 0.5 * (1.0 + t)
    slope = half + 0.5 * v * (1.0 - t * t) * (c * (1.0 + (3 * 0.044715) * square))
    return v * half, slope


def mlp_kernel(share, now, steps, x_ref, g_ref, w1_ref, w2_ref, out_ref, back_ref, d1_ref, d2_ref, xt, gt, out_sum, back_sum):
    @when(now == 0)
    def _():
        xt[...] = x_ref[...].T
        gt[...] = g_ref[...].T
        out_sum[...] = jnp.zeros_like(out_sum)
        back_sum[...] = jnp.zeros_like(back_sum)

    w1 = w1_ref[...].reshape(w1_ref.shape[-2:])
    w2 = w2_ref[...].reshape(w2_ref.shape[-2:])
    hidden, slope = gelu_both(matmul(x_ref[...], w1))
    hidden = hidden.astype(bf16)
    grad_pre = (slope * outer_nt(g_ref[...], w2)).astype(bf16)
    out_sum[...] += matmul(hidden, w2)
    back_sum[...] += outer_nt(grad_pre, w1)
    d1 = matmul(xt[...], grad_pre).astype(bf16)
    d2 = matmul(gt[...], hidden).astype(bf16)
    if share is None:
        d1_ref[...] = d1.reshape(d1_ref.shape)
        d2_ref[...] = d2.reshape(d2_ref.shape)
    else:
        for c in range(d1.shape[1] // 128):
            cols = slice(c * 128, (c + 1) * 128)
            for s in range(d1_ref.shape[0]):
                d1_ref[s, c * share : (c + 1) * share] = d1[s * share : (s + 1) * share, cols]
            d2_ref[c] = d2[:, cols]

    @when(now == steps - 1)
    def _():
        out_ref[...] = out_sum[...].astype(out_ref.dtype)
        back_ref[...] = back_sum[...].astype(back_ref.dtype)


def mlp(x, g, w1, w2, out_dtype, name, moves, collective_id, experts, devices=None):
    rows, width = x.shape
    share = None
    if w1.ndim == 3:
        blocks, _, size = w1.shape
        w1_spec = pl.BlockSpec((1, width, size), lambda j: (j, 0, 0))
        w2_spec = pl.BlockSpec((1, size, width), lambda j: (j, 0, 0))
        d_shape, d_specs = (blocks, width, size), [w1_spec] * 2
    else:
        size = BLOCK
        blocks = w1.shape[1] // size
        w1_spec = pl.BlockSpec((width, size), lambda j: (0, j))
        w2_spec = pl.BlockSpec((size, width), lambda j: (j, 0))
        d_shape, d_specs = (width, blocks * size), [w1_spec] * 2
        if devices:
            share = width // devices
            d_shape = (devices, width, 128)
            d_specs = [
                pl.BlockSpec((devices, size // 128 * share, 128), lambda j: (0, j, 0)),
                pl.BlockSpec((size // 128, width, 128), lambda j: (j, 0, 0)),
            ]
    whole = pl.BlockSpec(memory_space=pltpu.VMEM)
    return call(
        name,
        blocks,
        functools.partial(mlp_kernel, share),
        [x, g, w1, w2],
        [whole, whole, w1_spec, w2_spec],
        [jax.ShapeDtypeStruct((rows, width), out_dtype)] * 2 + [jax.ShapeDtypeStruct(d_shape, bf16)] * 2,
        [whole, whole] + d_specs,
        [
            pltpu.VMEM((width, rows), bf16),
            pltpu.VMEM((width, rows), bf16),
            pltpu.VMEM((rows, width), f32),
            pltpu.VMEM((rows, width), f32),
        ],
        moves,
        collective_id,
        experts,
        12 * rows * width * blocks * size,
    )


def move(name, moves, collective_id, experts):
    return call(name, 1, None, [], [], [], [], [], moves, collective_id, experts, 0)


def shards(
    fast,
    tokens,
    gain_attn,
    w_qkv,
    w_out,
    gain_mix,
    w_fc,
    w_proj,
    w_router,
    w_coef,
    expert_in,
    expert_out,
    routes,
    dropped,
    cotangent,
):
    experts = lax.axis_size("expert")
    nodes = lax.axis_size("node")
    devices = nodes * experts
    width = tokens.shape[1]
    tok_rows = tokens.shape[0]
    ff = w_fc.shape[1]
    share = w_qkv.shape[0]
    small = jnp.concatenate([gain_attn[:, None], gain_mix[:, None], w_router, w_coef], axis=1)
    small = jnp.pad(small, ((0, 0), (0, 128 - small.shape[1])))
    win, wout = expert_in[0], expert_out[0]
    together = lambda a: a.reshape((devices * a.shape[1],) + a.shape[2:])
    cut = lambda a, d, m: [(a, i * (d // m), d // m) for i in range(m)]
    gather_dense = gather_experts = None
    if fast:
        first = Gather(
            [small, w_qkv, w_out],
            [True] * 3,
            [(0, 0, 128)] + cut(1, 3 * width, 3) + [(2, 0, width)],
            nodes,
            experts,
        )
        small_full, qkv_full, out_full = move("gather_first", first, 1, experts)
        gather_dense = Gather([w_fc, w_proj], [True] * 2, cut(0, ff, 4) + cut(1, width, 4), nodes, experts)
        gather_experts = Gather(
            [win, wout], [False] * 2, cut(0, win.shape[1], 4) + cut(1, width, 4), nodes, experts
        )
    else:
        small_full, qkv_full, out_full, fc_full, proj_full = (
            lax.all_gather(a, AXES, axis=0, tiled=False) for a in (small, w_qkv, w_out, w_fc, w_proj)
        )
        win_full, wout_full = (lax.all_gather(a, "node", axis=0, tiled=False) for a in (win, wout))
    small_full, qkv_full, out_full = (together(a) for a in (small_full, qkv_full, out_full))

    def scatter_xla(parts, axes):
        return lax.psum_scatter(parts, axes, scatter_dimension=0, tiled=False).astype(f32)

    gain_first = small_full[:, 0].astype(f32)
    gain_second = small_full[:, 1].astype(f32)
    heads = small_full[:, 2 : 4 + experts]

    residual = tokens.astype(f32)
    normed_one, scale_one = normalize(residual)
    attn_in = (normed_one * gain_first).astype(bf16)
    qkv_rows = matmul(attn_in, qkv_full).astype(bf16)
    attended, lse, *gathered = attend_forward(qkv_rows, width, gather_dense, 2, experts)
    if fast:
        fc_full, proj_full = gathered
    fc_full, proj_full = together(fc_full), together(proj_full)
    after_attn = residual + matmul(attended, out_full)
    normed_two, scale_two = normalize(after_attn)
    mixed_in = (normed_two * gain_second).astype(bf16)
    logits = matmul(mixed_in, small_full)
    router_probs = jax.nn.softmax(logits[:, 2 : 2 + experts], axis=-1)
    coef_tok = jax.nn.softmax(logits[:, 2 + experts : 4 + experts], axis=-1)

    route_tok = routes[:, 0]
    capacity = -(-(tok_rows * 10) // (8 * experts))
    chosen = (route_tok[:, None] == jnp.arange(experts, dtype=jnp.int32)[None, :]).astype(f32)
    earlier = (
        lax.broadcasted_iota(jnp.int32, (tok_rows, tok_rows), 0)
        > lax.broadcasted_iota(jnp.int32, (tok_rows, tok_rows), 1)
    ).astype(bf16)
    position = jnp.sum(chosen * matmul(earlier, chosen.astype(bf16)), axis=1).astype(jnp.int32)
    turn = lax.rem(route_tok - lax.axis_index("expert") + experts, experts)
    target = turn * capacity + position
    dispatch = (
        lax.broadcasted_iota(jnp.int32, (experts * capacity, tok_rows), 0) == target[None, :]
    ).astype(bf16)
    kept_tok = (1 - dropped).astype(f32)
    gate_prob = jnp.sum(router_probs * chosen, axis=1)
    gate_tok = gate_prob * kept_tok
    weight_tok = coef_tok[:, 1:] * gate_tok[:, None]
    grad_out = cotangent.astype(f32)
    grad_dense = (coef_tok[:, :1] * grad_out).astype(bf16)
    grad_expert = (weight_tok * grad_out).astype(bf16)

    def exchange(parts, sign):
        moved = [parts[0]]
        for j in range(1, experts):
            shift = [(s, (s + sign * j) % experts) for s in range(experts)]
            moved.append(lax.ppermute(parts[j], "expert", shift))
        return jnp.concatenate(moved, axis=0)

    leaving = matmul(dispatch, jnp.concatenate([mixed_in, grad_expert], axis=1)).astype(bf16)
    arrived = exchange(leaving.reshape(experts, capacity, 2 * width), 1)

    dense_out, grad_mixed, d_fc, d_proj, *gathered = mlp(
        mixed_in, grad_dense, fc_full, proj_full, f32, "dense_mlp", gather_experts, 3, experts, devices if fast else None
    )
    scatter_dense = None
    if fast:
        win_full, wout_full = gathered
        by_chip = lambda a: a.reshape(4, 2, 2, experts // 2, 4, width // 4, 128)
        scatter_dense = Scatter([by_chip(d_fc), by_chip(d_proj)], "rows", experts)
    returned, grad_rows, d_win, d_wout, *scattered = mlp(
        arrived[:, :width], arrived[:, width:], win_full, wout_full, bf16, "expert_mlp", scatter_dense, 4, experts
    )
    leaving = jnp.concatenate([returned, grad_rows], axis=1)
    came_back = exchange(leaving.reshape(experts, capacity, 2 * width), -1)
    if fast:
        by_column = scattered[0].reshape(2, width, 128)
        grad_fc = by_column[0].reshape(ff // 128, share, 128).transpose(1, 0, 2).reshape(share, ff)
        grad_proj = by_column[1].T
        cut_rows = lambda a: a.reshape(4, 2, 8, 2, width // 16, a.shape[2])
        scatter_win = Scatter([cut_rows(d_win)], "plane", experts)
        scatter_wout = Scatter([cut_rows(d_wout)], "plane", experts)
        (grad_win,) = move("scatter_win", scatter_win, 5, experts)
        grad_win = grad_win.reshape(width, -1)
    else:
        grad_fc = scatter_xla(d_fc.reshape(devices, share, ff), AXES)
        by_unit = d_proj.reshape(width, devices, ff // devices).transpose(1, 0, 2)
        grad_proj = scatter_xla(by_unit, AXES).T
        grad_win = scatter_xla(d_win, "node")
        grad_wout = scatter_xla(d_wout, "node")
        scatter_wout = None
    came_back = product_tn(dispatch, came_back)
    expert_tok, grad_back = came_back[:, :width], came_back[:, width:]

    mixed = after_attn + coef_tok[:, :1] * dense_out + weight_tok * expert_tok
    shared = jnp.sum(grad_out * expert_tok, axis=1)
    grad_coef = jnp.stack([jnp.sum(grad_out * dense_out, axis=1), shared * gate_tok], axis=1)
    grad_coef_logit = coef_tok * (grad_coef - jnp.sum(coef_tok * grad_coef, axis=1, keepdims=True))
    grad_gate = shared * coef_tok[:, 1] * kept_tok
    grad_route_logit = (grad_gate * gate_prob)[:, None] * (chosen - router_probs)
    grad_logits = jnp.concatenate([grad_route_logit, grad_coef_logit], axis=1)
    grad_mixed = grad_mixed + grad_back
    grad_mixed = grad_mixed + jnp.dot(grad_logits, heads.astype(f32).T, precision=highest)
    grad_heads = jnp.dot(mixed_in.astype(f32).T, grad_logits, precision=highest)
    grad_gain_two = jnp.sum(grad_mixed * normed_two, axis=0)
    grad_after = grad_out + norm_back(grad_mixed * gain_second, normed_two, scale_two)
    grad_attn = grad_after.astype(bf16)
    d_out = product_tn(attended, grad_attn).astype(bf16)
    grad_attended = outer_nt(grad_attn, out_full).astype(bf16)
    grad_qkv, *scattered = attend_backward(qkv_rows, lse, grad_attended, width, scatter_wout, 6, experts)
    if fast:
        grad_wout = scattered[0].reshape(width, -1)
    d_qkv = [product_tn(attn_in, grad_qkv[i]).astype(bf16) for i in range(3)]
    grad_attn_in = sum(outer_nt(grad_qkv[i], qkv_full[:, i * width : (i + 1) * width]) for i in range(3))
    grad_gain_one = jnp.sum(grad_attn_in * normed_one, axis=0)
    tokens_grad = grad_after + norm_back(grad_attn_in * gain_first, normed_one, scale_one)
    d_small = jnp.concatenate([grad_gain_one[:, None], grad_gain_two[:, None], grad_heads], axis=1)
    d_small = jnp.pad(d_small, ((0, 0), (0, 128 - d_small.shape[1]))).astype(bf16)
    if fast:
        last = [d_out] + d_qkv + [jnp.pad(d_small, ((0, 0), (0, BLOCK - 128)))]
        last = [a.reshape(4, 2, 2, experts // 2, share, a.shape[1]) for a in last]
        (summed,) = move("scatter_last", Scatter(last, "columns", experts), 7, experts)
        per = width // BLOCK
        grad_wo = jnp.concatenate([summed[i] for i in range(per)], axis=1)
        grad_wqkv = jnp.concatenate([summed[i] for i in range(per, 4 * per)], axis=1)
        grad_small = summed[4 * per]
    else:
        grad_small = scatter_xla(d_small.reshape(devices, share, 128), AXES)
        grad_wqkv = scatter_xla(jnp.concatenate(d_qkv, axis=1).reshape(devices, share, 3 * width), AXES)
        grad_wo = scatter_xla(d_out.reshape(devices, share, width), AXES)
    return (
        mixed.astype(bf16),
        tokens_grad,
        grad_small[:, 0],
        grad_wqkv,
        grad_wo,
        grad_small[:, 1],
        grad_fc,
        grad_proj,
        grad_small[:, 2 : 2 + experts],
        grad_small[:, 2 + experts : 4 + experts],
        grad_win[None],
        grad_wout.T[None],
    )


def solution(mesh):
    rows = P(AXES, None)
    in_specs = (
        rows,
        P(AXES),
        rows,
        rows,
        P(AXES),
        rows,
        rows,
        rows,
        rows,
        P("expert", None, "node"),
        P("expert", "node", None),
        rows,
        P(AXES),
        rows,
    )
    out_specs = (
        rows,
        rows,
        P(AXES),
        rows,
        rows,
        P(AXES),
        rows,
        rows,
        rows,
        rows,
        P("expert", None, "node"),
        P("expert", "node", None),
    )
    fast = mesh.shape["node"] == 8 and mesh.shape["expert"] % 2 == 0
    return jax.shard_map(
        functools.partial(shards, fast), mesh=mesh, in_specs=in_specs, out_specs=out_specs, check_vma=False
    )
```

time: 881 us -> 575 us (0.65)
  waiting for transfers between devices: 235 us -> 0.02 us
  Pallas kernels: 369 us -> 472 us
  local copies, waits for them, and re-layouts: 86.9 us -> 21 us
  other arithmetic: 83.7 us -> 21.7 us
  starting transfers between devices: 56.8 us -> 10 us
    ppermute x50 -> x0, waiting for transfers between devices: 203 us -> none  [the longest x35 156 us: hop(): return lax.ppermute(values, 'node', neighbour(axis))]
    pallas_call x6 -> x7, Pallas kernels: 369 us -> 472 us  [call(): pl.pallas_call(kernel, grid=(total,), out_shape=list(outs) + (moves.outs...]
    ppermute x50 -> x0, starting transfers between devices: 46.3 us -> none  [the longest x35 28.4 us: hop(): return lax.ppermute(values, 'node', neighbour(axis))]
    ppermute x6, waiting for transfers between devices: 32 us -> 0.02 us  [exchange(): moved.append(lax.ppermute(parts[j], 'expert', shift))]
    convert_element_type x14 -> x0, other arithmetic: 28.6 us -> none  [the longest x7 24.7 us: scatter_plane(): chip = add(take(k), hop(take(1 - k), CORE)).astype(bf16)]
    unnamed x85 -> x66, local copies, waits for them, and re-layouts: 29.7 us -> 7.88 us
    another operation x35 -> x0, other arithmetic: 19.8 us -> none  [the longest x21 13.1 us: scatter_plane(): jnp.stack([add(own[0], from_x[1], last_y), add(own[1], last_x, from_y[1])])]
    dynamic_slice x5 -> x0, local copies, waits for them, and re-layouts: 19.8 us -> none  [the longest x2 19.6 us: scatter_plane(): take = lambda i: lax.dynamic_index_in_dim(by_core, i, 1, keepdims=False)]
  transfers between devices with their start and end apart: 56 -> 6, of which waited for: 26 -> 0; matrix products, arithmetic and copies ran while one was open for 20% -> 0% of each run, Pallas kernels for 35% -> 23%
where the time goes in v2:
time: 575 us; the launch traced here: 567 us
  Pallas kernels  472 us (82%)
  matrix products  40 us (7%)
  other arithmetic  21.7 us (4%)
  local copies, waits for them, and re-layouts  21 us (4%)
  starting transfers between devices  10 us (2%)
    pallas_call x7, Pallas kernels, call(): pl.pallas_call(kernel, grid=(total,), out_shape=list(outs) + (moves.outs...  472 us
    dot_general x14, matrix products, contract(): lax.dot_general(left_op, right_op, (((left_dim,), (right_dim,)), ((), ())...  37.1 us
  transfers between devices with their start and end apart: 6, of which 0 were waited for; matrix products, arithmetic and copies ran while one was open for 0% of the time, Pallas kernels for 23%

profile of v2, /device:TPU:0, one launch (start us, length us, event | category | flops | bytes accessed | tf_op | source)
XLA Modules:
  0.0 566.7 jit_solution(13842082152431871530)
XLA Ops:
  4.7 52.0 %gather_first.1 = (bf16[32,32,128]{2,1,0:T(8,128)(2,1)}, bf16[32,32,3072]{2,1,0:T(8,128)(2,1)}, bf16[32,32,1024]{2,1,0:T(8,128)(2,1)}) custom-call(bf16[32,128]{1,0:T(8,128)(2,1)} %pad.13.refs_0_, bf16[32,3072]{1,0:T(8,128)(2,1)} %refs_1_.1, bf16[32,1024]{1,0:T(8,128)(2,1)} %refs_2_.1), custom_call_target="tpu_custom_call" | custom-call | bytes 33554432 | tf_op jit(solution)/shard_map/gather_first/pallas_call | solution.py:394
  58.2 7.8 %convolution_convert_fusion.refs_0_.refs_1_.refs_2_ = bf16[512,3072]{1,0:T(8,128)(2,1)} fusion(bf16[1024,3072]{1,0:T(8,128)(2,1)} %bitcast.128, bf16[512,1024]{1,0:T(8,128)(2,1)S(1)} %copy-done.3, f32[1024]{0:T(1024)S(1)} %bitcast.117, f32[512]{0:T(512)S(1)} %add_rsqrt_fusion.1, f32[512]{0:T(512)S(1)} %broadcast_multiply_fusion.5), kind=kOutput, calls=%fused_computation | convolution fusion | flops 3225419776 | bytes 10493952 | tf_op jit(solution)/shard_map/dot_general | solution.py:38
  66.1 87.1 %attend_forward.1 = (bf16[512,1024]{1,0:T(8,128)(2,1)}, f32[8,2,512]{2,1,0:T(2,128)}, bf16[32,32,4096]{2,1,0:T(8,128)(2,1)}, bf16[32,128,1024]{2,1,0:T(8,128)(2,1)}) custom-call(bf16[512,3072]{1,0:T(8,128)(2,1)} %convolution_convert_fusion.refs_0_.refs_1_.refs_2_, bf16[512,3072]{1,0:T(8,128)(2,1)} %convolution_convert_fusion.refs_0_.refs_1_.refs_2_, ...), custom_call_target="tpu_custom_call" | custom-call | flops 1073741824 | bytes 33554432 | tf_op jit(solution)/shard_map/attend_forward/pallas_call | solution.py:394
  153.2 3.3 fusion.80
  162.3 2.6 fusion.22
  167.8 4.1 collective-permute-start.2
  173.1 89.9 %dense_mlp.1 = (f32[512,1024]{1,0:T(8,128)}, f32[512,1024]{1,0:T(8,128)}, bf16[32,1024,128]{2,1,0:T(8,128)(2,1)}, bf16[32,1024,128]{2,1,0:T(8,128)(2,1)}, bf16[8...) custom-call(bf16[512,1024]{1,0:T(8,128)(2,1)} %copy-done, bf16[512,1024]{1,0:T(8,128)(2,1)} %get-tuple-element.114.refs_1_, ...), custom_call_target="tpu_custom_call" | custom-call | flops 25769803776 | bytes 33554432 | tf_op jit(solution)/shard_map/dense_mlp/pallas_call | solution.py:394
  264.7 1.7 fusion.76
  266.4 94.3 %expert_mlp.1 = (bf16[640,1024]{1,0:T(8,128)(2,1)}, bf16[640,1024]{1,0:T(8,128)(2,1)}, bf16[8,1024,512]{2,1,0:T(8,128)(2,1)}, bf16[8,1024,512]{2,1,0:T(8,128)(2,1)}, f32[8,256,128]{2,1,0:T(8,128)}) custom-call(bf16[640,1024]{1,0:T(8,128)(2,1)} %get-tuple-element.106.refs_0_, bf16[640,1024]{1,0:T(8,128)(2,1)} %get-tuple-element.105.refs_1_, ...), custom_call_target="tpu_custom_call" | custom-call | flops 32212254720 | bytes 33554432 | tf_op jit(solution)/shard_map/expert_mlp/pallas_call | solution.py:394
  365.4 2.5 collective-permute-start.4
  370.8 43.0 %scatter_win.1 = f32[8,2,64,512]{3,2,1,0:T(8,128)} custom-call(bf16[4,2,8,2,64,512]{5,4,3,2,1,0:T(8,128)(2,1)} %bitcast.84), custom_call_target="tpu_custom_call" | custom-call | bytes 33554432 | tf_op jit(solution)/shard_map/scatter_win/pallas_call | solution.py:394
  413.9 3.5 fusion
  417.5 2.0 fusion.24
  421.5 2.3 multiply_reduce_fusion
  425.4 2.3 convolution_convert_fusion.6.refs_3_
  427.7 2.6 convolution_convert_fusion.5
  430.3 44.4 %attend_backward.1 = (bf16[3,512,1024]{2,1,0:T(8,128)(2,1)}, f32[8,2,64,512]{3,2,1,0:T(8,128)}) custom-call(bf16[512,3072]{1,0:T(8,128)(2,1)} %convolution_convert_fusion.refs_0_.refs_1_.refs_2_, bf16[512,3072]{1,0:T(8,128)(2,1)} %convolution_convert_fusion.refs_0_.refs_1_.refs_2_, bf16[512,3072]{1,0:T(8,128)(2,1)} %convolution_convert_fusion.refs_0_.refs_1_.refs_2_, ...), custom_call_target="tpu_custom_call" | custom-call | flops 2684354560 | bytes 33554432 | tf_op jit(solution)/shard_map/attend_backward/pallas_call | solution.py:394
  474.8 4.2 convolution_convert_fusion.4
  478.9 2.8 convolution_convert_fusion.3
  481.7 2.8 convolution_convert_fusion.2
  487.1 3.1 fusion.19
  491.4 61.4 %scatter_last.1 = f32[9,32,512]{2,1,0:T(8,128)} custom-call(bf16[4,2,2,2,32,1024]{5,4,3,2,1,0:T(8,128)(2,1)} %bitcast.91, bf16[4,2,2,2,32,1024]{5,4,3,2,1,0:T(8,128)(2,1)} %bitcast.92, bf16[4,2,2,2,32,1024]{5,4,3,2,1,0:T(8,128)(2,1)} %bitcast.93, bf16[4,2,2,2,32,1024]{5,4,3,2,1,0:T(8,128)(2,1)} %bitcast.94, bf16[4,2,2,2,32,512]{5,4,3,2,1,0:T(8,128)(2,1)} %bitcast.87), custom_call_target="tpu_custom_call" | custom-call | bytes 33554432 | tf_op jit(solution)/shard_map/scatter_last/pallas_call | solution.py:394
  555.5 2.9 copy.54
  560.6 4.4 fusion.18
  (129 shorter events, 37.9 us)
Async XLA Ops:
  0.6 3.3 copy-start.19
  0.7 3.3 copy-start.18
  0.7 3.3 copy-start.20
  2.1 56.1 %copy-start.3 = (bf16[512,1024]{1,0:T(8,128)(2,1)S(1)}, bf16[512,1024]{1,0:T(8,128)(2,1)}, u32[]{:S(2)}) copy-start(bf16[512,1024]{1,0:T(8,128)(2,1)} %param.14) | copy-start | bytes 3145732
  156.9 5.4 copy-start.17
  157.8 7.1 %copy-start = (bf16[512,1024]{1,0:T(8,128)(2,1)}, bf16[512,1024]{1,0:T(8,128)(2,1)S(1)}, u32[]{:S(2)}) copy-start(bf16[512,1024]{1,0:T(8,128)(2,1)S(1)} %multiply_convert_fusion.refs_0_) | copy-start | bytes 3145732
  167.8 95.2 %collective-permute-start.2 = (bf16[160,2048]{1,0:T(8,128)(2,1)}, bf16[160,2048]{1,0:T(8,128)(2,1)}, u32[]{:S(2)}, u32[]{:S(2)}) collective-permute-start(bf16[160,2048]{1,0:T(8,128)(2,1)} %get-tuple-element.108), channel_id=1, source_target_pairs={{0,3},{1,0},{2,1},{3,2},{4,7},{5,4},{6,5},{7,6},{8,11},{9,8},{10,9... | collective-permute-start | bytes 1966088 | tf_op jit(solution)/shard_map/ppermute | solution.py:706
  171.8 91.2 %collective-permute-start.1 = (bf16[160,2048]{1,0:T(8,128)(2,1)}, bf16[160,2048]{1,0:T(8,128)(2,1)}, u32[]{:S(2)}, u32[]{:S(2)}) collective-permute-start(bf16[160,2048]{1,0:T(8,128)(2,1)} %get-tuple-element.109), channel_id=1, source_target_pairs={{0,2},{1,3},{2,0},{3,1},{4,6},{5,7},{6,4},{7,5},{8,10},{9,11},{10,... | collective-permute-start | bytes 1966088 | tf_op jit(solution)/shard_map/ppermute | solution.py:706
  172.9 90.1 %collective-permute-start = (bf16[160,2048]{1,0:T(8,128)(2,1)}, bf16[160,2048]{1,0:T(8,128)(2,1)}, u32[]{:S(2)}, u32[]{:S(2)}) collective-permute-start(bf16[160,2048]{1,0:T(8,128)(2,1)} %get-tuple-element.110), channel_id=1, source_target_pairs={{0,1},{1,2},{2,3},{3,0},{4,5},{5,6},{6,7},{7,4},{8,9},{9,10},{10,1... | collective-permute-start | bytes 1966088 | tf_op jit(solution)/shard_map/ppermute | solution.py:706
  362.6 6.3 %copy-start.12 = (f32[8,256,128]{2,1,0:T(8,128)S(1)}, f32[8,256,128]{2,1,0:T(8,128)}, u32[]{:S(2)}) copy-start(f32[8,256,128]{2,1,0:T(8,128)} %get-tuple-element.49) | copy-start | bytes 3145732
  364.1 49.7 %collective-permute-start.5 = (bf16[160,2048]{1,0:T(8,128)(2,1)}, bf16[160,2048]{1,0:T(8,128)(2,1)}, u32[]{:S(2)}, u32[]{:S(2)}) collective-permute-start(bf16[160,2048]{1,0:T(8,128)(2,1)} %get-tuple-element.102), channel_id=1, source_target_pairs={{0,1},{1,2},{2,3},{3,0},{4,5},{5,6},{6,7},{7,4},{8,9},{9,10},{10,1... | collective-permute-start | bytes 1966088 | tf_op jit(solution)/shard_map/ppermute | solution.py:706
  365.4 48.4 %collective-permute-start.4 = (bf16[160,2048]{1,0:T(8,128)(2,1)}, bf16[160,2048]{1,0:T(8,128)(2,1)}, u32[]{:S(2)}, u32[]{:S(2)}) collective-permute-start(bf16[160,2048]{1,0:T(8,128)(2,1)} %get-tuple-element.103), channel_id=1, source_target_pairs={{0,2},{1,3},{2,0},{3,1},{4,6},{5,7},{6,4},{7,5},{8,10},{9,11},{10,... | collective-permute-start | bytes 1966088 | tf_op jit(solution)/shard_map/ppermute | solution.py:706
  367.9 45.9 %collective-permute-start.3 = (bf16[160,2048]{1,0:T(8,128)(2,1)}, bf16[160,2048]{1,0:T(8,128)(2,1)}, u32[]{:S(2)}, u32[]{:S(2)}) collective-permute-start(bf16[160,2048]{1,0:T(8,128)(2,1)} %get-tuple-element.104), channel_id=1, source_target_pairs={{0,3},{1,0},{2,1},{3,2},{4,7},{5,4},{6,5},{7,6},{8,11},{9,8},{10,9... | collective-permute-start | bytes 1966088 | tf_op jit(solution)/shard_map/ppermute | solution.py:706
  370.8 43.1 %copy-start.13 = (bf16[160,2048]{1,0:T(8,128)(2,1)S(1)}, bf16[160,2048]{1,0:T(8,128)(2,1)}, u32[]{:S(2)}) copy-start(bf16[160,2048]{1,0:T(8,128)(2,1)} %get-tuple-element.101) | copy-start | bytes 1966084
  413.9 3.6 copy-start.2
  413.9 3.6 copy-start.9
  417.4 3.5 copy-start.1
  417.5 4.0 copy-start.10
  430.3 44.4 %copy-start.4 = (bf16[512,1024]{1,0:T(8,128)(2,1)S(1)}, bf16[512,1024]{1,0:T(8,128)(2,1)}, u32[]{:S(2)}) copy-start(bf16[512,1024]{1,0:T(8,128)(2,1)} %param.14) | copy-start | bytes 3145732
  474.8 4.2 copy-start.22
  478.9 5.5 slice-start
  555.5 4.2 copy-start.8
  559.8 5.1 copy-start.16
  560.6 4.4 copy-start.5
  (9 other events, 17.7 us)

commit v3 on v2

--- a/solution.py
+++ b/solution.py
@@ -90,13 +90,13 @@
         ]
         hbm = pl.BlockSpec(memory_space=pltpu.HBM)
         self.in_specs, self.out_specs = [hbm] * len(args), [hbm] * len(args)
-        m = len(items)
+        m = sum(len(item) for item in items)
         self.scratch = [
             pltpu.SemaphoreType.DMA((m, experts + 7)),
             pltpu.SemaphoreType.DMA((m, experts + 7)),
             pltpu.SemaphoreType.DMA((m,)),
         ]
-        self.turns = m + self.late
+        self.turns = len(items) + self.late
         self.along_z = any(dense)
 
     def bind(self, ins, outs, scratch, place):
@@ -114,41 +114,43 @@
                 device_id_type=MESH,
             )
 
-        self.bound = []
-        for i, (arg, start, size) in enumerate(self.items):
+        self.full = outs
+        self.bound = [[] for _ in self.items]
+        pieces = [(turn, piece) for turn, item in enumerate(self.items) for piece in item]
+        for i, (turn, (arg, row, rows, col, columns)) in enumerate(pieces):
             dense = self.dense[arg]
-            cols = pl.ds(start, size)
             shard, whole = ins[arg], outs[arg]
-            rows = shard.shape[0]
             per = experts if dense else 1
             own = p.n * per + (e if dense else 0)
 
-            def bundle(m, whole=whole, per=per, cols=cols):
-                return whole.at[pl.ds(m * per, per), :, cols]
-
-            def half(m, h, whole=whole, per=per, cols=cols, dense=dense, rows=rows):
+            def view(ref, lead, start=0, size=None, whole_rows=rows, row=row, col=col, columns=columns):
+                return ref.at[lead, pl.ds(row + start, size or whole_rows), pl.ds(col, columns)]
+
+            def bundle(m, view=view, whole=whole, per=per):
+                return view(whole, pl.ds(m * per, per))
+
+            def half(m, h, view=view, whole=whole, per=per, dense=dense, rows=rows):
                 if dense:
-                    return whole.at[pl.ds(m * per + h * (per // 2), per // 2), :, cols]
-                return whole.at[m, pl.ds(h * (rows // 2), rows // 2), cols]
-
-            mine = shard.at[:, cols]
-            local = pltpu.make_async_copy(mine, whole.at[own, :, cols], loc.at[i])
+                    return view(whole, pl.ds(m * per + h * (per // 2), per // 2))
+                return view(whole, m, h * (rows // 2), rows // 2)
+
+            mine = shard.at[pl.ds(row, rows), pl.ds(col, columns)]
+            land = view(whole, own)
+            local = pltpu.make_async_copy(mine, land, loc.at[i])
             z = []
             if dense:
-                z = [remote(mine, whole.at[own, :, cols], i, j - 1, p.z(j)) for j in range(1, experts)]
-                first, land = bundle(p.n), bundle(p.n)
-            else:
-                first, land = mine, whole.at[p.n, :, cols]
+                z = [remote(mine, land, i, j - 1, p.z(j)) for j in range(1, experts)]
+            first, last = (bundle(p.n), bundle(p.n)) if dense else (mine, land)
             b = experts - 1
-            xy = [remote(first, land, i, b, (p.nx, e)), remote(first, land, i, b + 1, (p.ny, e))]
+            xy = [remote(first, last, i, b, (p.nx, e)), remote(first, last, i, b + 1, (p.ny, e))]
             diag = [
                 remote(half(p.nx, 0), half(p.nx, 0), i, b + 2, (p.ny, e)),
                 remote(half(p.ny, 1), half(p.ny, 1), i, b + 3, (p.nx, e)),
             ]
-            core = [remote(first, land, i, b + 4, (p.nc, e))] + [
+            core = [remote(first, last, i, b + 4, (p.nc, e))] + [
                 remote(bundle(m), bundle(m), i, b + 5 + j, (p.nc, e)) for j, m in enumerate((p.nx, p.ny, p.nd))
             ]
-            self.bound.append((local, z, xy, diag, core))
+            self.bound[turn].append((local, z, xy, diag, core))
 
     def turn(self, now):
         steps = (self.along, self.across, self.corner, self.over, self.end)
@@ -158,7 +160,8 @@
             def _(t=t):
                 for late, step in enumerate(steps):
                     if 0 <= t - late < len(self.items):
-                        step(*self.bound[t - late])
+                        for piece in self.bound[t - late]:
+                            step(*piece)
 
     def along(self, local, z, xy, diag, core):
         local.start()
@@ -418,15 +421,14 @@
     return jnp.where(keys <= queries, scores_t, -jnp.inf)
 
 
-def attend_forward_kernel(q_ref, k_ref, v_ref, o_ref, lse_ref):
-    q = q_ref[...] * (1.0 / math.sqrt(HD))
-    k = k_ref[...]
-    vt = v_ref[...].T
+def attend_pair(q, k, v):
+    q = q * (1.0 / math.sqrt(HD))
+    vt = v.T
     length = q.shape[0]
-    outs = []
+    outs, tops = [], []
     for h, mask in enumerate(masks()):
         kh = k * mask
-        row = []
+        row, logs = [], []
         for start in range(0, length, QB):
             end = start + QB
             scores = causal(outer_nt(kh[:end], q[start:end]), start)
@@ -435,33 +437,126 @@
             total = jnp.sum(expd, axis=0, keepdims=True)
             probs = (expd / total).astype(bf16)
             row.append(matmul(vt[h * HD : (h + 1) * HD, :end], probs))
-            lse_ref[0, h : h + 1, start:end] = top + jnp.log(total)
+            logs.append(top + jnp.log(total))
         outs.append(jnp.concatenate(row, axis=1))
-    o_ref[...] = jnp.concatenate(outs, axis=0).T.astype(bf16)
-
-
-def attend_forward(qkv, width, moves, collective_id, experts):
-    length = qkv.shape[0]
-    pairs = width // PAIR
-    part = lambda p: pl.BlockSpec((SEQ, PAIR), lambda j: (j // pairs, p * pairs + lax.rem(j, pairs)))
-    steps = length // SEQ * pairs
-    return call(
-        "attend_forward",
-        steps,
-        lambda now, steps, *refs: attend_forward_kernel(*refs),
-        [qkv] * 3,
-        [part(0), part(1), part(2)],
-        [
-            jax.ShapeDtypeStruct((length, width), bf16),
-            jax.ShapeDtypeStruct((steps, 2, SEQ), f32),
-        ],
-        [part(0), pl.BlockSpec((1, 2, SEQ), lambda j: (j, 0, 0))],
-        [],
-        moves,
-        collective_id,
-        experts,
-        4 * length * SEQ * width,
-    )
+        tops.append(jnp.concatenate(logs, axis=1))
+    return jnp.concatenate(outs, axis=0).T.astype(bf16), jnp.concatenate(tops, axis=0)
+
+
+class Front:
+    def __init__(self, length, width, experts, devices, capacity, moves):
+        self.length, self.width, self.experts, self.capacity, self.moves = length, width, experts, capacity, moves
+        pairs = width // PAIR
+        share = width // devices
+        self.at_norm, self.at_qkv = 4, 6
+        self.at_heads = self.at_qkv + 1
+        self.per_turn = 2
+        self.at_out = self.at_heads + length // SEQ * pairs // self.per_turn
+        self.steps = max(self.at_out + 1, moves.turns if moves else 0)
+        slots = experts * capacity
+        rows = lambda c, t: jax.ShapeDtypeStruct((length, c), t)
+        self.outs = [
+            rows(3 * width, bf16),
+            jax.ShapeDtypeStruct((length // SEQ * pairs, 2, SEQ), f32),
+            rows(width, bf16),
+            rows(width, f32),
+            rows(width, bf16),
+            rows(width, bf16),
+            jax.ShapeDtypeStruct((slots, 2 * width), bf16),
+            rows(slots, bf16),
+            rows(128, f32),
+        ]
+        self.scratch = [
+            pltpu.VMEM((devices, share, 128), bf16),
+            pltpu.VMEM((devices, share, 3 * width), bf16),
+            pltpu.VMEM((devices, share, width), bf16),
+            pltpu.VMEM((8, width), f32),
+            pltpu.VMEM((length, width), bf16),
+            pltpu.SemaphoreType.DMA((3,)),
+        ]
+
+    def __call__(self, now, steps, tok, cot, route, drop, *refs):
+        full = self.moves.full[:3] if self.moves else refs[:3]
+        refs = refs if self.moves else refs[3:]
+        qkv, lse, att, after, mixed, gd, leave, disp, info, ws, wq, wo, gains, attn_in, sems = refs
+        width, length = self.width, self.length
+        loads = [pltpu.make_async_copy(a, b, sems.at[i]) for i, (a, b) in enumerate(zip(full, (ws, wq, wo)))]
+
+        @when(now == self.at_norm)
+        def _():
+            loads[0].start()
+            loads[0].wait()
+            gains[...] = ws[...].reshape(width, 128).astype(f32).T[:8]
+            normed, _ = normalize(tok[...].astype(f32))
+            attn_in[...] = (normed * gains[0:1]).astype(bf16)
+
+        @when(now == self.at_qkv)
+        def _():
+            loads[1].start()
+            loads[1].wait()
+
+            def columns(c, _):
+                cols = pl.ds(pl.multiple_of(c * BLOCK, BLOCK), BLOCK)
+                weights = wq[:, :, cols].reshape(width, BLOCK)
+                qkv[:, cols] = matmul(attn_in[...], weights).astype(bf16)
+                return 0
+
+            lax.fori_loop(0, 3 * width // BLOCK, columns, 0)
+
+        @when(jnp.logical_and(now >= self.at_heads, now < self.at_out))
+        def _():
+            pairs = width // PAIR
+
+            def pair(i, _):
+                at = (now - self.at_heads) * self.per_turn + i
+                seq, at_pair = at // pairs, lax.rem(at, pairs)
+                rows = pl.ds(pl.multiple_of(seq * SEQ, SEQ), SEQ)
+                cols = lambda part: pl.ds(pl.multiple_of(part * width + at_pair * PAIR, PAIR), PAIR)
+                out, tops = attend_pair(qkv[rows, cols(0)], qkv[rows, cols(1)], qkv[rows, cols(2)])
+                att[rows, cols(0)] = out
+                lse[at] = tops
+                return 0
+
+            lax.fori_loop(0, self.per_turn, pair, 0)
+
+        @when(now == self.at_out)
+        def _():
+            loads[2].start()
+            loads[2].wait()
+            self.route(tok, cot, route, drop, att, wo, ws, gains, after, mixed, gd, leave, disp, info)
+
+    def route(self, tok, cot, route, drop, att, wo, ws, gains, after, mixed, gd, leave, disp, info):
+        width, length, experts = self.width, self.length, self.experts
+        after[...] = tok[...].astype(f32) + matmul(att[...], wo[...].reshape(width, width))
+        normed, _ = normalize(after[...])
+        mixed[...] = (normed * gains[1:2]).astype(bf16)
+        logits = matmul(mixed[...], ws[...].reshape(width, 128))
+        lane = lax.broadcasted_iota(jnp.int32, (length, 128), 1)
+
+        def softmax(first, last):
+            inside = jnp.logical_and(lane >= first, lane < last)
+            top = jnp.max(jnp.where(inside, logits, -jnp.inf), axis=1, keepdims=True)
+            expd = jnp.where(inside, jnp.exp(jnp.where(inside, logits, top) - top), 0.0)
+            return expd / jnp.sum(expd, axis=1, keepdims=True)
+
+        probs, coef = softmax(2, 2 + experts), softmax(2 + experts, 4 + experts)
+        info[...] = probs + coef
+        chosen = jnp.where(lane - 2 == route[...], 1.0, 0.0)
+        over_lanes = lambda a: jnp.sum(a, axis=1, keepdims=True)
+        gate = over_lanes(probs * chosen) * (1 - drop[...]).astype(f32)
+        coef_0 = over_lanes(jnp.where(lane == 2 + experts, coef, 0.0))
+        coef_1 = over_lanes(jnp.where(lane == 3 + experts, coef, 0.0))
+        grad = cot[...].astype(f32)
+        gd[...] = (coef_0 * grad).astype(bf16)
+        square = lambda d: lax.broadcasted_iota(jnp.int32, (length, length), d)
+        earlier = jnp.where(square(0) > square(1), 1.0, 0.0).astype(bf16)
+        position = over_lanes(chosen * matmul(earlier, chosen.astype(bf16))).astype(jnp.int32)
+        turn = route[...] - lax.axis_index("expert")
+        target = jnp.where(turn < 0, turn + experts, turn) * self.capacity + position
+        slot = lax.broadcasted_iota(jnp.int32, (length, experts * self.capacity), 1)
+        disp[...] = jnp.where(slot == target, 1.0, 0.0).astype(bf16)
+        leave[:, :width] = product_tn(disp[...], mixed[...]).astype(bf16)
+        leave[:, width:] = product_tn(disp[...], (coef_1 * gate * grad).astype(bf16)).astype(bf16)
 
 
 def attend_backward_kernel(q_ref, k_ref, v_ref, g_ref, lse_ref, d_ref):
@@ -634,27 +729,44 @@
     small = jnp.pad(small, ((0, 0), (0, 128 - small.shape[1])))
     win, wout = expert_in[0], expert_out[0]
     together = lambda a: a.reshape((devices * a.shape[1],) + a.shape[2:])
-    cut = lambda a, d, m: [(a, i * (d // m), d // m) for i in range(m)]
-    gather_dense = gather_experts = None
+    cut = lambda a, rows, columns, m, n: [
+        [(a, i * (rows // m), rows // m, j * (columns // n), columns // n)] for i in range(m) for j in range(n)
+    ]
+    moves = gather_experts = None
+    weights = (small, w_qkv, w_out, w_fc, w_proj)
+    capacity = -(-(tok_rows * 10) // (8 * experts))
     if fast:
-        first = Gather(
-            [small, w_qkv, w_out],
-            [True] * 3,
-            [(0, 0, 128)] + cut(1, 3 * width, 3) + [(2, 0, width)],
-            nodes,
-            experts,
+        items = cut(1, share, 3 * width, 1, 3) + cut(2, share, width, 1, 1)
+        items += cut(3, share, ff, 1, 4) + cut(4, ff // devices, width, 4, 1)
+        items[0] = cut(0, share, 128, 1, 1)[0] + items[0]
+        moves = Gather(list(weights), [True] * 5, items, nodes, experts)
+        gather_experts = Gather(
+            [win, wout], [False] * 2, cut(0, width, win.shape[1], 4, 1) + cut(1, wout.shape[0], width, 4, 1), nodes, experts
         )
-        small_full, qkv_full, out_full = move("gather_first", first, 1, experts)
-        gather_dense = Gather([w_fc, w_proj], [True] * 2, cut(0, ff, 4) + cut(1, width, 4), nodes, experts)
-        gather_experts = Gather(
-            [win, wout], [False] * 2, cut(0, win.shape[1], 4) + cut(1, width, 4), nodes, experts
-        )
+        full = []
     else:
-        small_full, qkv_full, out_full, fc_full, proj_full = (
-            lax.all_gather(a, AXES, axis=0, tiled=False) for a in (small, w_qkv, w_out, w_fc, w_proj)
-        )
+        full = [lax.all_gather(a, AXES, axis=0, tiled=False) for a in weights]
         win_full, wout_full = (lax.all_gather(a, "node", axis=0, tiled=False) for a in (win, wout))
-    small_full, qkv_full, out_full = (together(a) for a in (small_full, qkv_full, out_full))
+    front = Front(tok_rows, width, experts, devices, capacity, moves)
+    kept = full[:3]
+    whole, hbm = pl.BlockSpec(memory_space=pltpu.VMEM), pl.BlockSpec(memory_space=pltpu.HBM)
+    results = call(
+        "front",
+        front.steps,
+        front,
+        [tokens, cotangent, routes, dropped[:, None]] + kept,
+        [whole] * 4 + [hbm] * len(kept),
+        front.outs,
+        [whole] * len(front.outs),
+        front.scratch,
+        moves,
+        1,
+        experts,
+        12 * tok_rows * width * width,
+    )
+    qkv_rows, lse, attended, after_attn, mixed_in, grad_dense, leaving, dispatch, probs = results[:9]
+    full = results[9:] if fast else full
+    small_full, qkv_full, out_full, fc_full, proj_full = (together(a) for a in full)
 
     def scatter_xla(parts, axes):
         return lax.psum_scatter(parts, axes, scatter_dimension=0, tiled=False).astype(f32)
@@ -662,42 +774,17 @@
     gain_first = small_full[:, 0].astype(f32)
     gain_second = small_full[:, 1].astype(f32)
     heads = small_full[:, 2 : 4 + experts]
-
     residual = tokens.astype(f32)
     normed_one, scale_one = normalize(residual)
     attn_in = (normed_one * gain_first).astype(bf16)
-    qkv_rows = matmul(attn_in, qkv_full).astype(bf16)
-    attended, lse, *gathered = attend_forward(qkv_rows, width, gather_dense, 2, experts)
-    if fast:
-        fc_full, proj_full = gathered
-    fc_full, proj_full = together(fc_full), together(proj_full)
-    after_attn = residual + matmul(attended, out_full)
     normed_two, scale_two = normalize(after_attn)
-    mixed_in = (normed_two * gain_second).astype(bf16)
-    logits = matmul(mixed_in, small_full)
-    router_probs = jax.nn.softmax(logits[:, 2 : 2 + experts], axis=-1)
-    coef_tok = jax.nn.softmax(logits[:, 2 + experts : 4 + experts], axis=-1)
-
-    route_tok = routes[:, 0]
-    capacity = -(-(tok_rows * 10) // (8 * experts))
-    chosen = (route_tok[:, None] == jnp.arange(experts, dtype=jnp.int32)[None, :]).astype(f32)
-    earlier = (
-        lax.broadcasted_iota(jnp.int32, (tok_rows, tok_rows), 0)
-        > lax.broadcasted_iota(jnp.int32, (tok_rows, tok_rows), 1)
-    ).astype(bf16)
-    position = jnp.sum(chosen * matmul(earlier, chosen.astype(bf16)), axis=1).astype(jnp.int32)
-    turn = lax.rem(route_tok - lax.axis_index("expert") + experts, experts)
-    target = turn * capacity + position
-    dispatch = (
-        lax.broadcasted_iota(jnp.int32, (experts * capacity, tok_rows), 0) == target[None, :]
-    ).astype(bf16)
+    router_probs, coef_tok = probs[:, 2 : 2 + experts], probs[:, 2 + experts : 4 + experts]
+    chosen = (routes == jnp.arange(experts, dtype=jnp.int32)[None, :]).astype(f32)
     kept_tok = (1 - dropped).astype(f32)
     gate_prob = jnp.sum(router_probs * chosen, axis=1)
     gate_tok = gate_prob * kept_tok
     weight_tok = coef_tok[:, 1:] * gate_tok[:, None]
     grad_out = cotangent.astype(f32)
-    grad_dense = (coef_tok[:, :1] * grad_out).astype(bf16)
-    grad_expert = (weight_tok * grad_out).astype(bf16)
 
     def exchange(parts, sign):
         moved = [parts[0]]
@@ -706,7 +793,6 @@
             moved.append(lax.ppermute(parts[j], "expert", shift))
         return jnp.concatenate(moved, axis=0)
 
-    leaving = matmul(dispatch, jnp.concatenate([mixed_in, grad_expert], axis=1)).astype(bf16)
     arrived = exchange(leaving.reshape(experts, capacity, 2 * width), 1)
 
     dense_out, grad_mixed, d_fc, d_proj, *gathered = mlp(
@@ -738,7 +824,7 @@
         grad_win = scatter_xla(d_win, "node")
         grad_wout = scatter_xla(d_wout, "node")
         scatter_wout = None
-    came_back = product_tn(dispatch, came_back)
+    came_back = matmul(dispatch, came_back)
     expert_tok, grad_back = came_back[:, :width], came_back[:, width:]
 
     mixed = after_attn + coef_tok[:, :1] * dense_out + weight_tok * expert_tok

time: 575 us -> 572 us (level)
  local copies, waits for them, and re-layouts: 21 us -> 44.4 us
  Pallas kernels: 472 us -> 451 us
  other arithmetic: 21.7 us -> 15.8 us
    pallas_call x7 -> x6, Pallas kernels: 472 us -> 451 us  [call(): pl.pallas_call(kernel, grid=(total,), out_shape=list(outs) + (moves.outs...]
    unnamed x66 -> x51, local copies, waits for them, and re-layouts: 7.88 us -> 18 us
    dot_general x14 -> x9, matrix products: 37.1 us -> 29.1 us  [contract(): lax.dot_general(left_op, right_op, (((left_dim,), (right_dim,)), ((), ())...]
  transfers between devices with their start and end apart: 6 -> 6, of which waited for: 0 -> 1; matrix products, arithmetic and copies ran while one was open for 0% -> 2% of each run, Pallas kernels for 23% -> 23%
where the time goes in v3:
time: 572 us; the launch traced here: 564 us
  Pallas kernels  451 us (79%)
  local copies, waits for them, and re-layouts  44.4 us (8%)
  matrix products  35.4 us (6%)
  other arithmetic  15.8 us (3%)
  starting transfers between devices  9.83 us (2%)
  waiting for transfers between devices  5.72 us (1%)
    pallas_call x6, Pallas kernels, call(): pl.pallas_call(kernel, grid=(total,), out_shape=list(outs) + (moves.outs...  451 us
    dot_general x9, matrix products, contract(): lax.dot_general(left_op, right_op, (((left_dim,), (right_dim,)), ((), ())...  29.1 us
    unnamed x51, local copies, waits for them, and re-layouts  18 us
  transfers between devices with their start and end apart: 6, of which 1 were waited for; matrix products, arithmetic and copies ran while one was open for 2% of the time, Pallas kernels for 23%

profile of v3, /device:TPU:0, one launch (start us, length us, event | category | flops | bytes accessed | tf_op | source)
XLA Modules:
  0.0 564.0 jit_solution(562925231801016813)
XLA Ops:
  5.1 128.8 %front.1 = (bf16[512,3072]{1,0:T(8,128)(2,1)}, f32[8,2,512]{2,1,0:T(2,128)}, bf16[512,1024]{1,0:T(8,128)(2,1)}, f32[512,1024]{1,0:T(8,128)}, bf16[512,1024]{1,0:...) custom-call(bf16[512,1024]{1,0:T(8,128)(2,1)} %refs_0_.1, ...), custom_call_target="tpu_custom_call" | custom-call | flops 6442450944 | bytes 33554432 | tf_op jit(solution)/shard_map/front/pallas_call | solution.py:397
  134.0 3.4 fusion.59
  137.4 3.8 collective-permute-start
  145.9 89.8 %dense_mlp.1 = (f32[512,1024]{1,0:T(8,128)}, f32[512,1024]{1,0:T(8,128)}, bf16[32,1024,128]{2,1,0:T(8,128)(2,1)}, bf16[32,1024,128]{2,1,0:T(8,128)(2,1)}, bf16[8...) custom-call(bf16[512,1024]{1,0:T(8,128)(2,1)} %get-tuple-element.41.refs_0_, ...), custom_call_target="tpu_custom_call" | custom-call | flops 25769803776 | bytes 33554432 | tf_op jit(solution)/shard_map/dense_mlp/pallas_call | solution.py:397
  243.9 93.2 %expert_mlp.1 = (bf16[640,1024]{1,0:T(8,128)(2,1)}, bf16[640,1024]{1,0:T(8,128)(2,1)}, bf16[8,1024,512]{2,1,0:T(8,128)(2,1)}, bf16[8,1024,512]{2,1,0:T(8,128)(2,1)}, f32[8,256,128]{2,1,0:T(8,128)}) custom-call(bf16[640,1024]{1,0:T(8,128)(2,1)} %get-tuple-element.134.refs_0_, bf16[640,1024]{1,0:T(8,128)(2,1)} %get-tuple-element.133.refs_1_, ...), custom_call_target="tpu_custom_call" | custom-call | flops 32212254720 | bytes 33554432 | tf_op jit(solution)/shard_map/expert_mlp/pallas_call | solution.py:397
  340.5 2.8 collective-permute-start.3
  344.5 42.7 %scatter_win.1 = f32[8,2,64,512]{3,2,1,0:T(8,128)} custom-call(bf16[4,2,8,2,64,512]{5,4,3,2,1,0:T(8,128)(2,1)} %bitcast.78), custom_call_target="tpu_custom_call" | custom-call | bytes 33554432 | tf_op jit(solution)/shard_map/scatter_win/pallas_call | solution.py:397
  387.2 2.2 fusion.60
  393.4 5.7 %collective-permute-done.4 = bf16[160,2048]{1,0:T(8,128)(2,1)} collective-permute-done((bf16[160,2048]{1,0:T(8,128)(2,1)}, bf16[160,2048]{1,0:T(8,128)(2,1)}, u32[]{:S(2)}, u32[]{:S(2)}) %collective-permute-start.4) | collective-permute-done | bytes 655392 | tf_op jit(solution)/shard_map/ppermute | solution.py:793
  399.1 3.7 fusion
  412.5 4.6 multiply_reduce_fusion
  417.2 2.1 convert_add_fusion
  419.3 2.3 convolution_convert_fusion.4.refs_3_
  421.6 45.1 %attend_backward.1 = (bf16[3,512,1024]{2,1,0:T(8,128)(2,1)}, f32[8,2,64,512]{3,2,1,0:T(8,128)}) custom-call(bf16[512,3072]{1,0:T(8,128)(2,1)} %get-tuple-element.56.refs_0_.refs_1_.refs_2_, bf16[512,3072]{1,0:T(8,128)(2,1)} %get-tuple-element.56.refs_0_.refs_1_.refs_2_, bf16[512,3072]{1,0:T(8,128)(2,1)} %get-tuple-element.56.refs_0_.refs_1_.refs_2_, ...), custom_call_target="tpu_custom_call" | custom-call | flops 2684354560 | bytes 33554432 | tf_op jit(solution)/shard_map/attend_backward/pallas_call | solution.py:397
  466.7 3.3 fusion.25
  470.1 2.9 fusion.23
  473.0 2.8 convolution_convert_fusion
  475.8 2.7 convolution_convert_fusion.1
  478.5 2.8 convolution_convert_fusion.2
  481.3 4.8 fusion.19
  487.4 3.8 convolution_convert_fusion.3
  491.2 51.8 %scatter_last.1 = f32[9,32,512]{2,1,0:T(8,128)} custom-call(bf16[4,2,2,2,32,1024]{5,4,3,2,1,0:T(8,128)(2,1)} %bitcast.87, bf16[4,2,2,2,32,1024]{5,4,3,2,1,0:T(8,128)(2,1)} %bitcast.86, bf16[4,2,2,2,32,1024]{5,4,3,2,1,0:T(8,128)(2,1)} %bitcast.85, bf16[4,2,2,2,32,1024]{5,4,3,2,1,0:T(8,128)(2,1)} %bitcast.84, bf16[4,2,2,2,32,512]{5,4,3,2,1,0:T(8,128)(2,1)} %bitcast.81), custom_call_target="tpu_custom_call" | custom-call | bytes 33554432 | tf_op jit(solution)/shard_map/scatter_last/pallas_call | solution.py:397
  554.9 2.9 copy.86
  558.5 3.7 fusion.17
  (108 shorter events, 50.7 us)
Async XLA Ops:
  133.9 9.7 %copy-start.16 = (s32[512,1]{0,1:T(1,128)S(1)}, s32[512,1]{0,1:T(1,128)}, u32[]{:S(2)}) copy-start(s32[512,1]{0,1:T(1,128)} %param.25) | copy-start | bytes 6148
  134.0 9.9 %copy-start = (f32[512,1024]{1,0:T(8,128)S(1)}, f32[512,1024]{1,0:T(8,128)}, u32[]{:S(2)}) copy-start(f32[512,1024]{1,0:T(8,128)} %get-tuple-element.39) | copy-start | bytes 6291460
  137.3 6.7 %copy-start.13 = (bf16[32,32,128]{2,1,0:T(8,128)(2,1)S(1)}, bf16[32,32,128]{2,1,0:T(8,128)(2,1)}, u32[]{:S(2)}) copy-start(bf16[32,32,128]{2,1,0:T(8,128)(2,1)} %get-tuple-element.55) | copy-start | bytes 786436
  137.4 7.7 %copy-start.9 = (f32[512,128]{1,0:T(8,128)S(1)}, f32[512,128]{1,0:T(8,128)}, u32[]{:S(2)}) copy-start(f32[512,128]{1,0:T(8,128)} %get-tuple-element.40) | copy-start | bytes 786436
  137.4 102.5 %collective-permute-start = (bf16[160,2048]{1,0:T(8,128)(2,1)}, bf16[160,2048]{1,0:T(8,128)(2,1)}, u32[]{:S(2)}, u32[]{:S(2)}) collective-permute-start(bf16[160,2048]{1,0:T(8,128)(2,1)} %get-tuple-element.138), channel_id=1, source_target_pairs={{0,1},{1,2},{2,3},{3,0},{4,5},{5,6},{6,7},{7,4},{8,9},{9,10},{10,1... | collective-permute-start | bytes 1966088 | tf_op jit(solution)/shard_map/ppermute | solution.py:793
  141.2 98.7 %collective-permute-start.1 = (bf16[160,2048]{1,0:T(8,128)(2,1)}, bf16[160,2048]{1,0:T(8,128)(2,1)}, u32[]{:S(2)}, u32[]{:S(2)}) collective-permute-start(bf16[160,2048]{1,0:T(8,128)(2,1)} %get-tuple-element.137), channel_id=1, source_target_pairs={{0,2},{1,3},{2,0},{3,1},{4,6},{5,7},{6,4},{7,5},{8,10},{9,11},{10,... | collective-permute-start | bytes 1966088 | tf_op jit(solution)/shard_map/ppermute | solution.py:793
  143.0 96.9 %collective-permute-start.2 = (bf16[160,2048]{1,0:T(8,128)(2,1)}, bf16[160,2048]{1,0:T(8,128)(2,1)}, u32[]{:S(2)}, u32[]{:S(2)}) collective-permute-start(bf16[160,2048]{1,0:T(8,128)(2,1)} %get-tuple-element.136), channel_id=1, source_target_pairs={{0,3},{1,0},{2,1},{3,2},{4,7},{5,4},{6,5},{7,6},{8,11},{9,8},{10,9... | collective-permute-start | bytes 1966088 | tf_op jit(solution)/shard_map/ppermute | solution.py:793
  145.9 89.8 %copy-start.1 = (bf16[512,1024]{1,0:T(8,128)(2,1)S(1)}, bf16[512,1024]{1,0:T(8,128)(2,1)}, u32[]{:S(2)}) copy-start(bf16[512,1024]{1,0:T(8,128)(2,1)} %refs_0_.1) | copy-start | bytes 3145732
  337.1 1.7 copy-start.14
  340.5 52.9 %collective-permute-start.3 = (bf16[160,2048]{1,0:T(8,128)(2,1)}, bf16[160,2048]{1,0:T(8,128)(2,1)}, u32[]{:S(2)}, u32[]{:S(2)}) collective-permute-start(bf16[160,2048]{1,0:T(8,128)(2,1)} %get-tuple-element.132), channel_id=1, source_target_pairs={{0,3},{1,0},{2,1},{3,2},{4,7},{5,4},{6,5},{7,6},{8,11},{9,8},{10,9... | collective-permute-start | bytes 1966088 | tf_op jit(solution)/shard_map/ppermute | solution.py:793
  343.3 55.7 %collective-permute-start.4 = (bf16[160,2048]{1,0:T(8,128)(2,1)}, bf16[160,2048]{1,0:T(8,128)(2,1)}, u32[]{:S(2)}, u32[]{:S(2)}) collective-permute-start(bf16[160,2048]{1,0:T(8,128)(2,1)} %get-tuple-element.131), channel_id=1, source_target_pairs={{0,2},{1,3},{2,0},{3,1},{4,6},{5,7},{6,4},{7,5},{8,10},{9,11},{10,... | collective-permute-start | bytes 1966088 | tf_op jit(solution)/shard_map/ppermute | solution.py:793
  343.3 55.7 %collective-permute-start.5 = (bf16[160,2048]{1,0:T(8,128)(2,1)}, bf16[160,2048]{1,0:T(8,128)(2,1)}, u32[]{:S(2)}, u32[]{:S(2)}) collective-permute-start(bf16[160,2048]{1,0:T(8,128)(2,1)} %get-tuple-element.130), channel_id=1, source_target_pairs={{0,1},{1,2},{2,3},{3,0},{4,5},{5,6},{6,7},{7,4},{8,9},{9,10},{10,1... | collective-permute-start | bytes 1966088 | tf_op jit(solution)/shard_map/ppermute | solution.py:793
  399.1 3.7 copy-start.5
  399.1 3.7 copy-start.10
  402.8 2.0 copy-start.2
  402.8 1.9 copy-start.15
  412.5 4.7 copy-start.3
  412.5 4.7 copy-start.6
  412.5 4.7 copy-start.11
  417.2 2.1 copy-start.18
  419.3 2.3 copy-start.7
  466.7 3.4 copy-start.17
  481.3 6.1 %copy-start.8 = (f32[512,1024]{1,0:T(8,128)S(1)}, f32[512,1024]{1,0:T(8,128)}, u32[]{:S(2)}) copy-start(f32[512,1024]{1,0:T(8,128)} %copy-done.7) | copy-start | bytes 6291460
  558.4 3.8 copy-start.4
  (1 other events, 1.1 us)

commit v4 on v3

--- a/solution.py
+++ b/solution.py
@@ -16,7 +16,6 @@
 MIB = 1 << 20
 AXES = ("node", "expert")
 MESH = pl.DeviceIdType.MESH
-highest = lax.Precision.HIGHEST
 epsilon = 1e-05
 f32 = jnp.float32
 bf16 = jnp.bfloat16
@@ -193,27 +192,29 @@
 
 
 class Scatter:
-    def __init__(self, arrays, layout, experts):
-        self.args, self.layout, self.experts = arrays, layout, experts
+    RING = 4
+
+    def __init__(self, arrays, layout, experts, outs, store, start=0, stride=1, made=None):
+        self.layout, self.experts, self.outs, self.store = layout, experts, outs, store
+        self.start, self.stride = start, stride
+        self.args = [] if layout == "made" else arrays
         dense = self.dense = layout != "plane"
-        shape = arrays[0].shape
         if layout == "plane":
-            counts, h = [a.shape[2] for a in arrays], shape[4:]
+            counts, h = [a.shape[2] for a in arrays], arrays[0].shape[4:]
         elif layout == "rows":
-            counts, h = [a.shape[4] for a in arrays], shape[3:4] + shape[5:]
+            counts, h = [a.shape[4] for a in arrays], arrays[0].shape[3:4] + arrays[0].shape[5:]
         else:
-            counts, h = [a.shape[5] // BLOCK for a in arrays], shape[3:5] + (BLOCK,)
-        self.starts = [sum(counts[:a]) for a in range(len(arrays) + 1)]
+            counts, h = [made[0]], made[4:]
+        self.starts = [sum(counts[:a]) for a in range(len(counts) + 1)]
         m = self.m = sum(counts)
-        self.half = h
         unit = h[1:] if dense else (2,) + h
-        self.outs = [jax.ShapeDtypeStruct((m,) + unit, f32)]
-        self.in_specs = [pl.BlockSpec(memory_space=pltpu.HBM)] * len(arrays)
-        self.out_specs = [pl.BlockSpec(memory_space=pltpu.VMEM)]
+        ring = self.ring = min(self.RING, m)
+        self.in_specs = [pl.BlockSpec(memory_space=pltpu.HBM)] * len(self.args)
+        self.out_specs = [pl.BlockSpec(memory_space=pltpu.VMEM)] * len(outs)
         kinds = 7 + experts
         self.scratch = [
-            pltpu.VMEM((m, 4, 2) + h, bf16),
-            pltpu.VMEM((m, 4, 2) + h, bf16),
+            pltpu.VMEM(made or (m, 4, 2) + h, bf16),
+            pltpu.VMEM((ring, 4, 2) + h, bf16),
             pltpu.VMEM((m, 2) + h, bf16),
             pltpu.VMEM((m, 2) + h, bf16),
             pltpu.VMEM((m,) + h, bf16),
@@ -225,11 +226,11 @@
         if dense:
             self.scratch.append(pltpu.VMEM((m, experts - 1) + unit, bf16))
         self.late = 4 if dense else 3
-        self.turns = m + self.late
+        self.turns = start + (m - 1) * stride + 1 + self.late
         self.along_z = dense
 
     def bind(self, ins, outs, scratch, place):
-        self.ins, self.out, self.place = ins, outs[0], place
+        self.ins, self.out, self.place = ins, outs, place
         self.own, self.rc, self.rx, self.ry, self.lx, self.ly, self.send, self.recv, self.loc = scratch[:9]
         self.rz = scratch[9] if self.dense else None
 
@@ -246,15 +247,18 @@
     def part(self, source, core, chunk):
         if self.layout == "plane":
             return source.at[:, core, chunk]
-        if self.layout == "rows":
-            return source.at[:, core, :, :, chunk]
-        return source.at[:, core, :, :, :, pl.ds(pl.multiple_of(chunk * BLOCK, BLOCK), BLOCK)]
+        return source.at[:, core, :, :, chunk]
+
+    def at(self, i, site, *more):
+        return (i, site, self.place.k) + more if self.layout == "made" else (i, site) + more
 
     def first(self, source, i, chunk):
         p = self.place
+        land = self.rc.at[lax.rem(i, self.ring)]
+        if self.layout == "made":
+            return [self.remote(self.own.at[i, :, 1 - p.k], land, i, 0, (p.nc, p.e))]
         local = pltpu.make_async_copy(self.part(source, p.k, chunk), self.own.at[i], self.loc.at[i])
-        over = self.remote(self.part(source, 1 - p.k, chunk), self.rc.at[i], i, 0, (p.nc, p.e))
-        return local, over
+        return [self.remote(self.part(source, 1 - p.k, chunk), land, i, 0, (p.nc, p.e)), local]
 
     def sites(self):
         p = self.place
@@ -263,19 +267,20 @@
     def round_one(self, i):
         p = self.place
         _, to_x, to_y, diag = self.sites()
+        own = lambda *at: self.own.at[self.at(i, *at)]
         return [
-            self.remote(self.own.at[i, diag, 0], self.rx.at[i, 0], i, 1, (p.nx, p.e)),
-            self.remote(self.own.at[i, diag, 1], self.ry.at[i, 0], i, 2, (p.ny, p.e)),
-            self.remote(self.own.at[i, to_x, 0], self.rx.at[i, 1], i, 3, (p.nx, p.e)),
-            self.remote(self.own.at[i, to_y, 1], self.ry.at[i, 1], i, 4, (p.ny, p.e)),
+            self.remote(own(diag, 0), self.rx.at[i, 0], i, 1, (p.nx, p.e)),
+            self.remote(own(diag, 1), self.ry.at[i, 0], i, 2, (p.ny, p.e)),
+            self.remote(own(to_x, 0), self.rx.at[i, 1], i, 3, (p.nx, p.e)),
+            self.remote(own(to_y, 1), self.ry.at[i, 1], i, 4, (p.ny, p.e)),
         ]
 
     def round_two(self, i):
         p = self.place
         _, to_x, to_y, _ = self.sites()
         return [
-            self.remote(self.own.at[i, to_x, 1], self.lx.at[i], i, 5, (p.nx, p.e)),
-            self.remote(self.own.at[i, to_y, 0], self.ly.at[i], i, 6, (p.ny, p.e)),
+            self.remote(self.own.at[self.at(i, to_x, 1)], self.lx.at[i], i, 5, (p.nx, p.e)),
+            self.remote(self.own.at[self.at(i, to_y, 0)], self.ly.at[i], i, 6, (p.ny, p.e)),
         ]
 
     def round_z(self, i):
@@ -285,35 +290,41 @@
         copies = []
         for j in range(1, self.experts):
             to = lax.rem(p.e + j, self.experts)
-            source = self.own.at[i, mine, to // s, lax.rem(to, s)]
+            source = self.own.at[self.at(i, mine, to // s, lax.rem(to, s))]
             copies.append(self.remote(source, self.rz.at[i, j - 1], i, 6 + j, p.z(j)))
         return copies
 
     def turn(self, now):
         steps = (self.load, self.chip, self.cross, self.plane, self.column)
         for late, step in enumerate(steps[: self.late + 1]):
-            i = now - late
-
-            @when(jnp.logical_and(i >= 0, i < self.m))
+            since = now - self.start - late
+            i = since // self.stride
+            due = jnp.logical_and(since >= 0, i < self.m)
+            if self.stride > 1:
+                due = jnp.logical_and(due, lax.rem(since, self.stride) == 0)
+
+            @when(due)
             def _(step=step, i=i):
                 step(i)
 
     def load(self, i):
+        if self.layout == "made":
+            self.first(None, i, 0)[0].start()
+            return
         for a, source in enumerate(self.ins):
 
             @when(jnp.logical_and(i >= self.starts[a], i < self.starts[a + 1]))
             def _(a=a, source=source):
-                local, over = self.first(source, i, i - self.starts[a])
-                over.start()
-                local.start()
+                for copy in self.first(source, i, i - self.starts[a]):
+                    copy.start()
 
     def chip(self, i):
-        local, over = self.first(self.ins[0], i, 0)
-        local.wait()
-        over.wait()
+        for copy in self.first(None if self.layout == "made" else self.ins[0], i, 0):
+            copy.wait()
 
         def sum_one(q, _):
-            self.own[i, q] = add(self.own[i, q], self.rc[i, q]).astype(bf16)
+            at = self.at(i, q)
+            self.own[at] = add(self.own[at], self.rc[lax.rem(i, self.ring), q]).astype(bf16)
             return 0
 
         lax.fori_loop(0, 4, sum_one, 0)
@@ -326,9 +337,10 @@
         _, to_x, to_y, _ = self.sites()
         for copy in one:
             copy.wait()
-        self.own[i, to_x, 1] = add(self.own[i, to_x, 1], self.ry[i, 0]).astype(bf16)
+        at_x, at_y = self.at(i, to_x, 1), self.at(i, to_y, 0)
+        self.own[at_x] = add(self.own[at_x], self.ry[i, 0]).astype(bf16)
         two[0].start()
-        self.own[i, to_y, 0] = add(self.own[i, to_y, 0], self.rx[i, 0]).astype(bf16)
+        self.own[at_y] = add(self.own[at_y], self.rx[i, 0]).astype(bf16)
         two[1].start()
 
     def plane(self, i):
@@ -336,15 +348,14 @@
             copy.wait()
         mine, _, _, _ = self.sites()
         sums = (
-            add(self.own[i, mine, 0], self.rx[i, 1], self.ly[i]),
-            add(self.own[i, mine, 1], self.lx[i], self.ry[i, 1]),
+            add(self.own[self.at(i, mine, 0)], self.rx[i, 1], self.ly[i]),
+            add(self.own[self.at(i, mine, 1)], self.lx[i], self.ry[i, 1]),
         )
         if not self.dense:
-            for h in range(2):
-                self.out[i, h] = sums[h]
+            self.store(self.out, i, jnp.concatenate(sums, axis=0))
             return
         for h in range(2):
-            self.own[i, mine, h] = sums[h].astype(bf16)
+            self.own[self.at(i, mine, h)] = sums[h].astype(bf16)
         for copy in self.round_z(i):
             copy.start()
 
@@ -354,8 +365,8 @@
         p = self.place
         mine, _, _, _ = self.sites()
         s = self.experts // 2
-        terms = [self.own[i, mine, p.e // s, lax.rem(p.e, s)]] + [self.rz[i, j] for j in range(self.experts - 1)]
-        self.out[i] = add(*terms)
+        terms = [self.own[self.at(i, mine, p.e // s, lax.rem(p.e, s))]]
+        self.store(self.out, i, add(*terms, *(self.rz[i, j] for j in range(self.experts - 1))))
 
 
 def add(*terms):
@@ -363,7 +374,7 @@
 
 
 def call(name, steps, body, args, in_specs, outs, out_specs, scratch, moves, collective_id, experts, flops):
-    total = max(steps, moves.turns if moves else 0)
+    total = max([steps] + [m.turns for m in moves])
 
     def hold(spec):
         if spec.block_shape is None:
@@ -371,23 +382,26 @@
         index = spec.index_map
         return pl.BlockSpec(spec.block_shape, lambda j: index(jnp.minimum(j, steps - 1)))
 
-    n_in, n_out, n_scratch = len(args), len(outs), len(scratch)
-    m_in, m_out = (len(moves.args), len(moves.outs)) if moves else (0, 0)
+    join = lambda what: [x for m in moves for x in getattr(m, what)]
 
     def kernel(*refs):
         refs = list(refs)
-        take = lambda count: [refs.pop(0) for _ in range(count)]
-        ins, m_ins, os, m_os, own = take(n_in), take(m_in), take(n_out), take(m_out), take(n_scratch)
+        take = lambda group: [refs.pop(0) for _ in group]
+        ins, m_ins = take(args), [take(m.args) for m in moves]
+        os, m_os = take(outs), [take(m.outs) for m in moves]
+        own, m_own = take(scratch), [take(m.scratch) for m in moves]
         now = pl.program_id(0)
         if moves:
             place = Place(experts)
-            moves.bind(m_ins, m_os, refs, place)
+            for m, a, o, r in zip(moves, m_ins, m_os, m_own):
+                m.bind(a, o, r, place)
 
             @when(now == 0)
             def _():
-                place.greet(moves.along_z)
-
-            moves.turn(now)
+                place.greet(any(m.along_z for m in moves))
+
+            for m in moves:
+                m.turn(now)
         if body is not None:
 
             @when(now < steps)
@@ -397,17 +411,17 @@
     return pl.pallas_call(
         kernel,
         grid=(total,),
-        out_shape=list(outs) + (moves.outs if moves else []),
-        in_specs=[hold(s) for s in in_specs] + (moves.in_specs if moves else []),
-        out_specs=[hold(s) for s in out_specs] + (moves.out_specs if moves else []),
-        scratch_shapes=list(scratch) + (moves.scratch if moves else []),
+        out_shape=list(outs) + join("outs"),
+        in_specs=[hold(s) for s in in_specs] + join("in_specs"),
+        out_specs=[hold(s) for s in out_specs] + join("out_specs"),
+        scratch_shapes=list(scratch) + join("scratch"),
         cost_estimate=pl.CostEstimate(flops=flops, bytes_accessed=32 * MIB, transcendentals=0),
         compiler_params=pltpu.CompilerParams(
             vmem_limit_bytes=60 * MIB,
             **({"collective_id": collective_id, "has_side_effects": True} if moves else {}),
         ),
         name=name,
-    )(*args, *(moves.args if moves else []))
+    )(*args, *join("args"))
 
 
 def masks():
@@ -462,10 +476,9 @@
             rows(width, f32),
             rows(width, bf16),
             rows(width, bf16),
-            jax.ShapeDtypeStruct((slots, 2 * width), bf16),
             rows(slots, bf16),
             rows(128, f32),
-        ]
+        ] + [jax.ShapeDtypeStruct((capacity, 2 * width), bf16)] * experts
         self.scratch = [
             pltpu.VMEM((devices, share, 128), bf16),
             pltpu.VMEM((devices, share, 3 * width), bf16),
@@ -478,7 +491,9 @@
     def __call__(self, now, steps, tok, cot, route, drop, *refs):
         full = self.moves.full[:3] if self.moves else refs[:3]
         refs = refs if self.moves else refs[3:]
-        qkv, lse, att, after, mixed, gd, leave, disp, info, ws, wq, wo, gains, attn_in, sems = refs
+        qkv, lse, att, after, mixed, gd, disp, info = refs[:8]
+        leave = refs[8 : 8 + self.experts]
+        ws, wq, wo, gains, attn_in, sems = refs[8 + self.experts :]
         width, length = self.width, self.length
         loads = [pltpu.make_async_copy(a, b, sems.at[i]) for i, (a, b) in enumerate(zip(full, (ws, wq, wo)))]
 
@@ -523,9 +538,9 @@
         def _():
             loads[2].start()
             loads[2].wait()
-            self.route(tok, cot, route, drop, att, wo, ws, gains, after, mixed, gd, leave, disp, info)
-
-    def route(self, tok, cot, route, drop, att, wo, ws, gains, after, mixed, gd, leave, disp, info):
+            self.route(tok, cot, route, drop, att, wo, ws, gains, after, mixed, gd, disp, info, leave)
+
+    def route(self, tok, cot, route, drop, att, wo, ws, gains, after, mixed, gd, disp, info, leave):
         width, length, experts = self.width, self.length, self.experts
         after[...] = tok[...].astype(f32) + matmul(att[...], wo[...].reshape(width, width))
         normed, _ = normalize(after[...])
@@ -555,13 +570,15 @@
         target = jnp.where(turn < 0, turn + experts, turn) * self.capacity + position
         slot = lax.broadcasted_iota(jnp.int32, (length, experts * self.capacity), 1)
         disp[...] = jnp.where(slot == target, 1.0, 0.0).astype(bf16)
-        leave[:, :width] = product_tn(disp[...], mixed[...]).astype(bf16)
-        leave[:, width:] = product_tn(disp[...], (coef_1 * gate * grad).astype(bf16)).astype(bf16)
-
-
-def attend_backward_kernel(q_ref, k_ref, v_ref, g_ref, lse_ref, d_ref):
+        sent = (mixed[...], (coef_1 * gate * grad).astype(bf16))
+        for h, values in enumerate(sent):
+            placed = product_tn(disp[...], values).astype(bf16)
+            for j in range(experts):
+                leave[j][:, h * width : (h + 1) * width] = placed[j * self.capacity : (j + 1) * self.capacity]
+
+
+def attend_pair_backward(q, k, v, g, lse):
     scaling = 1.0 / math.sqrt(HD)
-    q, k, v, g = q_ref[...], k_ref[...], v_ref[...], g_ref[...]
     qs = q * scaling
     kt = k.T
     length = q.shape[0]
@@ -574,7 +591,7 @@
         for c, start in enumerate(range(0, length, QB)):
             end = start + QB
             scores = causal(outer_nt(kh[:end], qs[start:end]), start)
-            probs = jnp.exp(scores - lse_ref[0, h : h + 1, start:end])
+            probs = jnp.exp(scores - lse[h : h + 1, start:end])
             grad_probs = outer_nt(vh[:end], g[start:end])
             delta = jnp.sum(probs * grad_probs, axis=0, keepdims=True)
             grad_scores = (probs * (grad_probs - delta)).astype(bf16)
@@ -586,30 +603,215 @@
                 grad_k[b] = grad_k[b] + more_k[rows]
             row.append(matmul(kt[h * HD : (h + 1) * HD, :end], grad_scores))
         grad_q.append(jnp.concatenate(row, axis=1))
-    d_ref[0] = (jnp.concatenate(grad_q, axis=0).T * scaling).astype(bf16)
-    for b in range(length // QB):
-        d_ref[1, b * QB : (b + 1) * QB] = (grad_k[b] * scaling).astype(bf16)
-        d_ref[2, b * QB : (b + 1) * QB] = grad_v[b].astype(bf16)
-
-
-def attend_backward(qkv, lse, grad, width, moves, collective_id, experts):
-    length = qkv.shape[0]
-    pairs = width // PAIR
-    part = lambda p: pl.BlockSpec((SEQ, PAIR), lambda j: (j // pairs, p * pairs + lax.rem(j, pairs)))
-    return call(
-        "attend_backward",
-        length // SEQ * pairs,
-        lambda now, steps, *refs: attend_backward_kernel(*refs),
-        [qkv, qkv, qkv, grad, lse],
-        [part(0), part(1), part(2), part(0), pl.BlockSpec((1, 2, SEQ), lambda j: (j, 0, 0))],
-        [jax.ShapeDtypeStruct((3, length, width), bf16)],
-        [pl.BlockSpec((3, SEQ, PAIR), lambda j: (0, j // pairs, lax.rem(j, pairs)))],
-        [],
-        moves,
-        collective_id,
-        experts,
-        10 * length * SEQ * width,
+    return (
+        (jnp.concatenate(grad_q, axis=0).T * scaling).astype(bf16),
+        (jnp.concatenate(grad_k, axis=0) * scaling).astype(bf16),
+        jnp.concatenate(grad_v, axis=0).astype(bf16),
     )
+
+
+def thirds(values):
+    parts = []
+    for _ in range(3):
+        parts.append(values.astype(bf16))
+        values = values - parts[-1].astype(f32)
+    return parts
+
+
+class Back:
+    GROUP = 2
+
+    def __init__(self, length, width, experts, devices, capacity):
+        self.length, self.width, self.experts, self.capacity = length, width, experts, capacity
+        self.devices, self.share = devices, width // devices
+        self.pairs = width // PAIR
+        self.groups = self.pairs // self.GROUP
+        self.part = self.GROUP * PAIR
+        self.columns = 3 * self.part
+        self.rest = width - self.columns
+        self.items = self.groups + 2
+        self.heads_at = 3
+        self.last = self.heads_at + self.pairs
+        self.steps = self.last + 1
+        self.first_item = self.heads_at
+        self.outs = [
+            jax.ShapeDtypeStruct((length, width), bf16),
+            jax.ShapeDtypeStruct((length, width), f32),
+        ]
+        slots = experts * capacity
+        self.scratch = [
+            pltpu.VMEM((slots, 2 * width), bf16),
+            pltpu.VMEM((length, width), f32),
+            pltpu.VMEM((length, width), f32),
+            pltpu.VMEM((devices, self.share, 128), bf16),
+            pltpu.VMEM((devices, self.share, width), bf16),
+            pltpu.VMEM((2, devices, self.share, self.columns), bf16),
+            pltpu.VMEM((8, width), f32),
+            pltpu.VMEM((128, width), f32),
+            pltpu.VMEM((width, length), bf16),
+            pltpu.VMEM((length, width), bf16),
+            pltpu.VMEM((length, self.columns), bf16),
+            pltpu.SemaphoreType.DMA((5 + experts,)),
+            pltpu.SemaphoreType.DMA((2, 3)),
+        ]
+
+    def made(self):
+        chips = (4, 2, 2, self.experts // 2) if self.devices == 8 * self.experts else (self.devices,)
+        return (self.items,) + chips + (self.share, self.columns)
+
+    def final_outs(self):
+        share, width = self.share, self.width
+        return [jax.ShapeDtypeStruct((share, c), f32) for c in (3 * width, width, 128)]
+
+    def store(self, outs, i, value):
+        d_qkv, d_out, d_small = outs
+        part = self.part
+
+        @when(i == 0)
+        def _():
+            d_out[:, : self.columns] = value
+
+        @when(jnp.logical_and(i > 0, i <= self.groups))
+        def _():
+            for p in range(3):
+                at = pl.multiple_of(p * self.width + (i - 1) * part, part)
+                d_qkv[:, pl.ds(at, part)] = value[:, p * part : (p + 1) * part]
+
+        @when(i == self.groups + 1)
+        def _():
+            d_out[:, self.columns :] = value[:, : self.rest]
+            d_small[...] = value[:, self.rest : self.rest + 128]
+
+    def __call__(self, now, steps, *refs):
+        experts, width, length = self.experts, self.width, self.length
+        refs = list(refs)
+        tok, cot, route, drop, qkv, lse, att, mixed_in, disp, info = refs[:10]
+        small_hbm, qkv_hbm, out_hbm, dense_hbm, grad_hbm, after_hbm = refs[10:16]
+        came_hbm = refs[16 : 16 + experts]
+        mixed, tokens_grad, *rest = refs[16 + experts :]
+        if self.moves:
+            made = self.moves[-1].own
+        else:
+            made = rest.pop(0)
+        came, dense, grads, ws, wo, wq, gains, d_heads, attn_in_t, grad_att, d_group, sems, wq_sems = rest
+        fetch = lambda a, b, i: pltpu.make_async_copy(a, b, sems.at[i])
+        capacity = self.capacity
+        loads = [fetch(came_hbm[j], came.at[pl.ds(j * capacity, capacity)], j) for j in range(experts)]
+        loads += [
+            fetch(a, b, experts + i)
+            for i, (a, b) in enumerate(
+                ((dense_hbm, dense), (grad_hbm, grads), (after_hbm, tokens_grad), (small_hbm, ws), (out_hbm, wo))
+            )
+        ]
+
+        def group_weights(group):
+            slot = lax.rem(group, 2)
+            return [
+                pltpu.make_async_copy(
+                    qkv_hbm.at[:, :, pl.ds(pl.multiple_of(p * width + group * self.part, self.part), self.part)],
+                    wq.at[slot, :, :, pl.ds(p * self.part, self.part)],
+                    wq_sems.at[slot, p],
+                )
+                for p in range(3)
+            ]
+
+        put = lambda i, columns, values: self.put(made, i, columns, values)
+        lane = lax.broadcasted_iota(jnp.int32, (length, 128), 1)
+        over_lanes = lambda a: jnp.sum(a, axis=1, keepdims=True)
+
+        @when(now == 0)
+        def _():
+            for copy in loads:
+                copy.start()
+            for copy in group_weights(0):
+                copy.start()
+            for copy in loads:
+                copy.wait()
+            probs = jnp.where(jnp.logical_and(lane >= 2, lane < 2 + experts), info[...], 0.0)
+            coef_0 = over_lanes(jnp.where(lane == 2 + experts, info[...], 0.0))
+            coef_1 = over_lanes(jnp.where(lane == 3 + experts, info[...], 0.0))
+            chosen = jnp.where(lane - 2 == route[...], 1.0, 0.0)
+            kept = (1 - drop[...]).astype(f32)
+            gate_prob = over_lanes(probs * chosen)
+            gate = gate_prob * kept
+            grad = cot[...].astype(f32)
+            expert_tok = matmul(disp[...], came[:, :width])
+            mixed[...] = (tokens_grad[...] + coef_0 * dense[...] + (coef_1 * gate) * expert_tok).astype(bf16)
+            shared = over_lanes(grad * expert_tok)
+            grad_0, grad_1 = over_lanes(grad * dense[...]), shared * gate
+            both = coef_0 * grad_0 + coef_1 * grad_1
+            grad_gate = shared * coef_1 * kept
+            logits = jnp.where(
+                jnp.logical_and(lane >= 2, lane < 2 + experts), (grad_gate * gate_prob) * (chosen - probs), 0.0
+            )
+            logits = jnp.where(lane == 2 + experts, coef_0 * (grad_0 - both), logits)
+            logits = jnp.where(lane == 3 + experts, coef_1 * (grad_1 - both), logits)
+            pieces = thirds(logits)
+            d_heads[...] = add(*(product_tn(p, mixed_in[...]) for p in pieces))
+            weights = ws[...].reshape(width, 128)
+            grads[...] = (
+                grads[...] + matmul(disp[...], came[:, width:]) + add(*(outer_nt(p, weights) for p in pieces))
+            )
+            gains[...] = weights.astype(f32).T[:8]
+
+        @when(now == 1)
+        def _():
+            normed, scale = normalize(tokens_grad[...])
+            d_heads[1:2] = jnp.sum(grads[...] * normed, axis=0, keepdims=True)
+            grads[...] = cot[...].astype(f32) + norm_back(grads[...] * gains[1:2], normed, scale)
+            normed, _ = normalize(tok[...].astype(f32))
+            attn_in_t[...] = (normed * gains[0:1]).astype(bf16).T
+
+        @when(now == 2)
+        def _():
+            grad_attn = grads[...].astype(bf16)
+            grad_att[...] = outer_nt(grad_attn, wo[...].reshape(width, width)).astype(bf16)
+            d_out = product_tn(att[...], grad_attn).astype(bf16)
+            put(0, slice(0, self.columns), d_out[:, : self.columns])
+            put(self.groups + 1, slice(0, self.rest), d_out[:, self.columns :])
+            dense[...] = jnp.zeros_like(dense)
+
+        @when(jnp.logical_and(now >= self.heads_at, now < self.last))
+        def _():
+            pair = now - self.heads_at
+            group, of_group = pair // self.GROUP, lax.rem(pair, self.GROUP)
+            cols = lambda part: pl.ds(pl.multiple_of(part * width + pair * PAIR, PAIR), PAIR)
+            results = attend_pair_backward(
+                qkv[:, cols(0)], qkv[:, cols(1)], qkv[:, cols(2)], grad_att[:, cols(0)], lse[pair]
+            )
+            for p, values in enumerate(results):
+                d_group[:, pl.ds(pl.multiple_of(p * self.part + of_group * PAIR, PAIR), PAIR)] = values
+
+            @when(of_group == self.GROUP - 1)
+            def _():
+                for copy in group_weights(group):
+                    copy.wait()
+
+                @when(group + 1 < self.groups)
+                def _():
+                    for copy in group_weights(group + 1):
+                        copy.start()
+
+                put(group + 1, slice(None), matmul(attn_in_t[...], d_group[...]).astype(bf16))
+                weights = wq[lax.rem(group, 2)].reshape(width, self.columns)
+                dense[...] += outer_nt(d_group[...], weights)
+
+        @when(now == self.last)
+        def _():
+            normed, scale = normalize(tok[...].astype(f32))
+            d_heads[0:1] = jnp.sum(dense[...] * normed, axis=0, keepdims=True)
+            put(self.groups + 1, slice(self.rest, self.rest + 128), d_heads[...].T.astype(bf16))
+            put(
+                self.groups + 1,
+                slice(self.rest + 128, self.columns),
+                jnp.zeros((width, self.columns - self.rest - 128), bf16),
+            )
+            tokens_grad[...] = grads[...] + norm_back(dense[...] * gains[0:1], normed, scale)
+
+    def put(self, made, i, columns, values):
+        lead = made.shape[1:-1]
+        at = (i,) + (slice(None),) * len(lead) + (columns,)
+        made[at] = values.reshape(lead + values.shape[1:])
 
 
 def gelu_both(v):
@@ -621,19 +823,32 @@
     return v * half, slope
 
 
-def mlp_kernel(share, now, steps, x_ref, g_ref, w1_ref, w2_ref, out_ref, back_ref, d1_ref, d2_ref, xt, gt, out_sum, back_sum):
+def mlp_kernel(share, parts, now, steps, *refs):
+    if parts:
+        pieces, (w1_ref, w2_ref), refs = refs[:parts], refs[parts : parts + 2], refs[parts + 2 :]
+        results, (d1_ref, d2_ref) = refs[:parts], refs[parts : parts + 2]
+        x, g, xt, gt, out_sum, back_sum = refs[parts + 2 :]
+    else:
+        x, g, w1_ref, w2_ref, out_sum, back_sum, d1_ref, d2_ref, xt, gt = refs
+    width = xt.shape[0]
+
     @when(now == 0)
     def _():
-        xt[...] = x_ref[...].T
-        gt[...] = g_ref[...].T
+        if parts:
+            size = pieces[0].shape[0]
+            for j, piece in enumerate(pieces):
+                x[j * size : (j + 1) * size] = piece[:, :width]
+                g[j * size : (j + 1) * size] = piece[:, width:]
+        xt[...] = x[...].T
+        gt[...] = g[...].T
         out_sum[...] = jnp.zeros_like(out_sum)
         back_sum[...] = jnp.zeros_like(back_sum)
 
     w1 = w1_ref[...].reshape(w1_ref.shape[-2:])
     w2 = w2_ref[...].reshape(w2_ref.shape[-2:])
-    hidden, slope = gelu_both(matmul(x_ref[...], w1))
+    hidden, slope = gelu_both(matmul(x[...], w1))
     hidden = hidden.astype(bf16)
-    grad_pre = (slope * outer_nt(g_ref[...], w2)).astype(bf16)
+    grad_pre = (slope * outer_nt(g[...], w2)).astype(bf16)
     out_sum[...] += matmul(hidden, w2)
     back_sum[...] += outer_nt(grad_pre, w1)
     d1 = matmul(xt[...], grad_pre).astype(bf16)
@@ -648,22 +863,26 @@
                 d1_ref[s, c * share : (c + 1) * share] = d1[s * share : (s + 1) * share, cols]
             d2_ref[c] = d2[:, cols]
 
-    @when(now == steps - 1)
-    def _():
-        out_ref[...] = out_sum[...].astype(out_ref.dtype)
-        back_ref[...] = back_sum[...].astype(back_ref.dtype)
-
-
-def mlp(x, g, w1, w2, out_dtype, name, moves, collective_id, experts, devices=None):
-    rows, width = x.shape
+    if parts:
+
+        @when(now == steps - 1)
+        def _():
+            for h, total in enumerate((out_sum, back_sum)):
+                for j, result in enumerate(results):
+                    rows = slice(j * result.shape[0], (j + 1) * result.shape[0])
+                    result[:, h * width : (h + 1) * width] = total[rows].astype(bf16)
+
+
+def mlp(rows_in, w1, w2, name, moves, collective_id, experts, devices=None):
     share = None
     if w1.ndim == 3:
-        blocks, _, size = w1.shape
+        blocks, width, size = w1.shape
         w1_spec = pl.BlockSpec((1, width, size), lambda j: (j, 0, 0))
         w2_spec = pl.BlockSpec((1, size, width), lambda j: (j, 0, 0))
         d_shape, d_specs = (blocks, width, size), [w1_spec] * 2
     else:
         size = BLOCK
+        width = w1.shape[0]
         blocks = w1.shape[1] // size
         w1_spec = pl.BlockSpec((width, size), lambda j: (0, j))
         w2_spec = pl.BlockSpec((size, width), lambda j: (j, 0))
@@ -676,20 +895,24 @@
                 pl.BlockSpec((size // 128, width, 128), lambda j: (j, 0, 0)),
             ]
     whole = pl.BlockSpec(memory_space=pltpu.VMEM)
+    joined = rows_in[0].shape[1] == 2 * width
+    parts = len(rows_in) if joined else 0
+    rows = sum(a.shape[0] for a in rows_in) if joined else rows_in[0].shape[0]
+    if joined:
+        outs = [jax.ShapeDtypeStruct(a.shape, bf16) for a in rows_in]
+    else:
+        outs = [jax.ShapeDtypeStruct((rows, width), f32)] * 2
+    flat, across = pltpu.VMEM((rows, width), bf16), pltpu.VMEM((width, rows), bf16)
+    sums = [pltpu.VMEM((rows, width), f32)] * 2
     return call(
         name,
         blocks,
-        functools.partial(mlp_kernel, share),
-        [x, g, w1, w2],
-        [whole, whole, w1_spec, w2_spec],
-        [jax.ShapeDtypeStruct((rows, width), out_dtype)] * 2 + [jax.ShapeDtypeStruct(d_shape, bf16)] * 2,
-        [whole, whole] + d_specs,
-        [
-            pltpu.VMEM((width, rows), bf16),
-            pltpu.VMEM((width, rows), bf16),
-            pltpu.VMEM((rows, width), f32),
-            pltpu.VMEM((rows, width), f32),
-        ],
+        functools.partial(mlp_kernel, share, parts),
+        list(rows_in) + [w1, w2],
+        [whole] * len(rows_in) + [w1_spec, w2_spec],
+        outs + [jax.ShapeDtypeStruct(d_shape, bf16)] * 2,
+        [whole] * len(outs) + d_specs,
+        [flat, flat, across, across] + sums if joined else [across, across],
         moves,
         collective_id,
         experts,
@@ -732,139 +955,143 @@
     cut = lambda a, rows, columns, m, n: [
         [(a, i * (rows // m), rows // m, j * (columns // n), columns // n)] for i in range(m) for j in range(n)
     ]
-    moves = gather_experts = None
     weights = (small, w_qkv, w_out, w_fc, w_proj)
     capacity = -(-(tok_rows * 10) // (8 * experts))
+    gather_dense, gather_experts = [], []
     if fast:
         items = cut(1, share, 3 * width, 1, 3) + cut(2, share, width, 1, 1)
         items += cut(3, share, ff, 1, 4) + cut(4, ff // devices, width, 4, 1)
         items[0] = cut(0, share, 128, 1, 1)[0] + items[0]
-        moves = Gather(list(weights), [True] * 5, items, nodes, experts)
-        gather_experts = Gather(
-            [win, wout], [False] * 2, cut(0, width, win.shape[1], 4, 1) + cut(1, wout.shape[0], width, 4, 1), nodes, experts
-        )
+        gather_dense = [Gather(list(weights), [True] * 5, items, nodes, experts)]
+        items = cut(0, width, win.shape[1], 4, 1) + cut(1, wout.shape[0], width, 4, 1)
+        gather_experts = [Gather([win, wout], [False] * 2, items, nodes, experts)]
         full = []
     else:
         full = [lax.all_gather(a, AXES, axis=0, tiled=False) for a in weights]
         win_full, wout_full = (lax.all_gather(a, "node", axis=0, tiled=False) for a in (win, wout))
-    front = Front(tok_rows, width, experts, devices, capacity, moves)
-    kept = full[:3]
-    whole, hbm = pl.BlockSpec(memory_space=pltpu.VMEM), pl.BlockSpec(memory_space=pltpu.HBM)
-    results = call(
-        "front",
-        front.steps,
-        front,
-        [tokens, cotangent, routes, dropped[:, None]] + kept,
-        [whole] * 4 + [hbm] * len(kept),
-        front.outs,
-        [whole] * len(front.outs),
-        front.scratch,
-        moves,
-        1,
-        experts,
-        12 * tok_rows * width * width,
-    )
-    qkv_rows, lse, attended, after_attn, mixed_in, grad_dense, leaving, dispatch, probs = results[:9]
-    full = results[9:] if fast else full
-    small_full, qkv_full, out_full, fc_full, proj_full = (together(a) for a in full)
 
     def scatter_xla(parts, axes):
         return lax.psum_scatter(parts, axes, scatter_dimension=0, tiled=False).astype(f32)
-
-    gain_first = small_full[:, 0].astype(f32)
-    gain_second = small_full[:, 1].astype(f32)
-    heads = small_full[:, 2 : 4 + experts]
-    residual = tokens.astype(f32)
-    normed_one, scale_one = normalize(residual)
-    attn_in = (normed_one * gain_first).astype(bf16)
-    normed_two, scale_two = normalize(after_attn)
-    router_probs, coef_tok = probs[:, 2 : 2 + experts], probs[:, 2 + experts : 4 + experts]
-    chosen = (routes == jnp.arange(experts, dtype=jnp.int32)[None, :]).astype(f32)
-    kept_tok = (1 - dropped).astype(f32)
-    gate_prob = jnp.sum(router_probs * chosen, axis=1)
-    gate_tok = gate_prob * kept_tok
-    weight_tok = coef_tok[:, 1:] * gate_tok[:, None]
-    grad_out = cotangent.astype(f32)
 
     def exchange(parts, sign):
         moved = [parts[0]]
         for j in range(1, experts):
             shift = [(s, (s + sign * j) % experts) for s in range(experts)]
             moved.append(lax.ppermute(parts[j], "expert", shift))
-        return jnp.concatenate(moved, axis=0)
-
-    arrived = exchange(leaving.reshape(experts, capacity, 2 * width), 1)
+        return moved
+
+    front = Front(tok_rows, width, experts, devices, capacity, gather_dense[0] if fast else None)
+    kept = full[:3]
+    whole, hbm = pl.BlockSpec(memory_space=pltpu.VMEM), pl.BlockSpec(memory_space=pltpu.HBM)
+    dropped = dropped[:, None]
+    results = call(
+        "front",
+        front.steps,
+        front,
+        [tokens, cotangent, routes, dropped] + kept,
+        [whole] * 4 + [hbm] * len(kept),
+        front.outs,
+        [whole] * len(front.outs),
+        front.scratch,
+        gather_dense,
+        1,
+        experts,
+        12 * tok_rows * width * width,
+    )
+    qkv_rows, lse, attended, after_attn, mixed_in, grad_dense, dispatch, probs = results[:8]
+    arrived = exchange(results[8 : 8 + experts], 1)
+    small_full, qkv_full, out_full, fc_full, proj_full = results[8 + experts :] if fast else full
 
     dense_out, grad_mixed, d_fc, d_proj, *gathered = mlp(
-        mixed_in, grad_dense, fc_full, proj_full, f32, "dense_mlp", gather_experts, 3, experts, devices if fast else None
+        [mixed_in, grad_dense],
+        together(fc_full),
+        together(proj_full),
+        "dense_mlp",
+        gather_experts,
+        2,
+        experts,
+        devices if fast else None,
     )
-    scatter_dense = None
+    scatter_dense = []
     if fast:
         win_full, wout_full = gathered
-        by_chip = lambda a: a.reshape(4, 2, 2, experts // 2, 4, width // 4, 128)
-        scatter_dense = Scatter([by_chip(d_fc), by_chip(d_proj)], "rows", experts)
-    returned, grad_rows, d_win, d_wout, *scattered = mlp(
-        arrived[:, :width], arrived[:, width:], win_full, wout_full, bf16, "expert_mlp", scatter_dense, 4, experts
+        chunks = 4
+        by_chip = lambda a: a.reshape(4, 2, 2, experts // 2, chunks, width // chunks, 128)
+
+        def store_dense(outs, i, value):
+            step = width // chunks
+
+            @when(i < chunks)
+            def _():
+                for q in range(step // share):
+                    at = pl.multiple_of(i * (step // share * 128) + q * 128, 128)
+                    outs[0][:, pl.ds(at, 128)] = value[q * share : (q + 1) * share]
+
+            @when(i >= chunks)
+            def _():
+                at = pl.multiple_of((i - chunks) * step, step)
+                outs[1][:, pl.ds(at, step)] = value.T
+
+        outs = [jax.ShapeDtypeStruct((share, ff), f32), jax.ShapeDtypeStruct((ff // devices, width), f32)]
+        scatter_dense = [Scatter([by_chip(d_fc), by_chip(d_proj)], "rows", experts, outs, store_dense)]
+    *returned, d_win, d_wout, grad_fc, grad_proj = (
+        list(mlp(arrived, win_full, wout_full, "expert_mlp", scatter_dense, 3, experts)) + ([] if fast else [None] * 2)
     )
-    leaving = jnp.concatenate([returned, grad_rows], axis=1)
-    came_back = exchange(leaving.reshape(experts, capacity, 2 * width), -1)
+    came_back = exchange(returned, -1)
+    back = Back(tok_rows, width, experts, devices, capacity)
+    back.moves = []
     if fast:
-        by_column = scattered[0].reshape(2, width, 128)
-        grad_fc = by_column[0].reshape(ff // 128, share, 128).transpose(1, 0, 2).reshape(share, ff)
-        grad_proj = by_column[1].T
-        cut_rows = lambda a: a.reshape(4, 2, 8, 2, width // 16, a.shape[2])
-        scatter_win = Scatter([cut_rows(d_win)], "plane", experts)
-        scatter_wout = Scatter([cut_rows(d_wout)], "plane", experts)
-        (grad_win,) = move("scatter_win", scatter_win, 5, experts)
-        grad_win = grad_win.reshape(width, -1)
+        chunks_e = 8
+        size = width // chunks_e
+        cut_rows = lambda a: a.reshape(4, 2, chunks_e, 2, size // 2, a.shape[2])
+        at = lambda i: pl.ds(pl.multiple_of(i * size, size), size)
+
+        def store_win(outs, i, value):
+            outs[0][0, at(i)] = value
+
+        def store_wout(outs, i, value):
+            outs[0][0, :, at(i)] = value.T
+
+        like = lambda a: [jax.ShapeDtypeStruct(a.shape, f32)]
+        scatter_win = Scatter([cut_rows(d_win)], "plane", experts, like(expert_in), store_win)
+        scatter_wout = Scatter([cut_rows(d_wout)], "plane", experts, like(expert_out), store_wout)
+        (grad_win,) = move("scatter_win", [scatter_win], 4, experts)
+        scatter_rest = Scatter(
+            [], "made", experts, back.final_outs(), back.store, back.first_item, back.GROUP, back.made()
+        )
+        back.moves = [scatter_wout, scatter_rest]
+    outs = back.outs + ([] if fast else [jax.ShapeDtypeStruct((back.items, width, back.columns), bf16)])
+    mixed, tokens_grad, *results = call(
+        "back",
+        back.steps,
+        back,
+        [tokens, cotangent, routes, dropped, qkv_rows, lse, attended, mixed_in, dispatch, probs]
+        + [small_full, qkv_full, out_full, dense_out, grad_mixed, after_attn]
+        + came_back,
+        [whole] * 10 + [hbm] * (6 + experts),
+        outs,
+        [whole] * len(outs),
+        back.scratch,
+        back.moves,
+        5,
+        experts,
+        32 * tok_rows * width * width,
+    )
+    if fast:
+        grad_wout, grad_wqkv, grad_wo, grad_small = results
     else:
+        summed = scatter_xla(results[0].reshape(back.items, devices, share, -1).swapaxes(0, 1), AXES)
+        grad_wo = jnp.concatenate([summed[0], summed[-1][:, : back.rest]], axis=1)
+        grad_small = summed[-1][:, back.rest : back.rest + 128]
+        groups = summed[1:-1].reshape(back.groups, share, 3, back.part)
+        grad_wqkv = groups.transpose(1, 2, 0, 3).reshape(share, 3 * width)
         grad_fc = scatter_xla(d_fc.reshape(devices, share, ff), AXES)
         by_unit = d_proj.reshape(width, devices, ff // devices).transpose(1, 0, 2)
         grad_proj = scatter_xla(by_unit, AXES).T
-        grad_win = scatter_xla(d_win, "node")
-        grad_wout = scatter_xla(d_wout, "node")
-        scatter_wout = None
-    came_back = matmul(dispatch, came_back)
-    expert_tok, grad_back = came_back[:, :width], came_back[:, width:]
-
-    mixed = after_attn + coef_tok[:, :1] * dense_out + weight_tok * expert_tok
-    shared = jnp.sum(grad_out * expert_tok, axis=1)
-    grad_coef = jnp.stack([jnp.sum(grad_out * dense_out, axis=1), shared * gate_tok], axis=1)
-    grad_coef_logit = coef_tok * (grad_coef - jnp.sum(coef_tok * grad_coef, axis=1, keepdims=True))
-    grad_gate = shared * coef_tok[:, 1] * kept_tok
-    grad_route_logit = (grad_gate * gate_prob)[:, None] * (chosen - router_probs)
-    grad_logits = jnp.concatenate([grad_route_logit, grad_coef_logit], axis=1)
-    grad_mixed = grad_mixed + grad_back
-    grad_mixed = grad_mixed + jnp.dot(grad_logits, heads.astype(f32).T, precision=highest)
-    grad_heads = jnp.dot(mixed_in.astype(f32).T, grad_logits, precision=highest)
-    grad_gain_two = jnp.sum(grad_mixed * normed_two, axis=0)
-    grad_after = grad_out + norm_back(grad_mixed * gain_second, normed_two, scale_two)
-    grad_attn = grad_after.astype(bf16)
-    d_out = product_tn(attended, grad_attn).astype(bf16)
-    grad_attended = outer_nt(grad_attn, out_full).astype(bf16)
-    grad_qkv, *scattered = attend_backward(qkv_rows, lse, grad_attended, width, scatter_wout, 6, experts)
-    if fast:
-        grad_wout = scattered[0].reshape(width, -1)
-    d_qkv = [product_tn(attn_in, grad_qkv[i]).astype(bf16) for i in range(3)]
-    grad_attn_in = sum(outer_nt(grad_qkv[i], qkv_full[:, i * width : (i + 1) * width]) for i in range(3))
-    grad_gain_one = jnp.sum(grad_attn_in * normed_one, axis=0)
-    tokens_grad = grad_after + norm_back(grad_attn_in * gain_first, normed_one, scale_one)
-    d_small = jnp.concatenate([grad_gain_one[:, None], grad_gain_two[:, None], grad_heads], axis=1)
-    d_small = jnp.pad(d_small, ((0, 0), (0, 128 - d_small.shape[1]))).astype(bf16)
-    if fast:
-        last = [d_out] + d_qkv + [jnp.pad(d_small, ((0, 0), (0, BLOCK - 128)))]
-        last = [a.reshape(4, 2, 2, experts // 2, share, a.shape[1]) for a in last]
-        (summed,) = move("scatter_last", Scatter(last, "columns", experts), 7, experts)
-        per = width // BLOCK
-        grad_wo = jnp.concatenate([summed[i] for i in range(per)], axis=1)
-        grad_wqkv = jnp.concatenate([summed[i] for i in range(per, 4 * per)], axis=1)
-        grad_small = summed[4 * per]
-    else:
-        grad_small = scatter_xla(d_small.reshape(devices, share, 128), AXES)
-        grad_wqkv = scatter_xla(jnp.concatenate(d_qkv, axis=1).reshape(devices, share, 3 * width), AXES)
-        grad_wo = scatter_xla(d_out.reshape(devices, share, width), AXES)
+        grad_win = scatter_xla(d_win, "node")[None]
+        grad_wout = scatter_xla(d_wout, "node").T[None]
     return (
-        mixed.astype(bf16),
+        mixed,
         tokens_grad,
         grad_small[:, 0],
         grad_wqkv,
@@ -874,8 +1101,8 @@
         grad_proj,
         grad_small[:, 2 : 2 + experts],
         grad_small[:, 2 + experts : 4 + experts],
-        grad_win[None],
-        grad_wout.T[None],
+        grad_win,
+        grad_wout,
     )
 
 

time: 572 us -> 503 us (0.88); the launches traced: 564 us -> 503 us
  matrix products: 35.4 us -> 0 us
  local copies, waits for them, and re-layouts: 44.4 us -> 19.8 us
  other arithmetic: 15.8 us -> 0.72 us
  Pallas kernels: 451 us -> 459 us
  waiting for transfers between devices: 5.72 us -> 12.3 us
    dot_general x11 -> x0, matrix products: 35.4 us -> none  [the longest x9 29.1 us: contract(): lax.dot_general(left_op, right_op, (((left_dim,), (right_dim,)), ((), ())...]
    slice x6 -> x0, local copies, waits for them, and re-layouts: 11 us -> none  [the longest x2 4.91 us: exchange(): moved = [parts[0]]]
    pallas_call x6 -> x5, Pallas kernels: 451 us -> 459 us  [call(): pl.pallas_call(kernel, grid=(total,), out_shape=list(outs) + join('outs')...]
    ppermute x6, waiting for transfers between devices: 5.72 us -> 12.3 us  [exchange(): moved.append(lax.ppermute(parts[j], 'expert', shift))]
    add x2 -> x0, other arithmetic: 5.88 us -> none  [the longest x1 3.75 us: shards(): grad_after + norm_back(grad_attn_in * gain_first, normed_one, scale_one)]
    unnamed x51 -> x37, local copies, waits for them, and re-layouts: 18 us -> 14.4 us
  transfers between devices with their start and end apart: 6 -> 6, of which waited for: 1 -> 1; matrix products, arithmetic and copies ran while one was open for 2% -> 0% of each run, Pallas kernels for 23% -> 26%
where the time goes in v4:
time: 503 us
  Pallas kernels  459 us (91%)
  local copies, waits for them, and re-layouts  19.8 us (4%)
  waiting for transfers between devices  12.3 us (2%)
  starting transfers between devices  9.86 us (2%)
    pallas_call x5, Pallas kernels, call(): pl.pallas_call(kernel, grid=(total,), out_shape=list(outs) + join('outs')...  459 us
    unnamed x37, local copies, waits for them, and re-layouts  14.4 us
    ppermute x6, waiting for transfers between devices, exchange(): moved.append(lax.ppermute(parts[j], 'expert', shift))  12.3 us
  transfers between devices with their start and end apart: 6, of which 1 were waited for; matrix products, arithmetic and copies ran while one was open for 0% of the time, Pallas kernels for 26%

profile of v4, /device:TPU:0, one launch (start us, length us, event | category | flops | bytes accessed | tf_op | source)
XLA Modules:
  0.0 502.5 jit_solution(13011724289301432483)
XLA Ops:
  0.6 0.7 pad_maximum_fusion
  1.5 1.5 copy.47.refs_2_
  3.0 1.5 copy.48.refs_3_
  5.1 128.8 %front.1 = (bf16[512,3072]{1,0:T(8,128)(2,1)}, f32[8,2,512]{2,1,0:T(2,128)}, bf16[512,1024]{1,0:T(8,128)(2,1)}, f32[512,1024]{1,0:T(8,128)}, bf16[512,1024]{1,0:...) custom-call(bf16[512,1024]{1,0:T(8,128)(2,1)} %refs_0_.3, ...), custom_call_target="tpu_custom_call" | custom-call | flops 6442450944 | bytes 33554432 | tf_op jit(solution)/shard_map/front/pallas_call | solution.py:411
  133.9 3.9 collective-permute-start
  137.8 1.8 collective-permute-start.1
  140.2 89.5 %dense_mlp.1 = (f32[512,1024]{1,0:T(8,128)}, f32[512,1024]{1,0:T(8,128)}, bf16[32,1024,128]{2,1,0:T(8,128)(2,1)}, bf16[32,1024,128]{2,1,0:T(8,128)(2,1)}, bf16[8...) custom-call(bf16[512,1024]{1,0:T(8,128)(2,1)} %get-tuple-element.52.refs_0_.refs_7_, ...), custom_call_target="tpu_custom_call" | custom-call | flops 25769803776 | bytes 33554432 | tf_op jit(solution)/shard_map/dense_mlp/pallas_call | solution.py:411
  229.8 0.8 copy-done.10
  231.1 93.3 %expert_mlp.1 = (bf16[160,2048]{1,0:T(8,128)(2,1)}, bf16[160,2048]{1,0:T(8,128)(2,1)}, bf16[160,2048]{1,0:T(8,128)(2,1)}, bf16[160,2048]{1,0:T(8,128)(2,1)}, bf1...) custom-call(bf16[160,2048]{1,0:T(8,128)(2,1)} %get-tuple-element.64.refs_0, ...), custom_call_target="tpu_custom_call" | custom-call | flops 32212254720 | bytes 33554432 | tf_op jit(solution)/shard_map/expert_mlp/pallas_call | solution.py:411
  324.3 2.9 collective-permute-start.3
  327.9 42.6 %scatter_win.1 = f32[1,1024,512]{2,1,0:T(8,128)} custom-call(bf16[4,2,8,2,64,512]{5,4,3,2,1,0:T(8,128)(2,1)} %bitcast.11), custom_call_target="tpu_custom_call" | custom-call | bytes 33554432 | tf_op jit(solution)/shard_map/scatter_win/pallas_call | solution.py:411
  370.5 12.3 %collective-permute-done.4.refs_18_ = bf16[160,2048]{1,0:T(8,128)(2,1)S(1)} collective-permute-done((bf16[160,2048]{1,0:T(8,128)(2,1)}, bf16[160,2048]{1,0:T(8,128)(2,1)S(1)}, u32[]{:S(2)}, u32[]{:S(2)}) %collective-permute-start.4) | collective-permute-done | bytes 655392 | tf_op jit(solution)/shard_map/ppermute | solution.py:980
  382.8 0.8 copy-done.8
  383.9 104.9 %back.1 = (bf16[512,1024]{1,0:T(8,128)(2,1)}, f32[512,1024]{1,0:T(8,128)}, f32[1,512,1024]{2,1,0:T(8,128)}, f32[32,3072]{1,0:T(8,128)}, f32[32,1024]{1,0:T(8,128)}, /*index=5*/f32[32,128]{1,0:T(8,128)}) custom-call(bf16[512,1024]{1,0:T(8,128)(2,1)} %refs_0_.3, bf16[512,1024]{1,0:T(8,128)(2,1)} %refs_1_.3, s32[512,1]{1,0:T(8,128)} %copy.47.refs_2_, ...), custom_call_target="tpu_custom_call" | custom-call | flops 17179869184 | bytes 33554432 | tf_op jit(solution)/shard_map/back/pallas_call | solution.py:411
  488.8 1.6 slice_reduce_fusion
  490.3 0.8 slice.14
  491.1 0.8 slice.15
  493.2 2.3 copy.59
  495.6 1.3 copy.60
  496.9 0.7 copy.61
  498.3 0.8 copy.63
  499.1 0.8 copy.64
  499.9 1.3 copy.65
  501.2 1.3 copy.66
  (37 shorter events, 4.6 us)
Async XLA Ops:
  133.9 95.8 %collective-permute-start = (bf16[160,2048]{1,0:T(8,128)(2,1)}, bf16[160,2048]{1,0:T(8,128)(2,1)S(1)}, u32[]{:S(2)}, u32[]{:S(2)}) collective-permute-start(bf16[160,2048]{1,0:T(8,128)(2,1)} %get-tuple-element.65), channel_id=1, source_target_pairs={{0,1},{1,2},{2,3},{3,0},{4,5},{5,6},{6,7},{7,4},{8,9},{9,10},{10,1... | collective-permute-start | bytes 1966088 | tf_op jit(solution)/shard_map/ppermute | solution.py:980
  137.8 92.0 %collective-permute-start.1 = (bf16[160,2048]{1,0:T(8,128)(2,1)}, bf16[160,2048]{1,0:T(8,128)(2,1)S(1)}, u32[]{:S(2)}, u32[]{:S(2)}) collective-permute-start(bf16[160,2048]{1,0:T(8,128)(2,1)} %get-tuple-element.66), channel_id=1, source_target_pairs={{0,2},{1,3},{2,0},{3,1},{4,6},{5,7},{6,4},{7,5},{8,10},{9,11},{10,... | collective-permute-start | bytes 1966088 | tf_op jit(solution)/shard_map/ppermute | solution.py:980
  139.6 90.2 %collective-permute-start.2 = (bf16[160,2048]{1,0:T(8,128)(2,1)}, bf16[160,2048]{1,0:T(8,128)(2,1)S(1)}, u32[]{:S(2)}, u32[]{:S(2)}) collective-permute-start(bf16[160,2048]{1,0:T(8,128)(2,1)} %get-tuple-element.67), channel_id=1, source_target_pairs={{0,3},{1,0},{2,1},{3,2},{4,7},{5,4},{6,5},{7,6},{8,11},{9,8},{10,9... | collective-permute-start | bytes 1966088 | tf_op jit(solution)/shard_map/ppermute | solution.py:980
  229.8 0.8 copy-start.10
  229.8 1.0 copy-start.11
  229.8 1.2 copy-start.12
  324.3 46.2 %collective-permute-start.3 = (bf16[160,2048]{1,0:T(8,128)(2,1)}, bf16[160,2048]{1,0:T(8,128)(2,1)S(1)}, u32[]{:S(2)}, u32[]{:S(2)}) collective-permute-start(bf16[160,2048]{1,0:T(8,128)(2,1)} %get-tuple-element.73), channel_id=1, source_target_pairs={{0,3},{1,0},{2,1},{3,2},{4,7},{5,4},{6,5},{7,6},{8,11},{9,8},{10,9... | collective-permute-start | bytes 1966088 | tf_op jit(solution)/shard_map/ppermute | solution.py:980
  327.3 55.6 %collective-permute-start.4 = (bf16[160,2048]{1,0:T(8,128)(2,1)}, bf16[160,2048]{1,0:T(8,128)(2,1)S(1)}, u32[]{:S(2)}, u32[]{:S(2)}) collective-permute-start(bf16[160,2048]{1,0:T(8,128)(2,1)} %get-tuple-element.74), channel_id=1, source_target_pairs={{0,2},{1,3},{2,0},{3,1},{4,6},{5,7},{6,4},{7,5},{8,10},{9,11},{10,... | collective-permute-start | bytes 1966088 | tf_op jit(solution)/shard_map/ppermute | solution.py:980
  327.3 55.6 %collective-permute-start.5 = (bf16[160,2048]{1,0:T(8,128)(2,1)}, bf16[160,2048]{1,0:T(8,128)(2,1)S(1)}, u32[]{:S(2)}, u32[]{:S(2)}) collective-permute-start(bf16[160,2048]{1,0:T(8,128)(2,1)} %get-tuple-element.75), channel_id=1, source_target_pairs={{0,1},{1,2},{2,3},{3,0},{4,5},{5,6},{6,7},{7,4},{8,9},{9,10},{10,1... | collective-permute-start | bytes 1966088 | tf_op jit(solution)/shard_map/ppermute | solution.py:980
  370.5 12.3 %copy-start.7 = (bf16[160,2048]{1,0:T(8,128)(2,1)}, bf16[160,2048]{1,0:T(8,128)(2,1)S(1)}, u32[]{:S(2)}) copy-start(bf16[160,2048]{1,0:T(8,128)(2,1)S(1)} %collective-permute-done.3.refs_17_) | copy-start | bytes 1966084
  382.8 0.8 copy-start.8
  382.8 1.0 copy-start.9
  488.7 6.8 %copy-start.2 = (f32[512,1024]{1,0:T(8,128)S(1)}, f32[512,1024]{1,0:T(8,128)}, u32[]{:S(2)}) copy-start(f32[512,1024]{1,0:T(8,128)} %get-tuple-element.137) | copy-start | bytes 6291460
  493.2 3.7 copy-start.5
  493.2 4.4 copy-start.6
  493.2 5.1 %copy-start.4 = (f32[32,4096]{1,0:T(8,128)S(1)}, f32[32,4096]{1,0:T(8,128)}, u32[]{:S(2)}) copy-start(f32[32,4096]{1,0:T(8,128)} %get-tuple-element.142) | copy-start | bytes 1572868
  495.6 3.5 copy-start.3
  495.6 4.3 copy-start
  498.3 2.9 copy-start.1

commit v5 on v4

--- a/solution.py
+++ b/solution.py
@@ -79,8 +79,6 @@
 
 
 class Gather:
-    late = 4
-
     def __init__(self, args, dense, items, nodes, experts):
         self.args, self.dense, self.items, self.experts = args, dense, items, experts
         self.outs = [
@@ -95,8 +93,9 @@
             pltpu.SemaphoreType.DMA((m, experts + 7)),
             pltpu.SemaphoreType.DMA((m,)),
         ]
-        self.turns = len(items) + self.late
         self.along_z = any(dense)
+        self.steps = [self.along, self.across, self.corner, self.over, self.end][0 if self.along_z else 1 :]
+        self.turns = len(items) + len(self.steps) - 1
 
     def bind(self, ins, outs, scratch, place):
         experts = self.experts
@@ -152,15 +151,17 @@
             self.bound[turn].append((local, z, xy, diag, core))
 
     def turn(self, now):
-        steps = (self.along, self.across, self.corner, self.over, self.end)
         for t in range(self.turns):
 
             @when(now == t)
             def _(t=t):
-                for late, step in enumerate(steps):
+                for late, step in enumerate(self.steps):
                     if 0 <= t - late < len(self.items):
                         for piece in self.bound[t - late]:
                             step(*piece)
+
+    def finish(self, now):
+        pass
 
     def along(self, local, z, xy, diag, core):
         local.start()
@@ -168,9 +169,12 @@
             copy.start()
 
     def across(self, local, z, xy, diag, core):
+        if not self.along_z:
+            local.start()
         for copy in z:
             copy.wait()
-        local.wait()
+        if self.along_z:
+            local.wait()
         xy[0].start()
         xy[1].start()
         core[0].start()
@@ -187,78 +191,128 @@
         core[3].start()
 
     def end(self, local, z, xy, diag, core):
+        if not self.along_z:
+            local.wait()
         for copy in core:
             copy.wait()
 
 
+class Exchange:
+    along_z = True
+
+    def __init__(self, pieces, sign, experts, start, turns, shape):
+        self.args, self.sign, self.experts, self.start, self.turns = list(pieces), sign, experts, start, turns
+        self.given = None
+        self.outs = [jax.ShapeDtypeStruct(shape, bf16)] * (experts - 1)
+        hbm = pl.BlockSpec(memory_space=pltpu.HBM)
+        self.in_specs, self.out_specs = [hbm] * len(self.args), [hbm] * (experts - 1)
+        self.scratch = [pltpu.SemaphoreType.DMA((experts,)), pltpu.SemaphoreType.DMA((experts,))]
+
+    def bind(self, ins, outs, scratch, place):
+        self.out, self.sems, self.place = outs, scratch, place
+        if ins:
+            self.sources = ins
+
+    def copies(self):
+        return [
+            pltpu.make_async_remote_copy(
+                src_ref=source,
+                dst_ref=self.out[j],
+                send_sem=self.sems[0].at[j],
+                recv_sem=self.sems[1].at[j],
+                device_id=self.place.z((self.sign * (j + 1)) % self.experts),
+                device_id_type=MESH,
+            )
+            for j, source in enumerate(self.sources)
+        ]
+
+    def send(self):
+        for copy in self.copies():
+            copy.start()
+
+    def turn(self, now):
+        if self.start is not None:
+
+            @when(now == self.start)
+            def _():
+                self.send()
+
+    def finish(self, now):
+        @when(now == self.turns - 1)
+        def _():
+            for copy in self.copies():
+                copy.wait()
+
+
 class Scatter:
-    RING = 4
-
-    def __init__(self, arrays, layout, experts, outs, store, start=0, stride=1, made=None):
-        self.layout, self.experts, self.outs, self.store = layout, experts, outs, store
-        self.start, self.stride = start, stride
-        self.args = [] if layout == "made" else arrays
-        dense = self.dense = layout != "plane"
-        if layout == "plane":
-            counts, h = [a.shape[2] for a in arrays], arrays[0].shape[4:]
-        elif layout == "rows":
-            counts, h = [a.shape[4] for a in arrays], arrays[0].shape[3:4] + arrays[0].shape[5:]
-        else:
-            counts, h = [made[0]], made[4:]
-        self.starts = [sum(counts[:a]) for a in range(len(counts) + 1)]
-        m = self.m = sum(counts)
-        unit = h[1:] if dense else (2,) + h
+    RING = 6
+    CORE_RING = 4
+
+    def __init__(self, parts, half, experts, outs, store, start=0, made=None, z_late=4):
+        self.experts, self.outs, self.store, self.start, self.made = experts, outs, store, start, made
+        self.parts = parts
+        self.given = []
+        self.args = [p[0] for p in parts if p[0] is not None]
+        h = half
+        self.starts = [sum(p[3] for p in parts[:a]) for a in range(len(parts) + 1)]
+        m = self.m = self.starts[-1]
+        self.m_z = sum(p[3] for p in parts if p[1])
+        unit = h[1:]
         ring = self.ring = min(self.RING, m)
+        self.core_ring = min(self.CORE_RING, m)
         self.in_specs = [pl.BlockSpec(memory_space=pltpu.HBM)] * len(self.args)
         self.out_specs = [pl.BlockSpec(memory_space=pltpu.VMEM)] * len(outs)
         kinds = 7 + experts
         self.scratch = [
-            pltpu.VMEM(made or (m, 4, 2) + h, bf16),
-            pltpu.VMEM((ring, 4, 2) + h, bf16),
-            pltpu.VMEM((m, 2) + h, bf16),
-            pltpu.VMEM((m, 2) + h, bf16),
-            pltpu.VMEM((m,) + h, bf16),
-            pltpu.VMEM((m,) + h, bf16),
+            pltpu.VMEM(made or (ring, 4, 2) + h, bf16),
+            pltpu.VMEM((self.core_ring, 4, 2) + h, bf16),
+            pltpu.VMEM((ring, 2) + h, bf16),
+            pltpu.VMEM((ring, 2) + h, bf16),
+            pltpu.VMEM((ring,) + h, bf16),
+            pltpu.VMEM((ring,) + h, bf16),
             pltpu.SemaphoreType.DMA((m, kinds)),
             pltpu.SemaphoreType.DMA((m, kinds)),
             pltpu.SemaphoreType.DMA((m,)),
         ]
-        if dense:
-            self.scratch.append(pltpu.VMEM((m, experts - 1) + unit, bf16))
-        self.late = 4 if dense else 3
-        self.turns = start + (m - 1) * stride + 1 + self.late
-        self.along_z = dense
+        if self.m_z:
+            self.scratch.append(pltpu.VMEM((self.m_z, experts - 1) + unit, bf16))
+            self.scratch.append(pltpu.VMEM((self.m_z, experts) + unit, bf16))
+        self.z_late = z_late
+        self.turns = start + max(m + 3, self.m_z + z_late)
+        self.along_z = self.m_z > 0
 
     def bind(self, ins, outs, scratch, place):
-        self.ins, self.out, self.place = ins, outs, place
-        self.own, self.rc, self.rx, self.ry, self.lx, self.ly, self.send, self.recv, self.loc = scratch[:9]
-        self.rz = scratch[9] if self.dense else None
+        ins = list(ins)
+        given = list(self.given)
+        self.sources = [given.pop(0) if p[0] is None else ins.pop(0) for p in self.parts] if not self.made else []
+        self.out, self.place = outs, place
+        self.own, self.rc, self.rx, self.ry, self.lx, self.ly, self.sent, self.recv, self.loc = scratch[:9]
+        self.rz, self.zs = scratch[9:] if self.m_z else (None, None)
+
+    def slot(self, i):
+        return lax.rem(i, self.ring)
 
     def remote(self, source, target, item, kind, device):
         return pltpu.make_async_remote_copy(
             src_ref=source,
             dst_ref=target,
-            send_sem=self.send.at[item, kind],
+            send_sem=self.sent.at[item, kind],
             recv_sem=self.recv.at[item, kind],
             device_id=device,
             device_id_type=MESH,
         )
 
-    def part(self, source, core, chunk):
-        if self.layout == "plane":
-            return source.at[:, core, chunk]
-        return source.at[:, core, :, :, chunk]
-
     def at(self, i, site, *more):
-        return (i, site, self.place.k) + more if self.layout == "made" else (i, site) + more
+        return (i, site, self.place.k) + more if self.made else (self.slot(i), site) + more
 
     def first(self, source, i, chunk):
         p = self.place
-        land = self.rc.at[lax.rem(i, self.ring)]
-        if self.layout == "made":
+        land = self.rc.at[lax.rem(i, self.core_ring)]
+        if self.made:
             return [self.remote(self.own.at[i, :, 1 - p.k], land, i, 0, (p.nc, p.e))]
-        local = pltpu.make_async_copy(self.part(source, p.k, chunk), self.own.at[i], self.loc.at[i])
-        return [self.remote(self.part(source, 1 - p.k, chunk), land, i, 0, (p.nc, p.e)), local]
+        part = lambda core: source.at[:, core, :, :, chunk]
+        local = pltpu.make_async_copy(part(p.k), self.own.at[self.slot(i)], self.loc.at[i])
+        return [self.remote(part(1 - p.k), land, i, 0, (p.nc, p.e)), local]
 
     def sites(self):
         p = self.place
@@ -266,65 +320,64 @@
 
     def round_one(self, i):
         p = self.place
+        b = self.slot(i)
         _, to_x, to_y, diag = self.sites()
         own = lambda *at: self.own.at[self.at(i, *at)]
         return [
-            self.remote(own(diag, 0), self.rx.at[i, 0], i, 1, (p.nx, p.e)),
-            self.remote(own(diag, 1), self.ry.at[i, 0], i, 2, (p.ny, p.e)),
-            self.remote(own(to_x, 0), self.rx.at[i, 1], i, 3, (p.nx, p.e)),
-            self.remote(own(to_y, 1), self.ry.at[i, 1], i, 4, (p.ny, p.e)),
+            self.remote(own(diag, 0), self.rx.at[b, 0], i, 1, (p.nx, p.e)),
+            self.remote(own(diag, 1), self.ry.at[b, 0], i, 2, (p.ny, p.e)),
+            self.remote(own(to_x, 0), self.rx.at[b, 1], i, 3, (p.nx, p.e)),
+            self.remote(own(to_y, 1), self.ry.at[b, 1], i, 4, (p.ny, p.e)),
         ]
 
     def round_two(self, i):
         p = self.place
+        b = self.slot(i)
         _, to_x, to_y, _ = self.sites()
         return [
-            self.remote(self.own.at[self.at(i, to_x, 1)], self.lx.at[i], i, 5, (p.nx, p.e)),
-            self.remote(self.own.at[self.at(i, to_y, 0)], self.ly.at[i], i, 6, (p.ny, p.e)),
+            self.remote(self.own.at[self.at(i, to_x, 1)], self.lx.at[b], i, 5, (p.nx, p.e)),
+            self.remote(self.own.at[self.at(i, to_y, 0)], self.ly.at[b], i, 6, (p.ny, p.e)),
         ]
 
     def round_z(self, i):
         p = self.place
-        mine, _, _, _ = self.sites()
-        s = self.experts // 2
-        copies = []
-        for j in range(1, self.experts):
-            to = lax.rem(p.e + j, self.experts)
-            source = self.own.at[self.at(i, mine, to // s, lax.rem(to, s))]
-            copies.append(self.remote(source, self.rz.at[i, j - 1], i, 6 + j, p.z(j)))
-        return copies
+        return [
+            self.remote(self.zs.at[i, lax.rem(p.e + j, self.experts)], self.rz.at[i, j - 1], i, 6 + j, p.z(j))
+            for j in range(1, self.experts)
+        ]
 
     def turn(self, now):
+        limits = (self.m, self.m, self.m, self.m, self.m_z)
         steps = (self.load, self.chip, self.cross, self.plane, self.column)
-        for late, step in enumerate(steps[: self.late + 1]):
-            since = now - self.start - late
-            i = since // self.stride
-            due = jnp.logical_and(since >= 0, i < self.m)
-            if self.stride > 1:
-                due = jnp.logical_and(due, lax.rem(since, self.stride) == 0)
-
-            @when(due)
-            def _(step=step, i=i):
-                step(i)
+        for limit, late, step in zip(limits, (0, 1, 2, 3, self.z_late), steps):
+            i = now - self.start - late
+            if limit:
+
+                @when(jnp.logical_and(i >= 0, i < limit))
+                def _(step=step, i=i):
+                    step(i)
+
+    def finish(self, now):
+        pass
 
     def load(self, i):
-        if self.layout == "made":
+        if self.made:
             self.first(None, i, 0)[0].start()
             return
-        for a, source in enumerate(self.ins):
+        for a, source in enumerate(self.sources):
 
             @when(jnp.logical_and(i >= self.starts[a], i < self.starts[a + 1]))
             def _(a=a, source=source):
-                for copy in self.first(source, i, i - self.starts[a]):
+                for copy in self.first(source, i, i - self.starts[a] + self.parts[a][2]):
                     copy.start()
 
     def chip(self, i):
-        for copy in self.first(None if self.layout == "made" else self.ins[0], i, 0):
+        for copy in self.first(None if self.made else self.sources[0], i, 0):
             copy.wait()
 
         def sum_one(q, _):
             at = self.at(i, q)
-            self.own[at] = add(self.own[at], self.rc[lax.rem(i, self.ring), q]).astype(bf16)
+            self.own[at] = add(self.own[at], self.rc[lax.rem(i, self.core_ring), q]).astype(bf16)
             return 0
 
         lax.fori_loop(0, 4, sum_one, 0)
@@ -334,46 +387,55 @@
     def cross(self, i):
         one = self.round_one(i)
         two = self.round_two(i)
+        b = self.slot(i)
         _, to_x, to_y, _ = self.sites()
         for copy in one:
             copy.wait()
         at_x, at_y = self.at(i, to_x, 1), self.at(i, to_y, 0)
-        self.own[at_x] = add(self.own[at_x], self.ry[i, 0]).astype(bf16)
+        self.own[at_x] = add(self.own[at_x], self.ry[b, 0]).astype(bf16)
         two[0].start()
-        self.own[at_y] = add(self.own[at_y], self.rx[i, 0]).astype(bf16)
+        self.own[at_y] = add(self.own[at_y], self.rx[b, 0]).astype(bf16)
         two[1].start()
 
     def plane(self, i):
         for copy in self.round_two(i):
             copy.wait()
         mine, _, _, _ = self.sites()
-        sums = (
-            add(self.own[self.at(i, mine, 0)], self.rx[i, 1], self.ly[i]),
-            add(self.own[self.at(i, mine, 1)], self.lx[i], self.ry[i, 1]),
+        b = self.slot(i)
+        sums = lambda: (
+            add(self.own[self.at(i, mine, 0)], self.rx[b, 1], self.ly[b]),
+            add(self.own[self.at(i, mine, 1)], self.lx[b], self.ry[b, 1]),
         )
-        if not self.dense:
-            self.store(self.out, i, jnp.concatenate(sums, axis=0))
-            return
-        for h in range(2):
-            self.own[self.at(i, mine, h)] = sums[h].astype(bf16)
-        for copy in self.round_z(i):
-            copy.start()
+        if self.m_z:
+
+            @when(i < self.m_z)
+            def _():
+                s = self.experts // 2
+                for h, total in enumerate(sums()):
+                    self.zs[i, h * s : (h + 1) * s] = total.astype(bf16)
+                for copy in self.round_z(i):
+                    copy.start()
+
+        if self.m_z < self.m:
+
+            @when(i >= self.m_z)
+            def _():
+                self.store(self.out, i, sums())
 
     def column(self, i):
         for copy in self.round_z(i):
             copy.wait()
-        p = self.place
-        mine, _, _, _ = self.sites()
-        s = self.experts // 2
-        terms = [self.own[self.at(i, mine, p.e // s, lax.rem(p.e, s))]]
-        self.store(self.out, i, add(*terms, *(self.rz[i, j] for j in range(self.experts - 1))))
+        terms = [self.zs[i, self.place.e]] + [self.rz[i, j] for j in range(self.experts - 1)]
+        self.store(self.out, i, add(*terms))
 
 
 def add(*terms):
     return functools.reduce(jnp.add, [t.astype(f32) for t in terms])
 
 
-def call(name, steps, body, args, in_specs, outs, out_specs, scratch, moves, collective_id, experts, flops):
+def call(
+    name, steps, body, args, in_specs, outs, out_specs, scratch, moves, collective_id, experts, flops, given=None
+):
     total = max([steps] + [m.turns for m in moves])
 
     def hold(spec):
@@ -393,6 +455,8 @@
         now = pl.program_id(0)
         if moves:
             place = Place(experts)
+            if given is not None:
+                given(ins, os, own)
             for m, a, o, r in zip(moves, m_ins, m_os, m_own):
                 m.bind(a, o, r, place)
 
@@ -408,7 +472,10 @@
             def _():
                 body(now, steps, *ins, *os, *own)
 
-    return pl.pallas_call(
+        for m in moves:
+            m.finish(now)
+
+    results = pl.pallas_call(
         kernel,
         grid=(total,),
         out_shape=list(outs) + join("outs"),
@@ -422,6 +489,7 @@
         ),
         name=name,
     )(*args, *join("args"))
+    return list(results)
 
 
 def masks():
@@ -455,6 +523,11 @@
         outs.append(jnp.concatenate(row, axis=1))
         tops.append(jnp.concatenate(logs, axis=1))
     return jnp.concatenate(outs, axis=0).T.astype(bf16), jnp.concatenate(tops, axis=0)
+
+
+def columns_of(code):
+    length = code.shape[1]
+    return [jnp.broadcast_to(code[i : i + 1], (128, length)).T.astype(jnp.int32) for i in range(2)]
 
 
 class Front:
@@ -488,7 +561,7 @@
             pltpu.SemaphoreType.DMA((3,)),
         ]
 
-    def __call__(self, now, steps, tok, cot, route, drop, *refs):
+    def __call__(self, now, steps, tok, cot, code, *refs):
         full = self.moves.full[:3] if self.moves else refs[:3]
         refs = refs if self.moves else refs[3:]
         qkv, lse, att, after, mixed, gd, disp, info = refs[:8]
@@ -538,10 +611,11 @@
         def _():
             loads[2].start()
             loads[2].wait()
-            self.route(tok, cot, route, drop, att, wo, ws, gains, after, mixed, gd, disp, info, leave)
-
-    def route(self, tok, cot, route, drop, att, wo, ws, gains, after, mixed, gd, disp, info, leave):
+            self.route(tok, cot, code, att, wo, ws, gains, after, mixed, gd, disp, info, leave)
+
+    def route(self, tok, cot, code, att, wo, ws, gains, after, mixed, gd, disp, info, leave):
         width, length, experts = self.width, self.length, self.experts
+        route, drop = columns_of(code)
         after[...] = tok[...].astype(f32) + matmul(att[...], wo[...].reshape(width, width))
         normed, _ = normalize(after[...])
         mixed[...] = (normed * gains[1:2]).astype(bf16)
@@ -556,9 +630,9 @@
 
         probs, coef = softmax(2, 2 + experts), softmax(2 + experts, 4 + experts)
         info[...] = probs + coef
-        chosen = jnp.where(lane - 2 == route[...], 1.0, 0.0)
+        chosen = jnp.where(lane - 2 == route, 1.0, 0.0)
         over_lanes = lambda a: jnp.sum(a, axis=1, keepdims=True)
-        gate = over_lanes(probs * chosen) * (1 - drop[...]).astype(f32)
+        gate = over_lanes(probs * chosen) * (1 - drop[:, :1]).astype(f32)
         coef_0 = over_lanes(jnp.where(lane == 2 + experts, coef, 0.0))
         coef_1 = over_lanes(jnp.where(lane == 3 + experts, coef, 0.0))
         grad = cot[...].astype(f32)
@@ -566,7 +640,7 @@
         square = lambda d: lax.broadcasted_iota(jnp.int32, (length, length), d)
         earlier = jnp.where(square(0) > square(1), 1.0, 0.0).astype(bf16)
         position = over_lanes(chosen * matmul(earlier, chosen.astype(bf16))).astype(jnp.int32)
-        turn = route[...] - lax.axis_index("expert")
+        turn = route[:, :1] - lax.axis_index("expert")
         target = jnp.where(turn < 0, turn + experts, turn) * self.capacity + position
         slot = lax.broadcasted_iota(jnp.int32, (length, experts * self.capacity), 1)
         disp[...] = jnp.where(slot == target, 1.0, 0.0).astype(bf16)
@@ -619,18 +693,15 @@
 
 
 class Back:
-    GROUP = 2
-
     def __init__(self, length, width, experts, devices, capacity):
         self.length, self.width, self.experts, self.capacity = length, width, experts, capacity
         self.devices, self.share = devices, width // devices
         self.pairs = width // PAIR
-        self.groups = self.pairs // self.GROUP
-        self.part = self.GROUP * PAIR
-        self.columns = 3 * self.part
-        self.rest = width - self.columns
-        self.items = self.groups + 2
-        self.heads_at = 3
+        self.columns = 3 * PAIR
+        self.firsts = width // self.columns
+        self.rest = width - self.firsts * self.columns
+        self.items = self.firsts + self.pairs + 1
+        self.heads_at = 4
         self.last = self.heads_at + self.pairs
         self.steps = self.last + 1
         self.first_item = self.heads_at
@@ -650,7 +721,6 @@
             pltpu.VMEM((128, width), f32),
             pltpu.VMEM((width, length), bf16),
             pltpu.VMEM((length, width), bf16),
-            pltpu.VMEM((length, self.columns), bf16),
             pltpu.SemaphoreType.DMA((5 + experts,)),
             pltpu.SemaphoreType.DMA((2, 3)),
         ]
@@ -665,35 +735,37 @@
 
     def store(self, outs, i, value):
         d_qkv, d_out, d_small = outs
-        part = self.part
-
-        @when(i == 0)
-        def _():
-            d_out[:, : self.columns] = value
-
-        @when(jnp.logical_and(i > 0, i <= self.groups))
+        final = self.items - 1
+
+        for f in range(self.firsts):
+
+            @when(i == f)
+            def _(f=f):
+                d_out[:, f * self.columns : (f + 1) * self.columns] = value
+
+        @when(jnp.logical_and(i >= self.firsts, i < final))
         def _():
             for p in range(3):
-                at = pl.multiple_of(p * self.width + (i - 1) * part, part)
-                d_qkv[:, pl.ds(at, part)] = value[:, p * part : (p + 1) * part]
-
-        @when(i == self.groups + 1)
-        def _():
-            d_out[:, self.columns :] = value[:, : self.rest]
+                at = pl.multiple_of(p * self.width + (i - self.firsts) * PAIR, PAIR)
+                d_qkv[:, pl.ds(at, PAIR)] = value[:, p * PAIR : (p + 1) * PAIR]
+
+        @when(i == final)
+        def _():
+            d_out[:, self.firsts * self.columns :] = value[:, : self.rest]
             d_small[...] = value[:, self.rest : self.rest + 128]
 
     def __call__(self, now, steps, *refs):
         experts, width, length = self.experts, self.width, self.length
         refs = list(refs)
-        tok, cot, route, drop, qkv, lse, att, mixed_in, disp, info = refs[:10]
-        small_hbm, qkv_hbm, out_hbm, dense_hbm, grad_hbm, after_hbm = refs[10:16]
-        came_hbm = refs[16 : 16 + experts]
-        mixed, tokens_grad, *rest = refs[16 + experts :]
+        tok, cot, code, qkv, lse, att, mixed_in, disp, info = refs[:9]
+        small_hbm, qkv_hbm, out_hbm, dense_hbm, grad_hbm, after_hbm = refs[9:15]
+        came_hbm = refs[15 : 15 + experts]
+        mixed, tokens_grad, *rest = refs[15 + experts :]
         if self.moves:
             made = self.moves[-1].own
         else:
             made = rest.pop(0)
-        came, dense, grads, ws, wo, wq, gains, d_heads, attn_in_t, grad_att, d_group, sems, wq_sems = rest
+        came, dense, grads, ws, wo, wq, gains, d_heads, attn_in_t, grad_att, sems, wq_sems = rest
         fetch = lambda a, b, i: pltpu.make_async_copy(a, b, sems.at[i])
         capacity = self.capacity
         loads = [fetch(came_hbm[j], came.at[pl.ds(j * capacity, capacity)], j) for j in range(experts)]
@@ -704,12 +776,12 @@
             )
         ]
 
-        def group_weights(group):
-            slot = lax.rem(group, 2)
+        def pair_weights(pair):
+            slot = lax.rem(pair, 2)
             return [
                 pltpu.make_async_copy(
-                    qkv_hbm.at[:, :, pl.ds(pl.multiple_of(p * width + group * self.part, self.part), self.part)],
-                    wq.at[slot, :, :, pl.ds(p * self.part, self.part)],
+                    qkv_hbm.at[:, :, pl.ds(pl.multiple_of(p * width + pair * PAIR, PAIR), PAIR)],
+                    wq.at[slot, :, :, pl.ds(p * PAIR, PAIR)],
                     wq_sems.at[slot, p],
                 )
                 for p in range(3)
@@ -721,17 +793,19 @@
 
         @when(now == 0)
         def _():
-            for copy in loads:
+            for copy in loads + pair_weights(0):
                 copy.start()
-            for copy in group_weights(0):
-                copy.start()
+
+        @when(now == 1)
+        def _():
             for copy in loads:
                 copy.wait()
             probs = jnp.where(jnp.logical_and(lane >= 2, lane < 2 + experts), info[...], 0.0)
             coef_0 = over_lanes(jnp.where(lane == 2 + experts, info[...], 0.0))
             coef_1 = over_lanes(jnp.where(lane == 3 + experts, info[...], 0.0))
-            chosen = jnp.where(lane - 2 == route[...], 1.0, 0.0)
-            kept = (1 - drop[...]).astype(f32)
+            route, drop = columns_of(code)
+            chosen = jnp.where(lane - 2 == route, 1.0, 0.0)
+            kept = (1 - drop[:, :1]).astype(f32)
             gate_prob = over_lanes(probs * chosen)
             gate = gate_prob * kept
             grad = cot[...].astype(f32)
@@ -754,7 +828,7 @@
             )
             gains[...] = weights.astype(f32).T[:8]
 
-        @when(now == 1)
+        @when(now == 2)
         def _():
             normed, scale = normalize(tokens_grad[...])
             d_heads[1:2] = jnp.sum(grads[...] * normed, axis=0, keepdims=True)
@@ -762,50 +836,43 @@
             normed, _ = normalize(tok[...].astype(f32))
             attn_in_t[...] = (normed * gains[0:1]).astype(bf16).T
 
-        @when(now == 2)
+        @when(now == 3)
         def _():
             grad_attn = grads[...].astype(bf16)
             grad_att[...] = outer_nt(grad_attn, wo[...].reshape(width, width)).astype(bf16)
             d_out = product_tn(att[...], grad_attn).astype(bf16)
-            put(0, slice(0, self.columns), d_out[:, : self.columns])
-            put(self.groups + 1, slice(0, self.rest), d_out[:, self.columns :])
+            for f in range(self.firsts):
+                put(f, slice(None), d_out[:, f * self.columns : (f + 1) * self.columns])
+            put(self.items - 1, slice(0, self.rest), d_out[:, self.firsts * self.columns :])
             dense[...] = jnp.zeros_like(dense)
 
         @when(jnp.logical_and(now >= self.heads_at, now < self.last))
         def _():
             pair = now - self.heads_at
-            group, of_group = pair // self.GROUP, lax.rem(pair, self.GROUP)
             cols = lambda part: pl.ds(pl.multiple_of(part * width + pair * PAIR, PAIR), PAIR)
-            results = attend_pair_backward(
+            d_pair = attend_pair_backward(
                 qkv[:, cols(0)], qkv[:, cols(1)], qkv[:, cols(2)], grad_att[:, cols(0)], lse[pair]
             )
-            for p, values in enumerate(results):
-                d_group[:, pl.ds(pl.multiple_of(p * self.part + of_group * PAIR, PAIR), PAIR)] = values
-
-            @when(of_group == self.GROUP - 1)
+            d_pair = jnp.concatenate(d_pair, axis=1)
+            for copy in pair_weights(pair):
+                copy.wait()
+
+            @when(pair + 1 < self.pairs)
             def _():
-                for copy in group_weights(group):
-                    copy.wait()
-
-                @when(group + 1 < self.groups)
-                def _():
-                    for copy in group_weights(group + 1):
-                        copy.start()
-
-                put(group + 1, slice(None), matmul(attn_in_t[...], d_group[...]).astype(bf16))
-                weights = wq[lax.rem(group, 2)].reshape(width, self.columns)
-                dense[...] += outer_nt(d_group[...], weights)
+                for copy in pair_weights(pair + 1):
+                    copy.start()
+
+            put(pair + self.firsts, slice(None), matmul(attn_in_t[...], d_pair).astype(bf16))
+            dense[...] += outer_nt(d_pair, wq[lax.rem(pair, 2)].reshape(width, self.columns))
 
         @when(now == self.last)
         def _():
             normed, scale = normalize(tok[...].astype(f32))
             d_heads[0:1] = jnp.sum(dense[...] * normed, axis=0, keepdims=True)
-            put(self.groups + 1, slice(self.rest, self.rest + 128), d_heads[...].T.astype(bf16))
-            put(
-                self.groups + 1,
-                slice(self.rest + 128, self.columns),
-                jnp.zeros((width, self.columns - self.rest - 128), bf16),
-            )
+            put(self.items - 1, slice(self.rest, self.rest + 128), d_heads[...].T.astype(bf16))
+            if self.rest + 128 < self.columns:
+                spare = self.columns - self.rest - 128
+                put(self.items - 1, slice(self.rest + 128, None), jnp.zeros((width, spare), bf16))
             tokens_grad[...] = grads[...] + norm_back(dense[...] * gains[0:1], normed, scale)
 
     def put(self, made, i, columns, values):
@@ -823,39 +890,27 @@
     return v * half, slope
 
 
-def mlp_kernel(share, parts, now, steps, *refs):
-    if parts:
-        pieces, (w1_ref, w2_ref), refs = refs[:parts], refs[parts : parts + 2], refs[parts + 2 :]
-        results, (d1_ref, d2_ref) = refs[:parts], refs[parts : parts + 2]
-        x, g, xt, gt, out_sum, back_sum = refs[parts + 2 :]
-    else:
-        x, g, w1_ref, w2_ref, out_sum, back_sum, d1_ref, d2_ref, xt, gt = refs
-    width = xt.shape[0]
-
-    @when(now == 0)
-    def _():
-        if parts:
-            size = pieces[0].shape[0]
-            for j, piece in enumerate(pieces):
-                x[j * size : (j + 1) * size] = piece[:, :width]
-                g[j * size : (j + 1) * size] = piece[:, width:]
-        xt[...] = x[...].T
-        gt[...] = g[...].T
-        out_sum[...] = jnp.zeros_like(out_sum)
-        back_sum[...] = jnp.zeros_like(back_sum)
-
-    w1 = w1_ref[...].reshape(w1_ref.shape[-2:])
-    w2 = w2_ref[...].reshape(w2_ref.shape[-2:])
+def mlp_block(x, g, xt, gt, w1, w2, out_sum, back_sum):
     hidden, slope = gelu_both(matmul(x[...], w1))
     hidden = hidden.astype(bf16)
     grad_pre = (slope * outer_nt(g[...], w2)).astype(bf16)
     out_sum[...] += matmul(hidden, w2)
     back_sum[...] += outer_nt(grad_pre, w1)
-    d1 = matmul(xt[...], grad_pre).astype(bf16)
-    d2 = matmul(gt[...], hidden).astype(bf16)
+    return matmul(xt[...], grad_pre).astype(bf16), matmul(gt[...], hidden).astype(bf16)
+
+
+def mlp_kernel(share, now, steps, x, g, w1, w2, out_sum, back_sum, d1_ref, d2_ref, xt, gt):
+    @when(now == 0)
+    def _():
+        xt[...] = x[...].T
+        gt[...] = g[...].T
+        out_sum[...] = jnp.zeros_like(out_sum)
+        back_sum[...] = jnp.zeros_like(back_sum)
+
+    d1, d2 = mlp_block(x, g, xt, gt, w1[...], w2[...], out_sum, back_sum)
     if share is None:
-        d1_ref[...] = d1.reshape(d1_ref.shape)
-        d2_ref[...] = d2.reshape(d2_ref.shape)
+        d1_ref[...] = d1
+        d2_ref[...] = d2
     else:
         for c in range(d1.shape[1] // 128):
             cols = slice(c * 128, (c + 1) * 128)
@@ -863,61 +918,126 @@
                 d1_ref[s, c * share : (c + 1) * share] = d1[s * share : (s + 1) * share, cols]
             d2_ref[c] = d2[:, cols]
 
-    if parts:
-
-        @when(now == steps - 1)
-        def _():
-            for h, total in enumerate((out_sum, back_sum)):
-                for j, result in enumerate(results):
-                    rows = slice(j * result.shape[0], (j + 1) * result.shape[0])
-                    result[:, h * width : (h + 1) * width] = total[rows].astype(bf16)
-
-
-def mlp(rows_in, w1, w2, name, moves, collective_id, experts, devices=None):
+
+def mlp(x, g, w1, w2, name, moves, collective_id, experts, devices=None):
     share = None
-    if w1.ndim == 3:
-        blocks, width, size = w1.shape
-        w1_spec = pl.BlockSpec((1, width, size), lambda j: (j, 0, 0))
-        w2_spec = pl.BlockSpec((1, size, width), lambda j: (j, 0, 0))
-        d_shape, d_specs = (blocks, width, size), [w1_spec] * 2
-    else:
-        size = BLOCK
-        width = w1.shape[0]
-        blocks = w1.shape[1] // size
-        w1_spec = pl.BlockSpec((width, size), lambda j: (0, j))
-        w2_spec = pl.BlockSpec((size, width), lambda j: (j, 0))
-        d_shape, d_specs = (width, blocks * size), [w1_spec] * 2
-        if devices:
-            share = width // devices
-            d_shape = (devices, width, 128)
-            d_specs = [
-                pl.BlockSpec((devices, size // 128 * share, 128), lambda j: (0, j, 0)),
-                pl.BlockSpec((size // 128, width, 128), lambda j: (j, 0, 0)),
-            ]
+    size = BLOCK
+    rows, width = x.shape
+    blocks = w1.shape[1] // size
+    w1_spec = pl.BlockSpec((width, size), lambda j: (0, j))
+    w2_spec = pl.BlockSpec((size, width), lambda j: (j, 0))
+    d_shape, d_specs = (width, blocks * size), [w1_spec] * 2
+    if devices:
+        share = width // devices
+        d_shape = (devices, width, 128)
+        d_specs = [
+            pl.BlockSpec((devices, size // 128 * share, 128), lambda j: (0, j, 0)),
+            pl.BlockSpec((size // 128, width, 128), lambda j: (j, 0, 0)),
+        ]
     whole = pl.BlockSpec(memory_space=pltpu.VMEM)
-    joined = rows_in[0].shape[1] == 2 * width
-    parts = len(rows_in) if joined else 0
-    rows = sum(a.shape[0] for a in rows_in) if joined else rows_in[0].shape[0]
-    if joined:
-        outs = [jax.ShapeDtypeStruct(a.shape, bf16) for a in rows_in]
-    else:
-        outs = [jax.ShapeDtypeStruct((rows, width), f32)] * 2
-    flat, across = pltpu.VMEM((rows, width), bf16), pltpu.VMEM((width, rows), bf16)
-    sums = [pltpu.VMEM((rows, width), f32)] * 2
     return call(
         name,
         blocks,
-        functools.partial(mlp_kernel, share, parts),
-        list(rows_in) + [w1, w2],
-        [whole] * len(rows_in) + [w1_spec, w2_spec],
-        outs + [jax.ShapeDtypeStruct(d_shape, bf16)] * 2,
-        [whole] * len(outs) + d_specs,
-        [flat, flat, across, across] + sums if joined else [across, across],
+        functools.partial(mlp_kernel, share),
+        [x, g, w1, w2],
+        [whole] * 2 + [w1_spec, w2_spec],
+        [jax.ShapeDtypeStruct((rows, width), f32)] * 2 + [jax.ShapeDtypeStruct(d_shape, bf16)] * 2,
+        [whole] * 2 + d_specs,
+        [pltpu.VMEM((width, rows), bf16)] * 2,
         moves,
         collective_id,
         experts,
         12 * rows * width * blocks * size,
     )
+
+
+class Experts:
+    PER_STEP = 1
+
+    def __init__(self, pieces, blocks, width, size, chunks, back):
+        self.parts, self.piece = len(pieces), pieces[0].shape
+        self.blocks, self.width, self.size, self.back = blocks, width, size, back
+        rows = self.parts * self.piece[0]
+        if chunks:
+            self.block = (2, size // 256, chunks, width // chunks, 128)
+            whole = (blocks // 2, 2) + self.block
+        else:
+            self.block = (width, size)
+            whole = (blocks,) + self.block
+        piece = jax.ShapeDtypeStruct(self.piece, bf16)
+        self.outs = [piece] * self.parts + [jax.ShapeDtypeStruct(whole, bf16)] * 2
+        self.scratch = (
+            [pltpu.VMEM(self.piece, bf16)] * self.parts
+            + [pltpu.VMEM((rows, width), bf16)] * 2
+            + [pltpu.VMEM((width, rows), bf16)] * 2
+            + [pltpu.VMEM((rows, width), f32)] * 2
+            + [pltpu.VMEM((2,) + self.block, bf16)] * 2
+            + [pltpu.SemaphoreType.DMA((2, 2)), pltpu.SemaphoreType.DMA((self.parts,))]
+        )
+
+    def __call__(self, now, steps, *refs):
+        refs = list(refs)
+        take = lambda count: [refs.pop(0) for _ in range(count)]
+        pieces, (w1, w2) = take(self.parts), take(2)
+        kept, targets, results = take(self.parts), take(2), take(self.parts)
+        x, g, xt, gt, out_sum, back_sum, stage_1, stage_2, sems, kept_sems = refs
+        width, size = self.width, self.piece[0]
+
+        def flush(step):
+            at = lax.rem(step, 2)
+            where = (step // 2, at) if len(self.block) > 2 else (step,)
+            return [
+                pltpu.make_async_copy(stage.at[at], target.at[where], sems.at[at, i])
+                for i, (stage, target) in enumerate(zip((stage_1, stage_2), targets))
+            ]
+
+        @when(now == 0)
+        def _():
+            for j, piece in enumerate(pieces):
+                x[j * size : (j + 1) * size] = piece[:, :width]
+                g[j * size : (j + 1) * size] = piece[:, width:]
+            xt[...] = x[...].T
+            gt[...] = g[...].T
+            out_sum[...] = jnp.zeros_like(out_sum)
+            back_sum[...] = jnp.zeros_like(back_sum)
+
+        def block(b, _):
+            step = now * self.PER_STEP + b
+
+            @when(step >= 2)
+            def _():
+                for copy in flush(step - 2):
+                    copy.wait()
+
+            slot = lax.rem(step, 2)
+            for stage, d in zip((stage_1, stage_2), mlp_block(x, g, xt, gt, w1[b], w2[b], out_sum, back_sum)):
+                if len(self.block) == 2:
+                    stage[slot] = d
+                else:
+                    for c in range(d.shape[1] // 128):
+                        share = d[:, c * 128 : (c + 1) * 128].reshape(self.block[2:])
+                        stage[slot, c // self.block[1], c % self.block[1]] = share
+            for copy in flush(step):
+                copy.start()
+            return 0
+
+        lax.fori_loop(0, self.PER_STEP, block, 0)
+
+        @when(now == steps - 1)
+        def _():
+            for h, total in enumerate((out_sum, back_sum)):
+                for j, result in enumerate(results):
+                    result[:, h * width : (h + 1) * width] = total[j * size : (j + 1) * size].astype(bf16)
+            keep = [pltpu.make_async_copy(a, b, kept_sems.at[j]) for j, (a, b) in enumerate(zip(results, kept))]
+            for copy in keep:
+                copy.start()
+            for copy in keep:
+                copy.wait()
+            if self.back:
+                self.back.send()
+            for step in (self.blocks - 2, self.blocks - 1):
+                for copy in flush(step):
+                    copy.wait()
 
 
 def move(name, moves, collective_id, experts):
@@ -983,13 +1103,13 @@
     front = Front(tok_rows, width, experts, devices, capacity, gather_dense[0] if fast else None)
     kept = full[:3]
     whole, hbm = pl.BlockSpec(memory_space=pltpu.VMEM), pl.BlockSpec(memory_space=pltpu.HBM)
-    dropped = dropped[:, None]
+    code = jnp.stack([routes[:, 0], dropped]).astype(f32)
     results = call(
         "front",
         front.steps,
         front,
-        [tokens, cotangent, routes, dropped] + kept,
-        [whole] * 4 + [hbm] * len(kept),
+        [tokens, cotangent, code] + kept,
+        [whole] * 3 + [hbm] * len(kept),
         front.outs,
         [whole] * len(front.outs),
         front.scratch,
@@ -999,11 +1119,15 @@
         12 * tok_rows * width * width,
     )
     qkv_rows, lse, attended, after_attn, mixed_in, grad_dense, dispatch, probs = results[:8]
-    arrived = exchange(results[8 : 8 + experts], 1)
+    leaving = results[8 : 8 + experts]
     small_full, qkv_full, out_full, fc_full, proj_full = results[8 + experts :] if fast else full
 
-    dense_out, grad_mixed, d_fc, d_proj, *gathered = mlp(
-        [mixed_in, grad_dense],
+    if fast:
+        out_to = Exchange(leaving[1:], 1, experts, 0, gather_experts[0].turns, leaving[0].shape)
+        gather_experts = [out_to] + gather_experts
+    dense_out, grad_mixed, d_fc, d_proj, *moved = mlp(
+        mixed_in,
+        grad_dense,
         together(fc_full),
         together(proj_full),
         "dense_mlp",
@@ -1012,15 +1136,25 @@
         experts,
         devices if fast else None,
     )
-    scatter_dense = []
+    scatters, return_to, given = [], None, None
+    chunks = 4
+    step = width // chunks
+    half = (experts // 2, step, 128)
+    win_out = [jax.ShapeDtypeStruct(expert_in.shape, f32)]
+    wout_out = [jax.ShapeDtypeStruct(expert_out.shape[:2] + (width // 2,), f32)]
+
+    def store_wout(out, chunk, sums):
+        at = pl.ds(pl.multiple_of(chunk * step, step), step)
+        for h, total in enumerate(sums):
+            for c in range(half[0]):
+                out[0, (h * half[0] + c) * 128 : (h * half[0] + c + 1) * 128, at] = total[c].T
+
     if fast:
-        win_full, wout_full = gathered
-        chunks = 4
-        by_chip = lambda a: a.reshape(4, 2, 2, experts // 2, chunks, width // chunks, 128)
-
-        def store_dense(outs, i, value):
-            step = width // chunks
-
+        arrived = leaving[:1] + moved[: experts - 1]
+        win_full, wout_full = moved[experts - 1 :]
+        by_chip = lambda a: a.reshape(4, 2, 2, experts // 2, chunks, step, 128)
+
+        def store(outs, i, value):
             @when(i < chunks)
             def _():
                 for q in range(step // share):
@@ -1029,35 +1163,76 @@
 
             @when(i >= chunks)
             def _():
-                at = pl.multiple_of((i - chunks) * step, step)
-                outs[1][:, pl.ds(at, step)] = value.T
+                outs[1][:, pl.ds(pl.multiple_of((i - chunks) * step, step), step)] = value.T
+
+        def store_experts(outs, i, sums):
+            first = 2 * chunks
+
+            @when(i < first + chunks)
+            def _():
+                at = pl.ds(pl.multiple_of((i - first) * step, step), step)
+                for h, total in enumerate(sums):
+                    for c in range(half[0]):
+                        outs[2][0, at, (h * half[0] + c) * 128 : (h * half[0] + c + 1) * 128] = total[c]
+
+            @when(i >= first + chunks)
+            def _():
+                store_wout(outs[3], i - first - chunks, sums)
+
+        def store_any(outs, i, value):
+            (store_experts if isinstance(value, tuple) else store)(outs, i, value)
 
         outs = [jax.ShapeDtypeStruct((share, ff), f32), jax.ShapeDtypeStruct((ff // devices, width), f32)]
-        scatter_dense = [Scatter([by_chip(d_fc), by_chip(d_proj)], "rows", experts, outs, store_dense)]
-    *returned, d_win, d_wout, grad_fc, grad_proj = (
-        list(mlp(arrived, win_full, wout_full, "expert_mlp", scatter_dense, 3, experts)) + ([] if fast else [None] * 2)
+        parts = [(by_chip(d_fc), True, 0, chunks), (by_chip(d_proj), True, 0, chunks)]
+        parts += [(None, False, 0, chunks), (None, False, 0, chunks // 2)]
+        summing = Scatter(parts, half, experts, outs + win_out + wout_out, store_any, z_late=10)
+        return_to = Exchange([], -1, experts, None, summing.turns, leaving[0].shape)
+        scatters = [return_to, summing]
+    else:
+        arrived = exchange(leaving, 1)
+    blocks, size = win_full.shape[0], win_full.shape[2]
+    experts_kernel = Experts(arrived, blocks, width, size, chunks if fast else None, return_to)
+    if fast:
+
+        def given(ins, os, own):
+            summing.given = os[experts : experts + 2]
+            return_to.sources = os[1:experts]
+
+    per = experts_kernel.PER_STEP
+    results = call(
+        "expert_mlp",
+        blocks // per,
+        experts_kernel,
+        arrived + [win_full, wout_full],
+        [whole] * experts
+        + [pl.BlockSpec((per, width, size), lambda j: (j, 0, 0)), pl.BlockSpec((per, size, width), lambda j: (j, 0, 0))],
+        experts_kernel.outs,
+        [hbm] * len(experts_kernel.outs),
+        experts_kernel.scratch,
+        scatters,
+        3,
+        experts,
+        12 * experts * capacity * width * blocks * size,
+        given,
     )
-    came_back = exchange(returned, -1)
+    returned, (d_win, d_wout) = results[:experts], results[experts : experts + 2]
+    if fast:
+        results = results[experts + 2 :]
+        came_back = returned[:1] + results[: experts - 1]
+        grad_fc, grad_proj, grad_win, grad_wout = results[experts - 1 :]
+    else:
+        came_back = exchange(returned, -1)
     back = Back(tok_rows, width, experts, devices, capacity)
     back.moves = []
     if fast:
-        chunks_e = 8
-        size = width // chunks_e
-        cut_rows = lambda a: a.reshape(4, 2, chunks_e, 2, size // 2, a.shape[2])
-        at = lambda i: pl.ds(pl.multiple_of(i * size, size), size)
-
-        def store_win(outs, i, value):
-            outs[0][0, at(i)] = value
-
-        def store_wout(outs, i, value):
-            outs[0][0, :, at(i)] = value.T
-
-        like = lambda a: [jax.ShapeDtypeStruct(a.shape, f32)]
-        scatter_win = Scatter([cut_rows(d_win)], "plane", experts, like(expert_in), store_win)
-        scatter_wout = Scatter([cut_rows(d_wout)], "plane", experts, like(expert_out), store_wout)
-        (grad_win,) = move("scatter_win", [scatter_win], 4, experts)
+        parts = [(d_wout, False, chunks // 2, chunks // 2)]
+        scatter_wout = Scatter(
+            parts, half, experts, wout_out, lambda outs, i, sums: store_wout(outs[0], i, sums)
+        )
+        parts = [(None, True, 0, back.items)]
+        made = back.made()
         scatter_rest = Scatter(
-            [], "made", experts, back.final_outs(), back.store, back.first_item, back.GROUP, back.made()
+            parts, made[4:], experts, back.final_outs(), back.store, back.first_item, made
         )
         back.moves = [scatter_wout, scatter_rest]
     outs = back.outs + ([] if fast else [jax.ShapeDtypeStruct((back.items, width, back.columns), bf16)])
@@ -1065,10 +1240,10 @@
         "back",
         back.steps,
         back,
-        [tokens, cotangent, routes, dropped, qkv_rows, lse, attended, mixed_in, dispatch, probs]
+        [tokens, cotangent, code, qkv_rows, lse, attended, mixed_in, dispatch, probs]
         + [small_full, qkv_full, out_full, dense_out, grad_mixed, after_attn]
         + came_back,
-        [whole] * 10 + [hbm] * (6 + experts),
+        [whole] * 9 + [hbm] * (6 + experts),
         outs,
         [whole] * len(outs),
         back.scratch,
@@ -1078,13 +1253,15 @@
         32 * tok_rows * width * width,
     )
     if fast:
-        grad_wout, grad_wqkv, grad_wo, grad_small = results
+        more_wout, grad_wqkv, grad_wo, grad_small = results
+        grad_wout = jnp.concatenate([grad_wout, more_wout], axis=2)
     else:
         summed = scatter_xla(results[0].reshape(back.items, devices, share, -1).swapaxes(0, 1), AXES)
-        grad_wo = jnp.concatenate([summed[0], summed[-1][:, : back.rest]], axis=1)
-        grad_small = summed[-1][:, back.rest : back.rest + 128]
-        groups = summed[1:-1].reshape(back.groups, share, 3, back.part)
-        grad_wqkv = groups.transpose(1, 2, 0, 3).reshape(share, 3 * width)
+        last = summed[-1]
+        grad_wo = jnp.concatenate([*summed[: back.firsts], last[:, : back.rest]], axis=1)
+        grad_small = last[:, back.rest : back.rest + 128]
+        pairs = summed[back.firsts : -1].reshape(back.pairs, share, 3, PAIR)
+        grad_wqkv = pairs.transpose(1, 2, 0, 3).reshape(share, 3 * width)
         grad_fc = scatter_xla(d_fc.reshape(devices, share, ff), AXES)
         by_unit = d_proj.reshape(width, devices, ff // devices).transpose(1, 0, 2)
         grad_proj = scatter_xla(by_unit, AXES).T
@@ -1138,7 +1315,7 @@
         P("expert", None, "node"),
         P("expert", "node", None),
     )
-    fast = mesh.shape["node"] == 8 and mesh.shape["expert"] % 2 == 0
+    fast = mesh.shape["node"] == 8 and mesh.shape["expert"] == 4
     return jax.shard_map(
         functools.partial(shards, fast), mesh=mesh, in_specs=in_specs, out_specs=out_specs, check_vma=False
     )

time: 503 us -> 464 us (0.922)
  Pallas kernels: 459 us -> 445 us
  waiting for transfers between devices: 12.3 us -> 0 us
  starting transfers between devices: 9.86 us -> 0 us
  local copies, waits for them, and re-layouts: 19.8 us -> 12.7 us
    pallas_call x5 -> x4, Pallas kernels: 459 us -> 445 us  [call(): pl.pallas_call(kernel, grid=(total,), out_shape=list(outs) + join('outs')...]
    ppermute x6 -> x0, waiting for transfers between devices: 12.3 us -> none  [exchange(): moved.append(lax.ppermute(parts[j], 'expert', shift))]
    ppermute x6 -> x0, starting transfers between devices: 9.86 us -> none  [exchange(): moved.append(lax.ppermute(parts[j], 'expert', shift))]
    unnamed x37 -> x25, local copies, waits for them, and re-layouts: 14.4 us -> 8.92 us
  transfers between devices with their start and end apart: 6 -> 0, of which waited for: 1 -> 0; matrix products, arithmetic and copies ran while one was open for 0% -> 0% of each run, Pallas kernels for 26% -> 0%
where the time goes in v5:
time: 464 us; the launch traced here: 463 us
  Pallas kernels  445 us (96%)
  local copies, waits for them, and re-layouts  12.7 us (3%)
  other arithmetic  4.87 us (1%)
    pallas_call x4, Pallas kernels, call(): pl.pallas_call(kernel, grid=(total,), out_shape=list(outs) + join('outs')...  445 us

profile of v5, /device:TPU:0, one launch (start us, length us, event | category | flops | bytes accessed | tf_op | source)
XLA Modules:
  0.0 463.0 jit_solution(16310036010354178126)
XLA Ops:
  0.6 0.7 pad_maximum_fusion.1
  1.4 1.3 add_convert_fusion.refs_2_
  2.7 0.1 copy.38
  2.8 0.6 pad.4.refs_3_
  3.4 128.7 %front.1 = (bf16[512,3072]{1,0:T(8,128)(2,1)}, f32[8,2,512]{2,1,0:T(2,128)}, bf16[512,1024]{1,0:T(8,128)(2,1)}, f32[512,1024]{1,0:T(8,128)}, bf16[512,1024]{1,0:...) custom-call(bf16[512,1024]{1,0:T(8,128)(2,1)} %refs_0_.3, ...), custom_call_target="tpu_custom_call" | custom-call | flops 6442450944 | bytes 33554432 | tf_op jit(solution)/shard_map/front/pallas_call | solution.py:478
  132.1 83.4 %dense_mlp.1 = (f32[512,1024]{1,0:T(8,128)}, f32[512,1024]{1,0:T(8,128)}, bf16[32,1024,128]{2,1,0:T(8,128)(2,1)}, bf16[32,1024,128]{2,1,0:T(8,128)(2,1)}, bf16[1...) custom-call(bf16[512,1024]{1,0:T(8,128)(2,1)} %get-tuple-element.56., ...), custom_call_target="tpu_custom_call" | custom-call | flops 25769803776 | bytes 33554432 | tf_op jit(solution)/shard_map/dense_mlp/pallas_call | solution.py:478
  215.5 145.6 %expert_mlp.1 = (bf16[160,2048]{1,0:T(8,128)(2,1)}, bf16[160,2048]{1,0:T(8,128)(2,1)}, bf16[160,2048]{1,0:T(8,128)(2,1)}, bf16[160,2048]{1,0:T(8,128)(2,1)}, bf1...) custom-call(bf16[160,2048]{1,0:T(8,128)(2,1)} %get-tuple-element.71., ...), custom_call_target="tpu_custom_call" | custom-call | flops 32212254720 | bytes 33554432 | tf_op jit(solution)/shard_map/expert_mlp/pallas_call | solution.py:478
  361.1 87.0 %back.1 = (bf16[512,1024]{1,0:T(8,128)(2,1)}, f32[512,1024]{1,0:T(8,128)}, f32[1,512,512]{2,1,0:T(8,128)}, f32[32,3072]{1,0:T(8,128)}, f32[32,1024]{1,0:T(8,128)}, /*index=5*/f32[32,128]{1,0:T(8,128)}) custom-call(bf16[512,1024]{1,0:T(8,128)(2,1)} %refs_0_.3, bf16[512,1024]{1,0:T(8,128)(2,1)} %refs_1_.3, f32[2,512]{1,0:T(2,128)} %add_convert_fusion.refs_2_, ...), custom_call_target="tpu_custom_call" | custom-call | flops 17179869184 | bytes 33554432 | tf_op jit(solution)/shard_map/back/pallas_call | solution.py:478
  448.1 1.5 slice_reduce_fusion
  449.6 0.8 slice.14
  450.4 0.7 copy.39
  451.1 0.8 slice.15
  451.9 0.6 copy.40
  452.5 2.9 pad_maximum_fusion
  455.4 0.0 copy-done.2
  455.4 1.0 copy.48
  456.3 1.0 copy-done.1
  457.3 1.3 copy.49
  458.7 0.7 copy.50
  459.4 0.7 copy.51
  460.1 0.8 copy.52
  460.9 0.8 copy.53
  461.7 0.0 copy-done
  461.7 1.3 copy.54
  (13 shorter events, 0.0 us)
Async XLA Ops:
  361.1 91.4 %copy-start.3 = (f32[1,512,512]{2,1,0:T(8,128)S(1)}, f32[1,512,512]{2,1,0:T(8,128)}, u32[]{:S(2)}) copy-start(f32[1,512,512]{2,1,0:T(8,128)} %get-tuple-element.92) | copy-start | bytes 3145732
  452.5 2.9 copy-start.2
  455.4 2.0 copy-start.1
  457.3 1.3 copy-start.6
  457.3 2.1 copy-start.7
  457.3 2.7 copy-start.5
  457.3 3.5 copy-start.4
  458.7 3.0 copy-start

commit v6 on v5

--- a/solution.py
+++ b/solution.py
@@ -94,7 +94,7 @@
             pltpu.SemaphoreType.DMA((m,)),
         ]
         self.along_z = any(dense)
-        self.steps = [self.along, self.across, self.corner, self.over, self.end][0 if self.along_z else 1 :]
+        self.steps = [self.along, self.across, self.corner, self.over, self.end]
         self.turns = len(items) + len(self.steps) - 1
 
     def bind(self, ins, outs, scratch, place):
@@ -169,12 +169,9 @@
             copy.start()
 
     def across(self, local, z, xy, diag, core):
-        if not self.along_z:
-            local.start()
         for copy in z:
             copy.wait()
-        if self.along_z:
-            local.wait()
+        local.wait()
         xy[0].start()
         xy[1].start()
         core[0].start()
@@ -191,8 +188,6 @@
         core[3].start()
 
     def end(self, local, z, xy, diag, core):
-        if not self.along_z:
-            local.wait()
         for copy in core:
             copy.wait()
 
@@ -530,45 +525,97 @@
     return [jnp.broadcast_to(code[i : i + 1], (128, length)).T.astype(jnp.int32) for i in range(2)]
 
 
-class Front:
-    def __init__(self, length, width, experts, devices, capacity, moves):
-        self.length, self.width, self.experts, self.capacity, self.moves = length, width, experts, capacity, moves
+class Forward:
+    def __init__(self, length, width, experts, devices, capacity, ff, gather, leave):
+        self.length, self.width, self.experts, self.capacity = length, width, experts, capacity
+        self.gather, self.leave = gather, leave
         pairs = width // PAIR
-        share = width // devices
+        share = self.share = width // devices
+        self.blocks = ff // BLOCK
+        self.per_block = BLOCK * devices // ff
         self.at_norm, self.at_qkv = 4, 6
         self.at_heads = self.at_qkv + 1
         self.per_turn = 2
         self.at_out = self.at_heads + length // SEQ * pairs // self.per_turn
-        self.steps = max(self.at_out + 1, moves.turns if moves else 0)
+        self.at_leave = self.at_out + 1
+        self.at_mlp = max(self.at_leave + 2, self.DENSE_ITEMS + 3)
+        self.steps = self.at_mlp + self.blocks
         slots = experts * capacity
         rows = lambda c, t: jax.ShapeDtypeStruct((length, c), t)
+        piece = (capacity, 2 * width)
+        self.kept = 1 if leave else experts
         self.outs = [
             rows(3 * width, bf16),
             jax.ShapeDtypeStruct((length // SEQ * pairs, 2, SEQ), f32),
             rows(width, bf16),
             rows(width, f32),
             rows(width, bf16),
-            rows(width, bf16),
             rows(slots, bf16),
             rows(128, f32),
-        ] + [jax.ShapeDtypeStruct((capacity, 2 * width), bf16)] * experts
-        self.scratch = [
+            rows(width, f32),
+            rows(width, f32),
+        ] + [jax.ShapeDtypeStruct(piece, bf16)] * self.kept
+        if gather:
+            stages = [(devices, self.per_block * share * devices // ff * (ff // devices // 128), 128)]
+            stages = [(devices, BLOCK // 128 * share, 128), (self.per_block, width, 128)]
+            targets = [(devices, width, 128)] * 2
+        else:
+            stages, targets = [(width, BLOCK)] * 2, [(width, ff)] * 2
+        self.targets = [jax.ShapeDtypeStruct(t, bf16) for t in targets]
+        self.scratch = [pltpu.VMEM(piece, bf16)] * (experts - self.kept) + [
             pltpu.VMEM((devices, share, 128), bf16),
             pltpu.VMEM((devices, share, 3 * width), bf16),
             pltpu.VMEM((devices, share, width), bf16),
             pltpu.VMEM((8, width), f32),
             pltpu.VMEM((length, width), bf16),
             pltpu.SemaphoreType.DMA((3,)),
+            pltpu.VMEM((length, width), bf16),
+            pltpu.VMEM((length, width), bf16),
+            pltpu.VMEM((width, length), bf16),
+            pltpu.VMEM((width, length), bf16),
+            pltpu.VMEM((2, devices, share, BLOCK), bf16),
+            pltpu.VMEM((2, self.per_block, ff // devices, width), bf16),
+            pltpu.VMEM((2,) + stages[0], bf16),
+            pltpu.VMEM((2,) + stages[1], bf16),
+            pltpu.SemaphoreType.DMA((2, 2)),
+            pltpu.SemaphoreType.DMA((2, 2)),
         ]
 
+    DENSE_ITEMS = 12
+
     def __call__(self, now, steps, tok, cot, code, *refs):
-        full = self.moves.full[:3] if self.moves else refs[:3]
-        refs = refs if self.moves else refs[3:]
-        qkv, lse, att, after, mixed, gd, disp, info = refs[:8]
-        leave = refs[8 : 8 + self.experts]
-        ws, wq, wo, gains, attn_in, sems = refs[8 + self.experts :]
+        refs = list(refs)
+        take = lambda count: [refs.pop(0) for _ in range(count)]
+        full = self.gather.full[:5] if self.gather else take(5)
+        qkv, lse, att, after, mixed, disp, info, dense_out, grad_mixed = take(9)
+        leave = take(self.kept)
+        targets = take(2)
+        leave += take(self.experts - self.kept)
+        ws, wq, wo, gains, attn_in, sems, gd, ge, xt, gt, w1, w2, stage_1, stage_2, w_sems, d_sems = refs
         width, length = self.width, self.length
         loads = [pltpu.make_async_copy(a, b, sems.at[i]) for i, (a, b) in enumerate(zip(full, (ws, wq, wo)))]
+
+        def weights(block):
+            at = lax.rem(block, 2)
+            cols = pl.ds(pl.multiple_of(block * BLOCK, BLOCK), BLOCK)
+            return [
+                pltpu.make_async_copy(full[3].at[:, :, cols], w1.at[at], w_sems.at[at, 0]),
+                pltpu.make_async_copy(full[4].at[pl.ds(block * self.per_block, self.per_block)], w2.at[at], w_sems.at[at, 1]),
+            ]
+
+        def flush(block):
+            at = lax.rem(block, 2)
+            if self.gather:
+                size = BLOCK // 128 * self.share
+                first = targets[0].at[:, pl.ds(pl.multiple_of(block * size, size), size)]
+                second = targets[1].at[pl.ds(block * self.per_block, self.per_block)]
+            else:
+                cols = pl.ds(pl.multiple_of(block * BLOCK, BLOCK), BLOCK)
+                first, second = targets[0].at[:, cols], targets[1].at[:, cols]
+            return [
+                pltpu.make_async_copy(stage_1.at[at], first, d_sems.at[at, 0]),
+                pltpu.make_async_copy(stage_2.at[at], second, d_sems.at[at, 1]),
+            ]
 
         @when(now == self.at_norm)
         def _():
@@ -611,9 +658,77 @@
         def _():
             loads[2].start()
             loads[2].wait()
-            self.route(tok, cot, code, att, wo, ws, gains, after, mixed, gd, disp, info, leave)
-
-    def route(self, tok, cot, code, att, wo, ws, gains, after, mixed, gd, disp, info, leave):
+            self.route(tok, cot, code, att, wo, ws, gains, after, mixed, gd, ge, disp, info)
+
+        @when(now == self.at_leave)
+        def _():
+            for h, values in enumerate((mixed, ge)):
+                placed = product_tn(disp[...], values[...]).astype(bf16)
+                for j in range(self.experts):
+                    leave[j][:, h * width : (h + 1) * width] = placed[j * self.capacity : (j + 1) * self.capacity]
+            if self.leave:
+                self.leave.send()
+
+        @when(now == self.at_mlp - 1)
+        def _():
+            xt[...] = mixed[...].T
+            gt[...] = gd[...].T
+            dense_out[...] = jnp.zeros_like(dense_out)
+            grad_mixed[...] = jnp.zeros_like(grad_mixed)
+
+        @when(jnp.logical_and(now >= self.at_mlp, now < self.at_mlp + self.blocks))
+        def _():
+            block = now - self.at_mlp
+            at = lax.rem(block, 2)
+
+            @when(block == 0)
+            def _():
+                for copy in weights(0):
+                    copy.start()
+
+            @when(block + 1 < self.blocks)
+            def _():
+                for copy in weights(block + 1):
+                    copy.start()
+
+            for copy in weights(block):
+                copy.wait()
+
+            @when(block >= 2)
+            def _():
+                for copy in flush(block - 2):
+                    copy.wait()
+
+            d1, d2 = mlp_block(
+                mixed,
+                gd,
+                xt,
+                gt,
+                w1[at].reshape(width, BLOCK),
+                w2[at].reshape(BLOCK, width),
+                dense_out,
+                grad_mixed,
+            )
+            if self.gather:
+                share = self.share
+                for c in range(BLOCK // 128):
+                    cols = slice(c * 128, (c + 1) * 128)
+                    for s in range(width // share):
+                        stage_1[at, s, c * share : (c + 1) * share] = d1[s * share : (s + 1) * share, cols]
+                    stage_2[at, c] = d2[:, cols]
+            else:
+                stage_1[at] = d1
+                stage_2[at] = d2
+            for copy in flush(block):
+                copy.start()
+
+            @when(block == self.blocks - 1)
+            def _():
+                for last in (self.blocks - 2, self.blocks - 1):
+                    for copy in flush(last):
+                        copy.wait()
+
+    def route(self, tok, cot, code, att, wo, ws, gains, after, mixed, gd, ge, disp, info):
         width, length, experts = self.width, self.length, self.experts
         route, drop = columns_of(code)
         after[...] = tok[...].astype(f32) + matmul(att[...], wo[...].reshape(width, width))
@@ -637,6 +752,7 @@
         coef_1 = over_lanes(jnp.where(lane == 3 + experts, coef, 0.0))
         grad = cot[...].astype(f32)
         gd[...] = (coef_0 * grad).astype(bf16)
+        ge[...] = (coef_1 * gate * grad).astype(bf16)
         square = lambda d: lax.broadcasted_iota(jnp.int32, (length, length), d)
         earlier = jnp.where(square(0) > square(1), 1.0, 0.0).astype(bf16)
         position = over_lanes(chosen * matmul(earlier, chosen.astype(bf16))).astype(jnp.int32)
@@ -644,11 +760,6 @@
         target = jnp.where(turn < 0, turn + experts, turn) * self.capacity + position
         slot = lax.broadcasted_iota(jnp.int32, (length, experts * self.capacity), 1)
         disp[...] = jnp.where(slot == target, 1.0, 0.0).astype(bf16)
-        sent = (mixed[...], (coef_1 * gate * grad).astype(bf16))
-        for h, values in enumerate(sent):
-            placed = product_tn(disp[...], values).astype(bf16)
-            for j in range(experts):
-                leave[j][:, h * width : (h + 1) * width] = placed[j * self.capacity : (j + 1) * self.capacity]
 
 
 def attend_pair_backward(q, k, v, g, lse):
@@ -701,7 +812,7 @@
         self.firsts = width // self.columns
         self.rest = width - self.firsts * self.columns
         self.items = self.firsts + self.pairs + 1
-        self.heads_at = 4
+        self.heads_at = 3
         self.last = self.heads_at + self.pairs
         self.steps = self.last + 1
         self.first_item = self.heads_at
@@ -796,8 +907,6 @@
             for copy in loads + pair_weights(0):
                 copy.start()
 
-        @when(now == 1)
-        def _():
             for copy in loads:
                 copy.wait()
             probs = jnp.where(jnp.logical_and(lane >= 2, lane < 2 + experts), info[...], 0.0)
@@ -828,7 +937,7 @@
             )
             gains[...] = weights.astype(f32).T[:8]
 
-        @when(now == 2)
+        @when(now == 1)
         def _():
             normed, scale = normalize(tokens_grad[...])
             d_heads[1:2] = jnp.sum(grads[...] * normed, axis=0, keepdims=True)
@@ -836,7 +945,7 @@
             normed, _ = normalize(tok[...].astype(f32))
             attn_in_t[...] = (normed * gains[0:1]).astype(bf16).T
 
-        @when(now == 3)
+        @when(now == 2)
         def _():
             grad_attn = grads[...].astype(bf16)
             grad_att[...] = outer_nt(grad_attn, wo[...].reshape(width, width)).astype(bf16)
@@ -897,58 +1006,6 @@
     out_sum[...] += matmul(hidden, w2)
     back_sum[...] += outer_nt(grad_pre, w1)
     return matmul(xt[...], grad_pre).astype(bf16), matmul(gt[...], hidden).astype(bf16)
-
-
-def mlp_kernel(share, now, steps, x, g, w1, w2, out_sum, back_sum, d1_ref, d2_ref, xt, gt):
-    @when(now == 0)
-    def _():
-        xt[...] = x[...].T
-        gt[...] = g[...].T
-        out_sum[...] = jnp.zeros_like(out_sum)
-        back_sum[...] = jnp.zeros_like(back_sum)
-
-    d1, d2 = mlp_block(x, g, xt, gt, w1[...], w2[...], out_sum, back_sum)
-    if share is None:
-        d1_ref[...] = d1
-        d2_ref[...] = d2
-    else:
-        for c in range(d1.shape[1] // 128):
-            cols = slice(c * 128, (c + 1) * 128)
-            for s in range(d1_ref.shape[0]):
-                d1_ref[s, c * share : (c + 1) * share] = d1[s * share : (s + 1) * share, cols]
-            d2_ref[c] = d2[:, cols]
-
-
-def mlp(x, g, w1, w2, name, moves, collective_id, experts, devices=None):
-    share = None
-    size = BLOCK
-    rows, width = x.shape
-    blocks = w1.shape[1] // size
-    w1_spec = pl.BlockSpec((width, size), lambda j: (0, j))
-    w2_spec = pl.BlockSpec((size, width), lambda j: (j, 0))
-    d_shape, d_specs = (width, blocks * size), [w1_spec] * 2
-    if devices:
-        share = width // devices
-        d_shape = (devices, width, 128)
-        d_specs = [
-            pl.BlockSpec((devices, size // 128 * share, 128), lambda j: (0, j, 0)),
-            pl.BlockSpec((size // 128, width, 128), lambda j: (j, 0, 0)),
-        ]
-    whole = pl.BlockSpec(memory_space=pltpu.VMEM)
-    return call(
-        name,
-        blocks,
-        functools.partial(mlp_kernel, share),
-        [x, g, w1, w2],
-        [whole] * 2 + [w1_spec, w2_spec],
-        [jax.ShapeDtypeStruct((rows, width), f32)] * 2 + [jax.ShapeDtypeStruct(d_shape, bf16)] * 2,
-        [whole] * 2 + d_specs,
-        [pltpu.VMEM((width, rows), bf16)] * 2,
-        moves,
-        collective_id,
-        experts,
-        12 * rows * width * blocks * size,
-    )
 
 
 class Experts:
@@ -1071,20 +1128,20 @@
     small = jnp.concatenate([gain_attn[:, None], gain_mix[:, None], w_router, w_coef], axis=1)
     small = jnp.pad(small, ((0, 0), (0, 128 - small.shape[1])))
     win, wout = expert_in[0], expert_out[0]
-    together = lambda a: a.reshape((devices * a.shape[1],) + a.shape[2:])
     cut = lambda a, rows, columns, m, n: [
         [(a, i * (rows // m), rows // m, j * (columns // n), columns // n)] for i in range(m) for j in range(n)
     ]
     weights = (small, w_qkv, w_out, w_fc, w_proj)
     capacity = -(-(tok_rows * 10) // (8 * experts))
-    gather_dense, gather_experts = [], []
+    moves, given = [], None
     if fast:
         items = cut(1, share, 3 * width, 1, 3) + cut(2, share, width, 1, 1)
         items += cut(3, share, ff, 1, 4) + cut(4, ff // devices, width, 4, 1)
         items[0] = cut(0, share, 128, 1, 1)[0] + items[0]
-        gather_dense = [Gather(list(weights), [True] * 5, items, nodes, experts)]
-        items = cut(0, width, win.shape[1], 4, 1) + cut(1, wout.shape[0], width, 4, 1)
-        gather_experts = [Gather([win, wout], [False] * 2, items, nodes, experts)]
+        assert len(items) == Forward.DENSE_ITEMS
+        items += cut(5, width, win.shape[1], 4, 1) + cut(6, wout.shape[0], width, 4, 1)
+        moves = [Gather(list(weights) + [win, wout], [True] * 5 + [False] * 2, items, nodes, experts)]
+        moves.append(Exchange([], 1, experts, None, moves[0].turns, (capacity, 2 * width)))
         full = []
     else:
         full = [lax.all_gather(a, AXES, axis=0, tiled=False) for a in weights]
@@ -1100,48 +1157,43 @@
             moved.append(lax.ppermute(parts[j], "expert", shift))
         return moved
 
-    front = Front(tok_rows, width, experts, devices, capacity, gather_dense[0] if fast else None)
-    kept = full[:3]
+    forward = Forward(tok_rows, width, experts, devices, capacity, ff, *(moves or (None, None)))
     whole, hbm = pl.BlockSpec(memory_space=pltpu.VMEM), pl.BlockSpec(memory_space=pltpu.HBM)
     code = jnp.stack([routes[:, 0], dropped]).astype(f32)
+    if fast:
+
+        def given(ins, os, own):
+            moves[1].sources = own[: experts - 1]
+
     results = call(
-        "front",
-        front.steps,
-        front,
-        [tokens, cotangent, code] + kept,
-        [whole] * 3 + [hbm] * len(kept),
-        front.outs,
-        [whole] * len(front.outs),
-        front.scratch,
-        gather_dense,
+        "forward",
+        forward.steps,
+        forward,
+        [tokens, cotangent, code] + full,
+        [whole] * 3 + [hbm] * len(full),
+        forward.outs + forward.targets,
+        [whole] * len(forward.outs) + [hbm] * 2,
+        forward.scratch,
+        moves,
         1,
         experts,
-        12 * tok_rows * width * width,
+        12 * tok_rows * width * (width + ff),
+        given,
     )
-    qkv_rows, lse, attended, after_attn, mixed_in, grad_dense, dispatch, probs = results[:8]
-    leaving = results[8 : 8 + experts]
-    small_full, qkv_full, out_full, fc_full, proj_full = results[8 + experts :] if fast else full
-
-    if fast:
-        out_to = Exchange(leaving[1:], 1, experts, 0, gather_experts[0].turns, leaving[0].shape)
-        gather_experts = [out_to] + gather_experts
-    dense_out, grad_mixed, d_fc, d_proj, *moved = mlp(
-        mixed_in,
-        grad_dense,
-        together(fc_full),
-        together(proj_full),
-        "dense_mlp",
-        gather_experts,
-        2,
-        experts,
-        devices if fast else None,
+    qkv_rows, lse, attended, after_attn, mixed_in, dispatch, probs, dense_out, grad_mixed = results[:9]
+    results = results[9:]
+    leaving, (d_fc, d_proj), moved = (
+        results[: forward.kept],
+        results[forward.kept : forward.kept + 2],
+        results[forward.kept + 2 :],
     )
+    small_full, qkv_full, out_full = (moved if fast else full)[:3]
     scatters, return_to, given = [], None, None
     chunks = 4
     step = width // chunks
     half = (experts // 2, step, 128)
     win_out = [jax.ShapeDtypeStruct(expert_in.shape, f32)]
-    wout_out = [jax.ShapeDtypeStruct(expert_out.shape[:2] + (width // 2,), f32)]
+    wout_out = [jax.ShapeDtypeStruct(expert_out.shape, f32)]
 
     def store_wout(out, chunk, sums):
         at = pl.ds(pl.multiple_of(chunk * step, step), step)
@@ -1150,8 +1202,8 @@
                 out[0, (h * half[0] + c) * 128 : (h * half[0] + c + 1) * 128, at] = total[c].T
 
     if fast:
-        arrived = leaving[:1] + moved[: experts - 1]
-        win_full, wout_full = moved[experts - 1 :]
+        win_full, wout_full = moved[5:7]
+        arrived = leaving + moved[7:]
         by_chip = lambda a: a.reshape(4, 2, 2, experts // 2, chunks, step, 128)
 
         def store(outs, i, value):
@@ -1184,8 +1236,8 @@
 
         outs = [jax.ShapeDtypeStruct((share, ff), f32), jax.ShapeDtypeStruct((ff // devices, width), f32)]
         parts = [(by_chip(d_fc), True, 0, chunks), (by_chip(d_proj), True, 0, chunks)]
-        parts += [(None, False, 0, chunks), (None, False, 0, chunks // 2)]
-        summing = Scatter(parts, half, experts, outs + win_out + wout_out, store_any, z_late=10)
+        parts += [(None, False, 0, chunks)] * 2
+        summing = Scatter(parts, half, experts, outs + win_out + wout_out, store_any, z_late=12)
         return_to = Exchange([], -1, experts, None, summing.turns, leaving[0].shape)
         scatters = [return_to, summing]
     else:
@@ -1225,16 +1277,12 @@
     back = Back(tok_rows, width, experts, devices, capacity)
     back.moves = []
     if fast:
-        parts = [(d_wout, False, chunks // 2, chunks // 2)]
-        scatter_wout = Scatter(
-            parts, half, experts, wout_out, lambda outs, i, sums: store_wout(outs[0], i, sums)
-        )
         parts = [(None, True, 0, back.items)]
         made = back.made()
         scatter_rest = Scatter(
             parts, made[4:], experts, back.final_outs(), back.store, back.first_item, made
         )
-        back.moves = [scatter_wout, scatter_rest]
+        back.moves = [scatter_rest]
     outs = back.outs + ([] if fast else [jax.ShapeDtypeStruct((back.items, width, back.columns), bf16)])
     mixed, tokens_grad, *results = call(
         "back",
@@ -1253,8 +1301,7 @@
         32 * tok_rows * width * width,
     )
     if fast:
-        more_wout, grad_wqkv, grad_wo, grad_small = results
-        grad_wout = jnp.concatenate([grad_wout, more_wout], axis=2)
+        grad_wqkv, grad_wo, grad_small = results
     else:
         summed = scatter_xla(results[0].reshape(back.items, devices, share, -1).swapaxes(0, 1), AXES)
         last = summed[-1]

time: 464 us -> 452 us (0.974)
  Pallas kernels: 445 us -> 435 us
    pallas_call x4 -> x3, Pallas kernels: 445 us -> 435 us  [call(): pl.pallas_call(kernel, grid=(total,), out_shape=list(outs) + join('outs')...]
    unnamed x25 -> x24, local copies, waits for them, and re-layouts: 8.92 us -> 10.6 us
where the time goes in v6:
time: 452 us
  Pallas kernels  435 us (96%)
  local copies, waits for them, and re-layouts  14.5 us (3%)
    pallas_call x3, Pallas kernels, call(): pl.pallas_call(kernel, grid=(total,), out_shape=list(outs) + join('outs')...  435 us
    unnamed x24, local copies, waits for them, and re-layouts  10.6 us

profile of v6, /device:TPU:0, one launch (start us, length us, event | category | flops | bytes accessed | tf_op | source)
XLA Modules:
  0.0 451.7 jit_solution(5166965655549713194)
XLA Ops:
  0.6 0.7 pad_maximum_fusion
  1.4 1.3 add_convert_fusion.refs_2_
  2.7 0.1 copy.38
  2.8 0.6 pad.4.refs_3_
  3.4 202.5 %forward.1 = (bf16[512,3072]{1,0:T(8,128)(2,1)}, f32[8,2,512]{2,1,0:T(2,128)}, bf16[512,1024]{1,0:T(8,128)(2,1)}, f32[512,1024]{1,0:T(8,128)}, bf16[512,1024]{1,...) custom-call(bf16[512,1024]{1,0:T(8,128)(2,1)} %refs_0_.3, ...), custom_call_target="tpu_custom_call" | custom-call | flops 32212254720 | bytes 33554432 | tf_op jit(solution)/shard_map/forward/pallas_call | solution.py:473
  205.9 156.8 %expert_mlp.1 = (bf16[160,2048]{1,0:T(8,128)(2,1)}, bf16[160,2048]{1,0:T(8,128)(2,1)}, bf16[160,2048]{1,0:T(8,128)(2,1)}, bf16[160,2048]{1,0:T(8,128)(2,1)}, bf1...) custom-call(bf16[160,2048]{1,0:T(8,128)(2,1)} %get-tuple-element.57., ...), custom_call_target="tpu_custom_call" | custom-call | flops 32212254720 | bytes 33554432 | tf_op jit(solution)/shard_map/expert_mlp/pallas_call | solution.py:473
  362.7 75.2 %back.1 = (bf16[512,1024]{1,0:T(8,128)(2,1)}, f32[512,1024]{1,0:T(8,128)}, f32[32,3072]{1,0:T(8,128)}, f32[32,1024]{1,0:T(8,128)}, f32[32,128]{1,0:T(8,128)}) custom-call(bf16[512,1024]{1,0:T(8,128)(2,1)} %refs_0_.3, bf16[512,1024]{1,0:T(8,128)(2,1)} %refs_1_.3, f32[2,512]{1,0:T(2,128)} %add_convert_fusion.refs_2_, ...), custom_call_target="tpu_custom_call" | custom-call | flops 17179869184 | bytes 33554432 | tf_op jit(solution)/shard_map/back/pallas_call | solution.py:473
  437.9 1.6 slice_reduce_fusion
  439.5 0.8 slice.14
  440.3 0.7 copy.39
  441.0 0.8 slice.15
  441.7 0.6 copy.40
  442.4 2.3 copy.49
  444.7 1.3 copy.50
  446.1 0.7 copy.51
  446.8 0.0 copy-done.6
  446.8 0.7 copy.52
  447.5 0.0 copy-done.4
  447.5 0.8 copy.53
  448.3 0.0 copy-done.3
  448.3 0.8 copy.54
  449.1 1.3 copy.55
  450.4 0.0 copy-done
  450.4 1.3 copy.56
  (10 shorter events, 0.0 us)
Async XLA Ops:
  437.9 6.8 %copy-start.2 = (f32[512,1024]{1,0:T(8,128)S(1)}, f32[512,1024]{1,0:T(8,128)}, u32[]{:S(2)}) copy-start(f32[512,1024]{1,0:T(8,128)} %get-tuple-element.129) | copy-start | bytes 6291460
  442.4 3.7 copy-start.5
  442.4 4.4 copy-start.6
  442.4 5.1 %copy-start.4 = (f32[32,4096]{1,0:T(8,128)S(1)}, f32[32,4096]{1,0:T(8,128)}, u32[]{:S(2)}) copy-start(f32[32,4096]{1,0:T(8,128)} %get-tuple-element.134) | copy-start | bytes 1572868
  444.7 3.5 copy-start.3
  444.7 4.3 copy-start.1
  447.5 2.9 copy-start

commit v7 on v6

--- a/solution.py
+++ b/solution.py
@@ -240,10 +240,9 @@
 
 
 class Scatter:
-    RING = 6
-    CORE_RING = 4
-
-    def __init__(self, parts, half, experts, outs, store, start=0, made=None, z_late=4):
+    RING, SPREAD_RING, CORE_RING = 6, 8, 4
+
+    def __init__(self, parts, half, experts, outs, store, start=0, made=None, spread=False):
         self.experts, self.outs, self.store, self.start, self.made = experts, outs, store, start, made
         self.parts = parts
         self.given = []
@@ -253,7 +252,7 @@
         m = self.m = self.starts[-1]
         self.m_z = sum(p[3] for p in parts if p[1])
         unit = h[1:]
-        ring = self.ring = min(self.RING, m)
+        ring = self.ring = min(self.SPREAD_RING if spread else self.RING, m)
         self.core_ring = min(self.CORE_RING, m)
         self.in_specs = [pl.BlockSpec(memory_space=pltpu.HBM)] * len(self.args)
         self.out_specs = [pl.BlockSpec(memory_space=pltpu.VMEM)] * len(outs)
@@ -272,8 +271,8 @@
         if self.m_z:
             self.scratch.append(pltpu.VMEM((self.m_z, experts - 1) + unit, bf16))
             self.scratch.append(pltpu.VMEM((self.m_z, experts) + unit, bf16))
-        self.z_late = z_late
-        self.turns = start + max(m + 3, self.m_z + z_late)
+        self.stages = (0, 1, 3, 5, 7) if spread else (0, 1, 2, 3, 4)
+        self.turns = start + m + self.stages[4 if self.m_z else 3]
         self.along_z = self.m_z > 0
 
     def bind(self, ins, outs, scratch, place):
@@ -344,7 +343,7 @@
     def turn(self, now):
         limits = (self.m, self.m, self.m, self.m, self.m_z)
         steps = (self.load, self.chip, self.cross, self.plane, self.column)
-        for limit, late, step in zip(limits, (0, 1, 2, 3, self.z_late), steps):
+        for limit, late, step in zip(limits, self.stages, steps):
             i = now - self.start - late
             if limit:
 
@@ -422,6 +421,54 @@
             copy.wait()
         terms = [self.zs[i, self.place.e]] + [self.rz[i, j] for j in range(self.experts - 1)]
         self.store(self.out, i, add(*terms))
+
+
+class Along:
+    along_z = True
+
+    def __init__(self, shares, experts, outs, store, turns):
+        self.args, self.experts, self.outs, self.store, self.turns = [shares], experts, outs, store, turns
+        self.in_specs = [pl.BlockSpec(memory_space=pltpu.HBM)]
+        self.out_specs = [pl.BlockSpec(memory_space=pltpu.VMEM)] * len(outs)
+        self.items = shares.shape[1]
+        self.scratch = [
+            pltpu.VMEM(shares.shape, bf16),
+            pltpu.SemaphoreType.DMA((experts,)),
+            pltpu.SemaphoreType.DMA((experts,)),
+        ]
+
+    def bind(self, ins, outs, scratch, place):
+        self.source, self.out, self.place = ins[0], outs, place
+        self.land, self.sent, self.recv = scratch
+
+    def copies(self):
+        p = self.place
+        copies = [pltpu.make_async_copy(self.source.at[p.e], self.land.at[0], self.recv.at[0])]
+        return copies + [
+            pltpu.make_async_remote_copy(
+                src_ref=self.source.at[lax.rem(p.e + j, self.experts)],
+                dst_ref=self.land.at[j],
+                send_sem=self.sent.at[j],
+                recv_sem=self.recv.at[j],
+                device_id=p.z(j),
+                device_id_type=MESH,
+            )
+            for j in range(1, self.experts)
+        ]
+
+    def turn(self, now):
+        @when(now == 0)
+        def _():
+            for copy in self.copies():
+                copy.start()
+
+    def finish(self, now):
+        @when(now == self.turns - 1)
+        def _():
+            for copy in self.copies():
+                copy.wait()
+            for i in range(self.items):
+                self.store(self.out, i, add(*(self.land[j, i] for j in range(self.experts))))
 
 
 def add(*terms):
@@ -812,7 +859,7 @@
         self.firsts = width // self.columns
         self.rest = width - self.firsts * self.columns
         self.items = self.firsts + self.pairs + 1
-        self.heads_at = 3
+        self.heads_at = 4
         self.last = self.heads_at + self.pairs
         self.steps = self.last + 1
         self.first_item = self.heads_at
@@ -907,6 +954,8 @@
             for copy in loads + pair_weights(0):
                 copy.start()
 
+        @when(now == 1)
+        def _():
             for copy in loads:
                 copy.wait()
             probs = jnp.where(jnp.logical_and(lane >= 2, lane < 2 + experts), info[...], 0.0)
@@ -937,7 +986,7 @@
             )
             gains[...] = weights.astype(f32).T[:8]
 
-        @when(now == 1)
+        @when(now == 2)
         def _():
             normed, scale = normalize(tokens_grad[...])
             d_heads[1:2] = jnp.sum(grads[...] * normed, axis=0, keepdims=True)
@@ -945,7 +994,7 @@
             normed, _ = normalize(tok[...].astype(f32))
             attn_in_t[...] = (normed * gains[0:1]).astype(bf16).T
 
-        @when(now == 2)
+        @when(now == 3)
         def _():
             grad_attn = grads[...].astype(bf16)
             grad_att[...] = outer_nt(grad_attn, wo[...].reshape(width, width)).astype(bf16)
@@ -1009,7 +1058,7 @@
 
 
 class Experts:
-    PER_STEP = 1
+    TURNS = 6
 
     def __init__(self, pieces, blocks, width, size, chunks, back):
         self.parts, self.piece = len(pieces), pieces[0].shape
@@ -1030,14 +1079,16 @@
             + [pltpu.VMEM((rows, width), f32)] * 2
             + [pltpu.VMEM((2,) + self.block, bf16)] * 2
             + [pltpu.SemaphoreType.DMA((2, 2)), pltpu.SemaphoreType.DMA((self.parts,))]
+            + [pltpu.VMEM((2, width, size), bf16), pltpu.VMEM((2, size, width), bf16)]
+            + [pltpu.SemaphoreType.DMA((2, 2))]
         )
 
     def __call__(self, now, steps, *refs):
         refs = list(refs)
         take = lambda count: [refs.pop(0) for _ in range(count)]
-        pieces, (w1, w2) = take(self.parts), take(2)
+        pieces, full = take(self.parts), take(2)
         kept, targets, results = take(self.parts), take(2), take(self.parts)
-        x, g, xt, gt, out_sum, back_sum, stage_1, stage_2, sems, kept_sems = refs
+        x, g, xt, gt, out_sum, back_sum, stage_1, stage_2, sems, kept_sems, w1, w2, w_sems = refs
         width, size = self.width, self.piece[0]
 
         def flush(step):
@@ -1048,8 +1099,17 @@
                 for i, (stage, target) in enumerate(zip((stage_1, stage_2), targets))
             ]
 
+        def weights(step):
+            at = lax.rem(step, 2)
+            return [
+                pltpu.make_async_copy(a.at[step], b.at[at], w_sems.at[at, i])
+                for i, (a, b) in enumerate(zip(full, (w1, w2)))
+            ]
+
         @when(now == 0)
         def _():
+            for copy in weights(0):
+                copy.start()
             for j, piece in enumerate(pieces):
                 x[j * size : (j + 1) * size] = piece[:, :width]
                 g[j * size : (j + 1) * size] = piece[:, width:]
@@ -1058,8 +1118,14 @@
             out_sum[...] = jnp.zeros_like(out_sum)
             back_sum[...] = jnp.zeros_like(back_sum)
 
-        def block(b, _):
-            step = now * self.PER_STEP + b
+        def block(step, _):
+            for copy in weights(step):
+                copy.wait()
+
+            @when(step + 1 < self.blocks)
+            def _():
+                for copy in weights(step + 1):
+                    copy.start()
 
             @when(step >= 2)
             def _():
@@ -1067,7 +1133,7 @@
                     copy.wait()
 
             slot = lax.rem(step, 2)
-            for stage, d in zip((stage_1, stage_2), mlp_block(x, g, xt, gt, w1[b], w2[b], out_sum, back_sum)):
+            for stage, d in zip((stage_1, stage_2), mlp_block(x, g, xt, gt, w1[slot], w2[slot], out_sum, back_sum)):
                 if len(self.block) == 2:
                     stage[slot] = d
                 else:
@@ -1078,7 +1144,7 @@
                 copy.start()
             return 0
 
-        lax.fori_loop(0, self.PER_STEP, block, 0)
+        lax.fori_loop(now * self.blocks // steps, (now + 1) * self.blocks // steps, block, 0)
 
         @when(now == steps - 1)
         def _():
@@ -1207,37 +1273,29 @@
         by_chip = lambda a: a.reshape(4, 2, 2, experts // 2, chunks, step, 128)
 
         def store(outs, i, value):
-            @when(i < chunks)
+            if i < chunks:
+                for q in range(step // share):
+                    at = (i * (step // share) + q) * 128
+                    outs[0][:, at : at + 128] = value[q * share : (q + 1) * share]
+            else:
+                outs[1][:, (i - chunks) * step : (i - chunks + 1) * step] = value.T
+
+        def store_plane(outs, i, sums):
+            @when(i < 2 * chunks)
             def _():
-                for q in range(step // share):
-                    at = pl.multiple_of(i * (step // share * 128) + q * 128, 128)
-                    outs[0][:, pl.ds(at, 128)] = value[q * share : (q + 1) * share]
-
-            @when(i >= chunks)
+                for h, total in enumerate(sums):
+                    outs[0][h * half[0] : (h + 1) * half[0], i] = total.astype(bf16)
+
+            @when(i >= 2 * chunks)
             def _():
-                outs[1][:, pl.ds(pl.multiple_of((i - chunks) * step, step), step)] = value.T
-
-        def store_experts(outs, i, sums):
-            first = 2 * chunks
-
-            @when(i < first + chunks)
-            def _():
-                at = pl.ds(pl.multiple_of((i - first) * step, step), step)
+                at = pl.ds(pl.multiple_of((i - 2 * chunks) * step, step), step)
                 for h, total in enumerate(sums):
                     for c in range(half[0]):
-                        outs[2][0, at, (h * half[0] + c) * 128 : (h * half[0] + c + 1) * 128] = total[c]
-
-            @when(i >= first + chunks)
-            def _():
-                store_wout(outs[3], i - first - chunks, sums)
-
-        def store_any(outs, i, value):
-            (store_experts if isinstance(value, tuple) else store)(outs, i, value)
-
-        outs = [jax.ShapeDtypeStruct((share, ff), f32), jax.ShapeDtypeStruct((ff // devices, width), f32)]
-        parts = [(by_chip(d_fc), True, 0, chunks), (by_chip(d_proj), True, 0, chunks)]
-        parts += [(None, False, 0, chunks)] * 2
-        summing = Scatter(parts, half, experts, outs + win_out + wout_out, store_any, z_late=12)
+                        outs[1][0, at, (h * half[0] + c) * 128 : (h * half[0] + c + 1) * 128] = total[c]
+
+        outs = [jax.ShapeDtypeStruct((experts, 2 * chunks) + half[1:], bf16)]
+        parts = [(by_chip(d_fc), False, 0, chunks), (by_chip(d_proj), False, 0, chunks), (None, False, 0, chunks)]
+        summing = Scatter(parts, half, experts, outs + win_out, store_plane, spread=True)
         return_to = Exchange([], -1, experts, None, summing.turns, leaving[0].shape)
         scatters = [return_to, summing]
     else:
@@ -1247,17 +1305,15 @@
     if fast:
 
         def given(ins, os, own):
-            summing.given = os[experts : experts + 2]
+            summing.given = [os[experts]]
             return_to.sources = os[1:experts]
 
-    per = experts_kernel.PER_STEP
     results = call(
         "expert_mlp",
-        blocks // per,
+        experts_kernel.TURNS,
         experts_kernel,
         arrived + [win_full, wout_full],
-        [whole] * experts
-        + [pl.BlockSpec((per, width, size), lambda j: (j, 0, 0)), pl.BlockSpec((per, size, width), lambda j: (j, 0, 0))],
+        [whole] * experts + [hbm] * 2,
         experts_kernel.outs,
         [hbm] * len(experts_kernel.outs),
         experts_kernel.scratch,
@@ -1271,7 +1327,7 @@
     if fast:
         results = results[experts + 2 :]
         came_back = returned[:1] + results[: experts - 1]
-        grad_fc, grad_proj, grad_win, grad_wout = results[experts - 1 :]
+        plane_sums, grad_win = results[experts - 1 :]
     else:
         came_back = exchange(returned, -1)
     back = Back(tok_rows, width, experts, devices, capacity)
@@ -1280,9 +1336,15 @@
         parts = [(None, True, 0, back.items)]
         made = back.made()
         scatter_rest = Scatter(
-            parts, made[4:], experts, back.final_outs(), back.store, back.first_item, made
+            parts, made[4:], experts, back.final_outs(), back.store, back.first_item, made, spread=True
         )
-        back.moves = [scatter_rest]
+        parts = [(d_wout, False, 0, chunks)]
+        scatter_wout = Scatter(
+            parts, half, experts, wout_out, lambda outs, i, sums: store_wout(outs[0], i, sums), spread=True
+        )
+        outs = [jax.ShapeDtypeStruct((share, ff), f32), jax.ShapeDtypeStruct((ff // devices, width), f32)]
+        along = Along(plane_sums, experts, outs, store, max(scatter_rest.turns, scatter_wout.turns))
+        back.moves = [along, scatter_wout, scatter_rest]
     outs = back.outs + ([] if fast else [jax.ShapeDtypeStruct((back.items, width, back.columns), bf16)])
     mixed, tokens_grad, *results = call(
         "back",
@@ -1301,7 +1363,7 @@
         32 * tok_rows * width * width,
     )
     if fast:
-        grad_wqkv, grad_wo, grad_small = results
+        grad_fc, grad_proj, grad_wout, grad_wqkv, grad_wo, grad_small = results
     else:
         summed = scatter_xla(results[0].reshape(back.items, devices, share, -1).swapaxes(0, 1), AXES)
         last = summed[-1]

time: 452 us -> 437 us (0.967)
  Pallas kernels: 435 us -> 418 us
    pallas_call x3, Pallas kernels: 435 us -> 418 us  [call(): pl.pallas_call(kernel, grid=(total,), out_shape=list(outs) + join('outs')...]
where the time goes in v7:
time: 437 us
  Pallas kernels  418 us (96%)
  local copies, waits for them, and re-layouts  15.4 us (4%)
    pallas_call x3, Pallas kernels, call(): pl.pallas_call(kernel, grid=(total,), out_shape=list(outs) + join('outs')...  418 us
    unnamed x24, local copies, waits for them, and re-layouts  11.6 us

profile of v7, /device:TPU:0, one launch (start us, length us, event | category | flops | bytes accessed | tf_op | source)
XLA Modules:
  0.0 436.5 jit_solution(3443786989361465474)
XLA Ops:
  0.6 0.7 pad_maximum_fusion
  1.4 1.3 add_convert_fusion.refs_2_
  2.7 0.1 copy.38
  2.8 0.6 pad.4.refs_3_
  3.4 202.6 %forward.1 = (bf16[512,3072]{1,0:T(8,128)(2,1)}, f32[8,2,512]{2,1,0:T(2,128)}, bf16[512,1024]{1,0:T(8,128)(2,1)}, f32[512,1024]{1,0:T(8,128)}, bf16[512,1024]{1,...) custom-call(bf16[512,1024]{1,0:T(8,128)(2,1)} %refs_0_.3, ...), custom_call_target="tpu_custom_call" | custom-call | flops 32212254720 | bytes 33554432 | tf_op jit(solution)/shard_map/forward/pallas_call | solution.py:520
  206.0 123.5 %expert_mlp.1 = (bf16[160,2048]{1,0:T(8,128)(2,1)}, bf16[160,2048]{1,0:T(8,128)(2,1)}, bf16[160,2048]{1,0:T(8,128)(2,1)}, bf16[160,2048]{1,0:T(8,128)(2,1)}, bf1...) custom-call(bf16[160,2048]{1,0:T(8,128)(2,1)} %get-tuple-element.59., ...), custom_call_target="tpu_custom_call" | custom-call | flops 32212254720 | bytes 33554432 | tf_op jit(solution)/shard_map/expert_mlp/pallas_call | solution.py:520
  329.6 92.2 %back.1 = (bf16[512,1024]{1,0:T(8,128)(2,1)}, f32[512,1024]{1,0:T(8,128)}, f32[32,4096]{1,0:T(8,128)}, f32[128,1024]{1,0:T(8,128)}, f32[1,512,1024]{2,1,0:T(8,12...) custom-call(bf16[512,1024]{1,0:T(8,128)(2,1)} %refs_0_.3, bf16[512,1024]{1,0:T(8,128)(2,1)} %refs_1_.3, ...), custom_call_target="tpu_custom_call" | custom-call | flops 17179869184 | bytes 33554432 | tf_op jit(solution)/shard_map/back/pallas_call | solution.py:520
  421.8 0.0 copy-start.2
  421.8 1.6 slice_reduce_fusion
  423.4 0.8 slice.14
  424.2 0.7 copy.39
  424.8 0.8 slice.15
  425.6 0.6 copy.40
  426.2 2.3 copy.49
  428.5 0.0 copy-done.2
  428.5 1.3 copy.50
  429.8 0.0 copy-done.5
  429.8 0.7 copy.51
  430.6 0.7 copy.52
  431.3 0.8 copy.53
  432.1 0.8 copy.54
  432.8 1.3 copy.55
  434.2 1.0 copy-done.1
  435.2 1.3 copy.56
  (10 shorter events, 0.0 us)
Async XLA Ops:
  421.8 6.7 %copy-start.2 = (f32[512,1024]{1,0:T(8,128)S(1)}, f32[512,1024]{1,0:T(8,128)}, u32[]{:S(2)}) copy-start(f32[512,1024]{1,0:T(8,128)} %get-tuple-element.133) | copy-start | bytes 6291460
  428.5 1.3 copy-start.5
  428.5 2.1 copy-start.6
  428.5 2.7 copy-start.4
  428.5 3.5 copy-start.3
  429.8 3.0 copy-start
  432.8 2.3 copy-start.1

commit v8 on v7

--- a/solution.py
+++ b/solution.py
@@ -567,9 +567,8 @@
     return jnp.concatenate(outs, axis=0).T.astype(bf16), jnp.concatenate(tops, axis=0)
 
 
-def columns_of(code):
-    length = code.shape[1]
-    return [jnp.broadcast_to(code[i : i + 1], (128, length)).T.astype(jnp.int32) for i in range(2)]
+def columns_of(*rows):
+    return [jnp.broadcast_to(r[...].astype(f32), (128, r.shape[1])).T.astype(jnp.int32) for r in rows]
 
 
 class Forward:
@@ -630,7 +629,7 @@
 
     DENSE_ITEMS = 12
 
-    def __call__(self, now, steps, tok, cot, code, *refs):
+    def __call__(self, now, steps, tok, cot, routes, dropped, *refs):
         refs = list(refs)
         take = lambda count: [refs.pop(0) for _ in range(count)]
         full = self.gather.full[:5] if self.gather else take(5)
@@ -705,7 +704,7 @@
         def _():
             loads[2].start()
             loads[2].wait()
-            self.route(tok, cot, code, att, wo, ws, gains, after, mixed, gd, ge, disp, info)
+            self.route(tok, cot, routes, dropped, att, wo, ws, gains, after, mixed, gd, ge, disp, info)
 
         @when(now == self.at_leave)
         def _():
@@ -775,9 +774,9 @@
                     for copy in flush(last):
                         copy.wait()
 
-    def route(self, tok, cot, code, att, wo, ws, gains, after, mixed, gd, ge, disp, info):
+    def route(self, tok, cot, routes, dropped, att, wo, ws, gains, after, mixed, gd, ge, disp, info):
         width, length, experts = self.width, self.length, self.experts
-        route, drop = columns_of(code)
+        route, drop = columns_of(routes, dropped)
         after[...] = tok[...].astype(f32) + matmul(att[...], wo[...].reshape(width, width))
         normed, _ = normalize(after[...])
         mixed[...] = (normed * gains[1:2]).astype(bf16)
@@ -915,10 +914,10 @@
     def __call__(self, now, steps, *refs):
         experts, width, length = self.experts, self.width, self.length
         refs = list(refs)
-        tok, cot, code, qkv, lse, att, mixed_in, disp, info = refs[:9]
-        small_hbm, qkv_hbm, out_hbm, dense_hbm, grad_hbm, after_hbm = refs[9:15]
-        came_hbm = refs[15 : 15 + experts]
-        mixed, tokens_grad, *rest = refs[15 + experts :]
+        tok, cot, routes, dropped, qkv, lse, att, mixed_in, disp, info = refs[:10]
+        small_hbm, qkv_hbm, out_hbm, dense_hbm, grad_hbm, after_hbm = refs[10:16]
+        came_hbm = refs[16 : 16 + experts]
+        mixed, tokens_grad, *rest = refs[16 + experts :]
         if self.moves:
             made = self.moves[-1].own
         else:
@@ -961,7 +960,7 @@
             probs = jnp.where(jnp.logical_and(lane >= 2, lane < 2 + experts), info[...], 0.0)
             coef_0 = over_lanes(jnp.where(lane == 2 + experts, info[...], 0.0))
             coef_1 = over_lanes(jnp.where(lane == 3 + experts, info[...], 0.0))
-            route, drop = columns_of(code)
+            route, drop = columns_of(routes, dropped)
             chosen = jnp.where(lane - 2 == route, 1.0, 0.0)
             kept = (1 - drop[:, :1]).astype(f32)
             gate_prob = over_lanes(probs * chosen)
@@ -1161,6 +1160,48 @@
             for step in (self.blocks - 2, self.blocks - 1):
                 for copy in flush(step):
                     copy.wait()
+
+
+def finish(arrays, small, cuts):
+    pieces = []
+    for i, a in enumerate(arrays):
+        axis = 1 if a.shape[0] == 1 else 0
+        parts = 4 if a.size * a.dtype.itemsize >= MIB else 1
+        size = a.shape[axis] // parts
+        pieces += [(i, (0,) * axis + (pl.ds(p * size, size),)) for p in range(parts)]
+    n = len(arrays)
+
+    def kernel(*refs):
+        ins, columns, outs, rows = refs[:n], refs[n], refs[n + 1 : 2 * n + 1], refs[2 * n + 1 : -n - 1]
+        held, sems = refs[-n - 1 : -1], refs[-1]
+        move = lambda a, b, way: [
+            pltpu.make_async_copy(a[i].at[at], b[i].at[at], sems.at[way, c]) for c, (i, at) in enumerate(pieces)
+        ]
+        loads, copies = move(ins, held, 0), move(held, outs, 1)
+        for load in loads:
+            load.start()
+        for load, copy in zip(loads, copies):
+            load.wait()
+            copy.start()
+        turned = columns[...].T
+        for ref, first, last in zip(rows, cuts, cuts[1:]):
+            ref[...] = turned[first:last]
+        for copy in copies:
+            copy.wait()
+
+    whole, hbm = pl.BlockSpec(memory_space=pltpu.VMEM), pl.BlockSpec(memory_space=pltpu.HBM)
+    shapes = [jax.ShapeDtypeStruct(a.shape, a.dtype) for a in arrays]
+    shapes += [jax.ShapeDtypeStruct((b - a, small.shape[0]), f32) for a, b in zip(cuts, cuts[1:])]
+    results = pl.pallas_call(
+        kernel,
+        out_shape=shapes,
+        in_specs=[hbm] * n + [whole],
+        out_specs=[hbm] * n + [whole] * (len(cuts) - 1),
+        scratch_shapes=[pltpu.VMEM(a.shape, a.dtype) for a in arrays] + [pltpu.SemaphoreType.DMA((2, len(pieces)))],
+        compiler_params=pltpu.CompilerParams(vmem_limit_bytes=60 * MIB),
+        name="finish",
+    )(*arrays, small)
+    return results[:n], results[n:]
 
 
 def move(name, moves, collective_id, experts):
@@ -1225,7 +1266,7 @@
 
     forward = Forward(tok_rows, width, experts, devices, capacity, ff, *(moves or (None, None)))
     whole, hbm = pl.BlockSpec(memory_space=pltpu.VMEM), pl.BlockSpec(memory_space=pltpu.HBM)
-    code = jnp.stack([routes[:, 0], dropped]).astype(f32)
+    routes, dropped = routes.reshape(1, tok_rows), dropped.reshape(1, tok_rows)
     if fast:
 
         def given(ins, os, own):
@@ -1235,8 +1276,8 @@
         "forward",
         forward.steps,
         forward,
-        [tokens, cotangent, code] + full,
-        [whole] * 3 + [hbm] * len(full),
+        [tokens, cotangent, routes, dropped] + full,
+        [whole] * 4 + [hbm] * len(full),
         forward.outs + forward.targets,
         [whole] * len(forward.outs) + [hbm] * 2,
         forward.scratch,
@@ -1350,10 +1391,10 @@
         "back",
         back.steps,
         back,
-        [tokens, cotangent, code, qkv_rows, lse, attended, mixed_in, dispatch, probs]
+        [tokens, cotangent, routes, dropped, qkv_rows, lse, attended, mixed_in, dispatch, probs]
         + [small_full, qkv_full, out_full, dense_out, grad_mixed, after_attn]
         + came_back,
-        [whole] * 9 + [hbm] * (6 + experts),
+        [whole] * 10 + [hbm] * (6 + experts),
         outs,
         [whole] * len(outs),
         back.scratch,
@@ -1363,12 +1404,22 @@
         32 * tok_rows * width * width,
     )
     if fast:
-        grad_fc, grad_proj, grad_wout, grad_wqkv, grad_wo, grad_small = results
+        done, (gain_1, gain_2, router, coef) = finish(
+            [mixed, tokens_grad, grad_win] + results[:5], results[5], (0, 1, 2, 2 + experts, 4 + experts)
+        )
+        mixed, tokens_grad, grad_win, grad_fc, grad_proj, grad_wout, grad_wqkv, grad_wo = done
+        small_grads = (gain_1[0], gain_2[0], router.T, coef.T)
     else:
         summed = scatter_xla(results[0].reshape(back.items, devices, share, -1).swapaxes(0, 1), AXES)
         last = summed[-1]
         grad_wo = jnp.concatenate([*summed[: back.firsts], last[:, : back.rest]], axis=1)
         grad_small = last[:, back.rest : back.rest + 128]
+        small_grads = (
+            grad_small[:, 0],
+            grad_small[:, 1],
+            grad_small[:, 2 : 2 + experts],
+            grad_small[:, 2 + experts : 4 + experts],
+        )
         pairs = summed[back.firsts : -1].reshape(back.pairs, share, 3, PAIR)
         grad_wqkv = pairs.transpose(1, 2, 0, 3).reshape(share, 3 * width)
         grad_fc = scatter_xla(d_fc.reshape(devices, share, ff), AXES)
@@ -1379,14 +1430,14 @@
     return (
         mixed,
         tokens_grad,
-        grad_small[:, 0],
+        small_grads[0],
         grad_wqkv,
         grad_wo,
-        grad_small[:, 1],
+        small_grads[1],
         grad_fc,
         grad_proj,
-        grad_small[:, 2 : 2 + experts],
-        grad_small[:, 2 + experts : 4 + experts],
+        small_grads[2],
+        small_grads[3],
         grad_win,
         grad_wout,
     )

time: 437 us -> 429 us (0.982)
  local copies, waits for them, and re-layouts: 15.4 us -> 0.7 us
  Pallas kernels: 418 us -> 427 us
    unnamed x24 -> x0, local copies, waits for them, and re-layouts: 11.6 us -> none
    pallas_call x0 -> x1, Pallas kernels: none -> 8.43 us  [finish(): pl.pallas_call(kernel, out_shape=shapes, in_specs=[hbm] * n + [whole], ou...]
where the time goes in v8:
time: 429 us
  Pallas kernels  427 us (100%)
    pallas_call x3, Pallas kernels, call(): pl.pallas_call(kernel, grid=(total,), out_shape=list(outs) + join('outs')...  418 us

profile of v8, /device:TPU:0, one launch (start us, length us, event | category | flops | bytes accessed | tf_op | source)
XLA Modules:
  0.0 429.0 jit_solution(8302412566907985482)
XLA Ops:
  0.6 0.7 pad_maximum_fusion
  1.4 0.1 copy.30
  1.5 0.6 pad.4.refs_4_
  2.1 202.5 %forward.1 = (bf16[512,3072]{1,0:T(8,128)(2,1)}, f32[8,2,512]{2,1,0:T(2,128)}, bf16[512,1024]{1,0:T(8,128)(2,1)}, f32[512,1024]{1,0:T(8,128)}, bf16[512,1024]{1,...) custom-call(bf16[512,1024]{1,0:T(8,128)(2,1)} %refs_0_.3, ...), custom_call_target="tpu_custom_call" | custom-call | flops 32212254720 | bytes 33554432 | tf_op jit(solution)/shard_map/forward/pallas_call | solution.py:520
  204.6 123.6 %expert_mlp.1 = (bf16[160,2048]{1,0:T(8,128)(2,1)}, bf16[160,2048]{1,0:T(8,128)(2,1)}, bf16[160,2048]{1,0:T(8,128)(2,1)}, bf16[160,2048]{1,0:T(8,128)(2,1)}, bf1...) custom-call(bf16[160,2048]{1,0:T(8,128)(2,1)} %get-tuple-element.71., ...), custom_call_target="tpu_custom_call" | custom-call | flops 32212254720 | bytes 33554432 | tf_op jit(solution)/shard_map/expert_mlp/pallas_call | solution.py:520
  328.2 92.3 %back.1 = (bf16[512,1024]{1,0:T(8,128)(2,1)}, f32[512,1024]{1,0:T(8,128)}, f32[32,4096]{1,0:T(8,128)}, f32[128,1024]{1,0:T(8,128)}, f32[1,512,1024]{2,1,0:T(8,12...) custom-call(bf16[512,1024]{1,0:T(8,128)(2,1)} %refs_0_.3, bf16[512,1024]{1,0:T(8,128)(2,1)} %refs_1_.3, ...), custom_call_target="tpu_custom_call" | custom-call | flops 17179869184 | bytes 33554432 | tf_op jit(solution)/shard_map/back/pallas_call | solution.py:520
  420.4 8.4 %finish.1 = (bf16[512,1024]{1,0:T(8,128)(2,1)}, f32[512,1024]{1,0:T(8,128)}, f32[1,1024,512]{2,1,0:T(8,128)}, f32[32,4096]{1,0:T(8,128)}, f32[128,1024]{1,0:T(8,...) custom-call(bf16[512,1024]{1,0:T(8,128)(2,1)} %get-tuple-element.85., ...), custom_call_target="tpu_custom_call" | custom-call | tf_op jit(solution)/shard_map/finish/pallas_call | solution.py:1195

commit v9 on v8

--- a/solution.py
+++ b/solution.py
@@ -579,7 +579,7 @@
         share = self.share = width // devices
         self.blocks = ff // BLOCK
         self.per_block = BLOCK * devices // ff
-        self.at_norm, self.at_qkv = 4, 6
+        self.at_norm, self.at_qkv = 4, 7
         self.at_heads = self.at_qkv + 1
         self.per_turn = 2
         self.at_out = self.at_heads + length // SEQ * pairs // self.per_turn
@@ -627,7 +627,7 @@
             pltpu.SemaphoreType.DMA((2, 2)),
         ]
 
-    DENSE_ITEMS = 12
+    DENSE_ITEMS = 13
 
     def __call__(self, now, steps, tok, cot, routes, dropped, *refs):
         refs = list(refs)
@@ -1057,7 +1057,7 @@
 
 
 class Experts:
-    TURNS = 6
+    TURNS = 7
 
     def __init__(self, pieces, blocks, width, size, chunks, back):
         self.parts, self.piece = len(pieces), pieces[0].shape
@@ -1242,7 +1242,8 @@
     capacity = -(-(tok_rows * 10) // (8 * experts))
     moves, given = [], None
     if fast:
-        items = cut(1, share, 3 * width, 1, 3) + cut(2, share, width, 1, 1)
+        sixth = cut(1, share, 3 * width, 1, 6)
+        items = sixth[:2] + [sixth[2] + sixth[3], sixth[4] + sixth[5]] + cut(2, share, width, 1, 1)
         items += cut(3, share, ff, 1, 4) + cut(4, ff // devices, width, 4, 1)
         items[0] = cut(0, share, 128, 1, 1)[0] + items[0]
         assert len(items) == Forward.DENSE_ITEMS

time: 429 us -> 422 us (0.984)
  Pallas kernels: 427 us -> 419 us
    pallas_call x3, Pallas kernels: 418 us -> 410 us  [call(): pl.pallas_call(kernel, grid=(total,), out_shape=list(outs) + join('outs')...]
where the time goes in v9:
time: 422 us; the launch traced here: 421 us
  Pallas kernels  419 us (99%)
    pallas_call x3, Pallas kernels, call(): pl.pallas_call(kernel, grid=(total,), out_shape=list(outs) + join('outs')...  410 us

profile of v9, /device:TPU:0, one launch (start us, length us, event | category | flops | bytes accessed | tf_op | source)
XLA Modules:
  0.0 421.1 jit_solution(5388769013108129697)
XLA Ops:
  0.6 0.7 pad_maximum_fusion
  1.4 0.1 copy.30
  1.5 0.6 pad.4.refs_4_
  2.1 200.5 %forward.1 = (bf16[512,3072]{1,0:T(8,128)(2,1)}, f32[8,2,512]{2,1,0:T(2,128)}, bf16[512,1024]{1,0:T(8,128)(2,1)}, f32[512,1024]{1,0:T(8,128)}, bf16[512,1024]{1,...) custom-call(bf16[512,1024]{1,0:T(8,128)(2,1)} %refs_0_.3, ...), custom_call_target="tpu_custom_call" | custom-call | flops 32212254720 | bytes 33554432 | tf_op jit(solution)/shard_map/forward/pallas_call | solution.py:520
  202.6 117.8 %expert_mlp.1 = (bf16[160,2048]{1,0:T(8,128)(2,1)}, bf16[160,2048]{1,0:T(8,128)(2,1)}, bf16[160,2048]{1,0:T(8,128)(2,1)}, bf16[160,2048]{1,0:T(8,128)(2,1)}, bf1...) custom-call(bf16[160,2048]{1,0:T(8,128)(2,1)} %get-tuple-element.71., ...), custom_call_target="tpu_custom_call" | custom-call | flops 32212254720 | bytes 33554432 | tf_op jit(solution)/shard_map/expert_mlp/pallas_call | solution.py:520
  320.4 92.2 %back.1 = (bf16[512,1024]{1,0:T(8,128)(2,1)}, f32[512,1024]{1,0:T(8,128)}, f32[32,4096]{1,0:T(8,128)}, f32[128,1024]{1,0:T(8,128)}, f32[1,512,1024]{2,1,0:T(8,12...) custom-call(bf16[512,1024]{1,0:T(8,128)(2,1)} %refs_0_.3, bf16[512,1024]{1,0:T(8,128)(2,1)} %refs_1_.3, ...), custom_call_target="tpu_custom_call" | custom-call | flops 17179869184 | bytes 33554432 | tf_op jit(solution)/shard_map/back/pallas_call | solution.py:520
  412.6 8.4 %finish.1 = (bf16[512,1024]{1,0:T(8,128)(2,1)}, f32[512,1024]{1,0:T(8,128)}, f32[1,1024,512]{2,1,0:T(8,128)}, f32[32,4096]{1,0:T(8,128)}, f32[128,1024]{1,0:T(8,...) custom-call(bf16[512,1024]{1,0:T(8,128)(2,1)} %get-tuple-element.85., ...), custom_call_target="tpu_custom_call" | custom-call | tf_op jit(solution)/shard_map/finish/pallas_call | solution.py:1195

commit v10 on v9

--- a/solution.py
+++ b/solution.py
@@ -1057,7 +1057,7 @@
 
 
 class Experts:
-    TURNS = 7
+    TURNS = 8
 
     def __init__(self, pieces, blocks, width, size, chunks, back):
         self.parts, self.piece = len(pieces), pieces[0].shape

time: 422 us -> 422 us (level)
  no operation moved by 1% of the time
where the time goes in v10:
time: 422 us; the launch traced here: 421 us
  Pallas kernels  419 us (99%)
    pallas_call x3, Pallas kernels, call(): pl.pallas_call(kernel, grid=(total,), out_shape=list(outs) + join('outs')...  410 us

profile of v10, /device:TPU:0, one launch (start us, length us, event | category | flops | bytes accessed | tf_op | source)
XLA Modules:
  0.0 421.1 jit_solution(10530940880343238131)
XLA Ops:
  0.6 0.7 pad_maximum_fusion
  1.4 0.1 copy.30
  1.5 0.6 pad.4.refs_4_
  2.1 200.5 %forward.1 = (bf16[512,3072]{1,0:T(8,128)(2,1)}, f32[8,2,512]{2,1,0:T(2,128)}, bf16[512,1024]{1,0:T(8,128)(2,1)}, f32[512,1024]{1,0:T(8,128)}, bf16[512,1024]{1,...) custom-call(bf16[512,1024]{1,0:T(8,128)(2,1)} %refs_0_.3, ...), custom_call_target="tpu_custom_call" | custom-call | flops 32212254720 | bytes 33554432 | tf_op jit(solution)/shard_map/forward/pallas_call | solution.py:520
  202.6 117.8 %expert_mlp.1 = (bf16[160,2048]{1,0:T(8,128)(2,1)}, bf16[160,2048]{1,0:T(8,128)(2,1)}, bf16[160,2048]{1,0:T(8,128)(2,1)}, bf16[160,2048]{1,0:T(8,128)(2,1)}, bf1...) custom-call(bf16[160,2048]{1,0:T(8,128)(2,1)} %get-tuple-element.71., ...), custom_call_target="tpu_custom_call" | custom-call | flops 32212254720 | bytes 33554432 | tf_op jit(solution)/shard_map/expert_mlp/pallas_call | solution.py:520
  320.4 92.2 %back.1 = (bf16[512,1024]{1,0:T(8,128)(2,1)}, f32[512,1024]{1,0:T(8,128)}, f32[32,4096]{1,0:T(8,128)}, f32[128,1024]{1,0:T(8,128)}, f32[1,512,1024]{2,1,0:T(8,12...) custom-call(bf16[512,1024]{1,0:T(8,128)(2,1)} %refs_0_.3, bf16[512,1024]{1,0:T(8,128)(2,1)} %refs_1_.3, ...), custom_call_target="tpu_custom_call" | custom-call | flops 17179869184 | bytes 33554432 | tf_op jit(solution)/shard_map/back/pallas_call | solution.py:520
  412.6 8.4 %finish.1 = (bf16[512,1024]{1,0:T(8,128)(2,1)}, f32[512,1024]{1,0:T(8,128)}, f32[1,1024,512]{2,1,0:T(8,128)}, f32[32,4096]{1,0:T(8,128)}, f32[128,1024]{1,0:T(8,...) custom-call(bf16[512,1024]{1,0:T(8,128)(2,1)} %get-tuple-element.85., ...), custom_call_target="tpu_custom_call" | custom-call | tf_op jit(solution)/shard_map/finish/pallas_call | solution.py:1195
